TPU v7x, 256 devices: a whole 4x4x8 slice. The times are simulated.
256 devices in a mesh: row: 4 (over x), col: 8 (over y, z_lo), depth: 8 (over z_hi, core).
Axes of the slice: x: 4, y: 4, z: 8 (z_hi: 4, z_lo: 2; z = z_hi * 2 + z_lo), core: 2. Of those that a mesh axis runs over, the one named last changes fastest.
Arguments:
- features: bfloat16 [256, 16384], P('depth', ('row', 'col')), may hold values from -6 to 6
- weight: bfloat16 [256, 256], replicated, may hold values from -0.375 to 0.375
- tiles: bfloat16 [4, 8, 8, 64, 128, 128], P('row', 'col', 'depth'), may hold values from -0.03125 to 0.03125
- pairs: int32 [4, 8, 8, 2, 64], P('row', 'col', 'depth'), may hold values from 0 to 31, as said below
- counts: int32 [4, 8, 8], P('row', 'col', 'depth'), may hold values from 16 to 64, as said below
- cotangent: bfloat16 [256, 16384], P('depth', ('row', 'col')), may hold values from -6 to 6
Outputs:
- activation: bfloat16 [256, 16384], P('depth', ('row', 'col'))
- weight_grad: float32 [256, 256], P(None, 'depth')
Inputs may be any that keep to these rules, and one draw needn't show every extreme that they name: `pairs`: each device's local block numbers: row blocks below 32, column blocks below 16. Within one grid cell (r, c), no two slots of its devices along depth name the same pair of blocks. `counts`: slots at and past a device's count hold values that are not part of the adjacency.
All inputs are finite; a program needn't handle non-finite values.
Results may differ from a plain program's by a relative error of at most 0.0051.
Values may be sent and summed in bfloat16 or wider, within the bound.
No kernel may reach another device: no remote copies, remote signals or barrier semaphores. Data moves between devices by JAX's collectives and lax.ppermute only.
A program may use at most 64 MiB of HBM per device.

v0:
```python
import jax
import jax.numpy as jnp
from jax import lax
from jax.sharding import PartitionSpec as P

FEAT = 256
TILE = 128
NODE_DEV = 512


def collect(piece):
    gathered_cols = lax.all_gather(piece[None], ("row", "depth"), axis=0, tiled=True)
    gathered_rows = lax.all_gather(piece[None], ("col", "depth"), axis=0, tiled=True)
    return (
        gathered_cols.reshape(lax.axis_size("row"), FEAT, NODE_DEV),
        gathered_rows.reshape(lax.axis_size("col"), FEAT, NODE_DEV),
    )


def spread_terms(col_segment, row_segment, tile_stack, pair_list, keep_mask):
    row_parts = col_segment.shape[0]
    col_parts = row_segment.shape[0]
    per_piece = NODE_DEV // TILE
    col_view = col_segment.reshape(row_parts, FEAT, per_piece, TILE)
    row_view = row_segment.reshape(col_parts, FEAT, per_piece, TILE)
    slot_total = tile_stack.shape[0]
    group_size = min(32, slot_total)
    group_turns = slot_total // group_size
    scanned = (
        tile_stack.reshape(group_turns, group_size, TILE, TILE),
        pair_list[0].reshape(group_turns, group_size),
        pair_list[1].reshape(group_turns, group_size),
        keep_mask.reshape(group_turns, group_size),
    )

    def visiting(carried, element):
        row_acc, col_acc = carried
        tile_values, row_select, col_select, keep_group = element
        row_piece = row_select // per_piece
        row_offset = row_select % per_piece
        col_piece = col_select // per_piece
        col_offset = col_select % per_piece
        from_cols = col_view[col_piece, :, col_offset, :]
        from_rows = row_view[row_piece, :, row_offset, :]
        to_rows = (
            jnp.einsum("gfj,gij->gfi", from_cols, tile_values, preferred_element_type=jnp.float32)
            * keep_group[:, None, None]
        )
        to_cols = (
            jnp.einsum("gfi,gij->gfj", from_rows, tile_values, preferred_element_type=jnp.float32)
            * keep_group[:, None, None]
        )
        row_acc = row_acc.at[row_piece, :, row_offset, :].add(to_rows)
        col_acc = col_acc.at[col_piece, :, col_offset, :].add(to_cols)
        return ((row_acc, col_acc), None)

    initial = (
        jnp.zeros((col_parts, FEAT, per_piece, TILE), jnp.float32),
        jnp.zeros((row_parts, FEAT, per_piece, TILE), jnp.float32),
    )
    (row_acc, col_acc), _ = lax.scan(visiting, initial, scanned)
    return (row_acc.reshape(col_parts, FEAT, NODE_DEV), col_acc.reshape(row_parts, FEAT, NODE_DEV))


def settle(row_partial, col_partial):
    feat_share = FEAT // lax.axis_size("depth")
    row_share = lax.psum_scatter(
        row_partial.reshape(-1, feat_share, NODE_DEV),
        ("col", "depth"),
        scatter_dimension=0,
        tiled=True,
    )
    col_share = lax.psum_scatter(
        col_partial.reshape(-1, feat_share, NODE_DEV),
        ("row", "depth"),
        scatter_dimension=0,
        tiled=True,
    )
    return (row_share + col_share)[0]


def body(features, weight, tiles, pairs, counts, cotangent):
    feat_share = FEAT // lax.axis_size("depth")
    slot_total = tiles.shape[3]
    tile_stack = tiles.reshape(slot_total, TILE, TILE)
    pair_list = pairs.reshape(2, slot_total)
    keep_mask = (jnp.arange(slot_total) < counts.reshape(())).astype(jnp.float32)
    cols_input, rows_input = collect(features)
    hidden_cols = jnp.einsum(
        "fo,rfn->ron", weight, cols_input, preferred_element_type=jnp.float32
    ).astype(jnp.bfloat16)
    hidden_rows = jnp.einsum(
        "fo,cfn->con", weight, rows_input, preferred_element_type=jnp.float32
    ).astype(jnp.bfloat16)
    row_partial, col_partial = spread_terms(
        hidden_cols, hidden_rows, tile_stack, pair_list, keep_mask
    )
    preact = settle(row_partial, col_partial)
    activation = jax.nn.silu(preact).astype(jnp.bfloat16)
    sigmoid_pre = jax.nn.sigmoid(preact)
    slope_bf = (
        cotangent.astype(jnp.float32) * sigmoid_pre * (1.0 + preact * (1.0 - sigmoid_pre))
    ).astype(jnp.bfloat16)
    cols_slope, rows_slope = collect(slope_bf)
    row_spread, col_spread = spread_terms(cols_slope, rows_slope, tile_stack, pair_list, keep_mask)
    partial_grad = jnp.einsum(
        "cfn,con->fo", rows_input.astype(jnp.float32), row_spread, precision=lax.Precision.HIGHEST
    )
    partial_grad = partial_grad + jnp.einsum(
        "rfn,ron->fo", cols_input.astype(jnp.float32), col_spread, precision=lax.Precision.HIGHEST
    )
    summed_grad = lax.psum(partial_grad, ("row", "col", "depth"))
    weight_grad = lax.dynamic_slice_in_dim(
        summed_grad, lax.axis_index("depth") * feat_share, feat_share, 1
    )
    return (activation, weight_grad)


def solution(mesh):
    placed = (
        P("depth", ("row", "col")),
        P(),
        P("row", "col", "depth", None, None, None),
        P("row", "col", "depth", None, None),
        P("row", "col", "depth"),
        P("depth", ("row", "col")),
    )
    return jax.shard_map(
        body,
        mesh=mesh,
        in_specs=placed,
        out_specs=(P("depth", ("row", "col")), P(None, "depth")),
        check_vma=False,
    )
```

profile of v0, /device:TPU:8, one launch (start us, length us, event | category | flops | bytes accessed | tf_op | source)
XLA Modules:
  0.0 1120.9 jit_solution(15381080088072883487)
XLA Ops:
  10.3 55.2 %all-gather.9.cloned.1.call-done = bf16[1024,512]{1,0:T(8,128)(2,1)} async-done(((bf16[32,512]{1,0:T(8,128)(2,1)}), bf16[1024,512]{1,0:T(8,128)(2,1)}) %all-gather.9.cloned.1.call-update) | async-done | bytes 1048592 | tf_op jit(solution)/shard_map/all_gather | solution.py:12
  65.5 1.7 convolution_convert_fusion.1
  67.9 110.8 %all-gather.11.cloned.1.call-done = bf16[2048,512]{1,0:T(8,128)(2,1)} async-done(((bf16[32,512]{1,0:T(8,128)(2,1)}), bf16[2048,512]{1,0:T(8,128)(2,1)}) %all-gather.11.cloned.1.call-update) | async-done | bytes 2097168 | tf_op jit(solution)/shard_map/all_gather | solution.py:13
  178.7 2.4 convolution_convert_fusion
  181.0 2.4 copy.21
  183.5 2.5 broadcast.695.clone
  186.1 64.4 %while.30 = (s32[]{:T(128)}, f32[8,256,4,128]{3,1,2,0:T(8,128)}, f32[4,256,4,128]{3,1,2,0:T(8,128)S(1)}, s32[2,32]{1,0:T(2,128)S(1)}, s32[2,32]{1,0:T(2,128)S(1)...) while((s32[]{:T(128)}, f32[8,256,4,128]{3,1,2,0:T(8,128)}, ...), condition=%wide.region_3.4_spmd, body=%wide.region_0.3_spmd.sunk | while | flops 541068032 | bytes 48239344 | solution.py:61
  186.2 2.1 gather_fusion
  188.3 4.6 convolution_multiply_fusion.8
  193.0 10.1 scatter_fusion
  203.1 3.7 gather_fusion.1
  206.8 4.6 convolution_multiply_fusion.9
  211.4 6.9 scatter_fusion.1
  218.4 2.1 gather_fusion
  220.5 4.6 convolution_multiply_fusion.8
  225.2 10.0 scatter_fusion
  235.3 3.7 gather_fusion.1
  239.0 4.6 convolution_multiply_fusion.9
  243.6 6.9 scatter_fusion.1
  250.5 2.7 copy.23
  253.2 3.1 reshape_reshape.18
  256.6 7.0 copy.22
  263.6 5.5 reshape_reshape.17
  269.1 77.6 %reduce-scatter.5.cloned.1.call-done = f32[1,32,512]{2,1,0:T(8,128)} async-done(((f32[32,32,512]{2,1,0:T(8,128)}), f32[1,32,512]{2,1,0:T(8,128)}) %reduce-scatter.5.cloned.1.call-update) | async-done | bytes 65552 | tf_op jit(solution)/shard_map/reduce_scatter | solution.py:73
  346.7 241.5 %reduce-scatter.3.cloned.1.call-done = f32[1,32,512]{2,1,0:T(8,128)} async-done(((f32[64,32,512]{2,1,0:T(8,128)}), f32[1,32,512]{2,1,0:T(8,128)}) %reduce-scatter.3.cloned.1.call-update) | async-done | bytes 65552 | tf_op jit(solution)/shard_map/reduce_scatter | solution.py:67
  590.3 70.8 %all-gather.13.cloned.1.call-done = bf16[1024,512]{1,0:T(8,128)(2,1)} async-done(((bf16[32,512]{1,0:T(8,128)(2,1)}), bf16[1024,512]{1,0:T(8,128)(2,1)}) %all-gather.13.cloned.1.call-update) | async-done | bytes 1048592 | tf_op jit(solution)/shard_map/all_gather | solution.py:12
  662.7 112.2 %all-gather.15.cloned.1.call-done = bf16[2048,512]{1,0:T(8,128)(2,1)} async-done(((bf16[32,512]{1,0:T(8,128)(2,1)}), bf16[2048,512]{1,0:T(8,128)(2,1)}) %all-gather.15.cloned.1.call-update) | async-done | bytes 2097168 | tf_op jit(solution)/shard_map/all_gather | solution.py:13
  774.9 2.5 reshape_reshape.20
  777.5 1.9 copy.25
  779.4 2.5 broadcast.695
  782.1 64.4 %while.31 = (s32[]{:T(128)}, f32[8,256,4,128]{3,1,2,0:T(8,128)}, f32[4,256,4,128]{3,1,2,0:T(8,128)S(1)}, s32[2,32]{1,0:T(2,128)S(1)}, s32[2,32]{1,0:T(2,128)S(1)...) while((s32[]{:T(128)}, f32[8,256,4,128]{3,1,2,0:T(8,128)}, ...), condition=%wide.region_9.10_spmd, body=%wide.region_6.9_spmd.sunk | while | flops 541068032 | bytes 48239344 | solution.py:61
  782.1 2.1 gather_fusion.2
  784.3 4.6 convolution_multiply_fusion.10
  788.9 10.1 scatter_fusion.2
  799.0 3.7 gather_fusion.3
  802.7 4.6 convolution_multiply_fusion.11
  807.3 6.9 scatter_fusion.3
  814.4 2.1 gather_fusion.2
  816.5 4.6 convolution_multiply_fusion.10
  821.1 10.0 scatter_fusion.2
  831.2 3.7 gather_fusion.3
  834.9 4.6 convolution_multiply_fusion.11
  839.5 6.9 scatter_fusion.3
  846.5 1.9 copy.28
  848.4 3.4 convolution_bitcast_fusion.1
  851.8 5.5 copy.26
  857.3 6.3 fusion.31
  863.7 249.0 %all-reduce.2.cloned.1.call-done = f32[256,256]{0,1:T(8,128)} async-done(((f32[256,256]{0,1:T(8,128)}), f32[256,256]{0,1:T(8,128)}) %all-reduce.2.cloned.1.call-update) | async-done | bytes 262160 | tf_op jit(solution)/shard_map/psum | solution.py:112
  (55 shorter events, 9.2 us)
Async XLA Ops:
  7.2 58.3 %copy-start = (bf16[256,256]{1,0:T(8,128)(2,1)S(1)}, bf16[256,256]{1,0:T(8,128)(2,1)}, u32[]{:S(2)}) copy-start(bf16[256,256]{1,0:T(8,128)(2,1)} %param.11) | copy-start | bytes 393220
  7.2 58.3 %all-gather.9.cloned.1.call-start = ((), (), s32[]{:S(2)}) async-start(), calls=%async_computation.5 | async-start | bytes 1081344 | tf_op jit(solution)/shard_map/all_gather | solution.py:12
  7.9 170.8 %all-gather.11.cloned.1.call-start = ((), (), s32[]{:S(2)}) async-start(), calls=%async_computation.6 | async-start | bytes 2129920 | tf_op jit(solution)/shard_map/all_gather | solution.py:13
  8.7 338.0 %reduce-scatter.5.cloned.1.call-start = ((), (), s32[]{:S(2)}) async-start(), calls=%async_computation.3 | async-start | bytes 2162688 | tf_op jit(solution)/shard_map/reduce_scatter | solution.py:73
  256.4 331.8 %reduce-scatter.3.cloned.1.call-start = ((), (), s32[]{:S(2)}) async-start(), calls=%async_computation.2 | async-start | bytes 4259840 | tf_op jit(solution)/shard_map/reduce_scatter | solution.py:67
  269.0 319.1 %copy-start.4 = (bf16[32,512]{1,0:T(8,128)(2,1)S(1)}, bf16[32,512]{1,0:T(8,128)(2,1)}, u32[]{:S(2)}) copy-start(bf16[32,512]{1,0:T(8,128)(2,1)} %param.15) | copy-start | bytes 98308
  269.1 392.1 %all-gather.13.cloned.1.call-start = ((), (), s32[]{:S(2)}) async-start(), calls=%async_computation.7 | async-start | bytes 1081344 | tf_op jit(solution)/shard_map/all_gather | solution.py:12
  589.7 185.2 %all-gather.15.cloned.1.call-start = ((), (), s32[]{:S(2)}) async-start(), calls=%async_computation.8 | async-start | bytes 2129920 | tf_op jit(solution)/shard_map/all_gather | solution.py:13
  590.3 522.4 %all-reduce.2.cloned.1.call-start = ((), (), s32[]{:S(2)}) async-start(), calls=%async_computation.4 | async-start | bytes 524288 | tf_op jit(solution)/shard_map/psum | solution.py:112
  846.5 1.9 copy-start.3
  851.8 5.5 copy-start.2
  857.3 256.7 %copy-start.1 = (bf16[256,256]{1,0:T(8,128)(2,1)S(1)}, bf16[256,256]{1,0:T(8,128)(2,1)}, u32[]{:S(2)}) copy-start(bf16[256,256]{1,0:T(8,128)(2,1)} %param.11) | copy-start | bytes 393220
Sparse Core Ops, SparseCore 0:
  10.6 54.8 all-gather.8
  67.4 111.2 all-gather.10
  256.5 90.1 reduce-scatter.4
  349.1 239.0 reduce-scatter.2
  591.4 69.6 all-gather.12
  663.6 111.2 all-gather.14
  863.8 248.8 all-reduce.1
where the time goes:
time: 1120 us
  waiting for transfers between devices  919 us (82%)
  other arithmetic  69.8 us (6%)
  local copies, waits for them, and re-layouts  65.8 us (6%)
  matrix products  50.8 us (5%)
  between operations  14.9 us (1%)
    psum x1, waiting for transfers between devices, body(): summed_grad = lax.psum(partial_grad, ('row', 'col', 'depth'))  249 us
    reduce_scatter x1, waiting for transfers between devices, settle(): lax.psum_scatter(row_partial.reshape(-1, feat_share, NODE_DEV), ('col', '...  241 us
    all_gather x2, waiting for transfers between devices, collect(): lax.all_gather(piece[None], ('col', 'depth'), axis=0, tiled=True)  223 us
    all_gather x2, waiting for transfers between devices, collect(): lax.all_gather(piece[None], ('row', 'depth'), axis=0, tiled=True)  126 us
    reduce_scatter x1, waiting for transfers between devices, settle(): lax.psum_scatter(col_partial.reshape(-1, feat_share, NODE_DEV), ('row', '...  77.6 us
    scatter-add x4, other arithmetic, visiting(): row_acc = row_acc.at[row_piece, :, row_offset, :].add(to_rows)  40.2 us
    scatter-add x4, other arithmetic, visiting(): col_acc = col_acc.at[col_piece, :, col_offset, :].add(to_cols)  27.8 us
  transfers between devices with their start and end apart: 7, of which 7 were waited for; matrix products, arithmetic and copies ran while one was open for 2% of the time, Pallas kernels for 0%

commit v1 on v0

v1 whole, which is shorter than its diff:
```python
import functools

import jax
import jax.numpy as jnp
from jax import lax
from jax.experimental import pallas as pl
from jax.experimental.pallas import tpu as pltpu
from jax.sharding import Mesh, PartitionSpec as P

FEAT = 256
TILE = 128
NODE_DEV = 512
PER_PIECE = NODE_DEV // TILE
HALF = FEAT // 2
GROUP = 4
MIB = 1 << 20

VMEM = pl.BlockSpec(memory_space=pltpu.VMEM)
SMEM = pl.BlockSpec(memory_space=pltpu.SMEM)


def params(mib):
    return pltpu.CompilerParams(vmem_limit_bytes=mib * MIB)


def shifted(value, axes, step):
    total = lax.axis_size(axes)
    return lax.ppermute(value, axes, [(i, (i + step) % total) for i in range(total)])


def order_kernel(place, own, r1, r2, r3, out):
    for back, ref in enumerate((own, r1, r2, r3)):
        slot = lax.rem(place[0] + 4 - back, 4)
        out[pl.ds(pl.multiple_of(slot * 32, 32), 32), :] = ref[...]


def agg_kernel(pieces, outs, transpose, meta, own_tiles, sib_tiles, *refs):
    sources = refs[:pieces]
    results = refs[pieces : pieces + outs]
    field, acc = refs[pieces + outs :]
    for back, ref in enumerate(sources):
        slot = (pieces - back) % pieces
        for part in range(PER_PIECE):
            field[slot * PER_PIECE + part] = ref[:, part * TILE : (part + 1) * TILE]
    acc[...] = jnp.zeros_like(acc)
    contract = (((1,), (1,)), ((), ())) if transpose else (((1,), (0,)), ((), ()))
    for base, tiles in ((0, own_tiles), (3, sib_tiles)):

        def visiting(turn, carry, base=base, tiles=tiles):
            terms = []
            for member in range(GROUP):
                slot = turn * GROUP + member
                terms.append(
                    lax.dot_general(
                        field[meta[base, slot]],
                        tiles[slot],
                        contract,
                        preferred_element_type=jnp.float32,
                    )
                )
            for member in range(GROUP):
                target = meta[base + 1, turn * GROUP + member]
                acc[target] += terms[member]
            return carry

        lax.fori_loop(0, meta[base + 2, 0], visiting, 0)
    for piece in range(outs):
        for part in range(PER_PIECE):
            results[piece][:, part * TILE : (part + 1) * TILE] = acc[
                piece * PER_PIECE + part
            ].astype(jnp.bfloat16)


def agg(meta, own_tiles, sib_tiles, sources, outs, transpose, flops):
    pieces = len(sources)
    piece = jax.ShapeDtypeStruct((HALF, NODE_DEV), jnp.bfloat16)
    return pl.pallas_call(
        functools.partial(agg_kernel, pieces, outs, transpose),
        out_shape=[piece] * outs,
        in_specs=[SMEM, VMEM, VMEM] + [VMEM] * pieces,
        out_specs=[VMEM] * outs,
        scratch_shapes=[
            pltpu.VMEM((pieces * PER_PIECE, HALF, TILE), jnp.bfloat16),
            pltpu.VMEM((outs * PER_PIECE + 1, HALF, TILE), jnp.float32),
        ],
        compiler_params=params(24),
        cost_estimate=pl.CostEstimate(flops=flops, bytes_accessed=6 * MIB, transcendentals=0),
    )(meta, own_tiles, sib_tiles, *sources)


def split(value):
    high = value.astype(jnp.bfloat16)
    low = (value - high.astype(jnp.float32)).astype(jnp.bfloat16)
    return high, low


def dense_kernel(own_ref, sib_ref, weight_own, weight_sib, cotangent, activation, grads):
    own = split(own_ref[...])
    sib = split(sib_ref[...])
    preact = 0.0
    for weight, field in ((weight_own[...], own), (weight_sib[...], sib)):
        for part in field[::-1]:
            preact += jnp.dot(weight, part, preferred_element_type=jnp.float32)
    sigmoid = jax.nn.sigmoid(preact)
    activation[...] = (preact * sigmoid).astype(jnp.bfloat16)
    slope = (
        cotangent[...].astype(jnp.float32) * sigmoid * (1.0 + preact * (1.0 - sigmoid))
    ).astype(jnp.bfloat16)
    for side, field in enumerate((own, sib)):
        total = 0.0
        for part in field[::-1]:
            total += lax.dot_general(
                slope, part, (((1,), (1,)), ((), ())), preferred_element_type=jnp.float32
            )
        for copy in range(grads.shape[0]):
            grads[copy, :, side * HALF : (side + 1) * HALF] = total


def body(features, weight, tiles, pairs, counts, cotangent):
    at_h, at_c = lax.axis_index("h"), lax.axis_index("c")
    at_x = lax.axis_index("x")
    at_yl = lax.axis_index(("y", "l"))
    slot_total = tiles.shape[3]
    own_tiles = tiles.reshape(slot_total, TILE, TILE)
    pair_list = pairs.reshape(2, slot_total)
    count = counts.reshape(())

    keep = jnp.arange(slot_total) < count
    rows = ((pair_list[0] // PER_PIECE - at_yl) % 8) * PER_PIECE + pair_list[0] % PER_PIECE
    cols = ((pair_list[1] // PER_PIECE - at_x) % 4) * PER_PIECE + pair_list[1] % PER_PIECE
    groups = jnp.full((slot_total,), (count + GROUP - 1) // GROUP, jnp.int32)
    own_meta = jnp.stack(
        [
            jnp.where(keep, cols, 0),
            jnp.where(keep, rows, 32),
            jnp.where(keep, rows, 0),
            jnp.where(keep, cols, 16),
            groups,
        ]
    ).astype(jnp.int32)
    sib_meta = shifted(own_meta, "c", 1)
    sib_tiles = shifted(own_tiles, "c", 1)
    both = (own_meta, sib_meta)
    to_rows_meta = jnp.concatenate([m[i : i + 1] for m in both for i in (0, 1, 4)])
    to_cols_meta = jnp.concatenate([m[i : i + 1] for m in both for i in (2, 3, 4)])

    from_h = [shifted(features, "h", k) for k in (1, 2, 3)]
    field = pl.pallas_call(
        order_kernel,
        out_shape=jax.ShapeDtypeStruct((HALF, NODE_DEV), jnp.bfloat16),
        in_specs=[SMEM] + [VMEM] * 4,
        out_specs=VMEM,
    )(at_h.reshape(1), features, *from_h)

    col_seg = [field] + [shifted(field, "x", k) for k in range(1, 4)]
    row_seg = [field] + [shifted(field, ("y", "l"), k) for k in range(1, 8)]
    flops = 2 * 2 * 48 * HALF * TILE * TILE
    row_part = agg(to_rows_meta, own_tiles, sib_tiles, col_seg, 8, True, flops)
    row_got = [shifted(row_part[k], ("y", "l"), k) for k in range(1, 8)]
    col_part = agg(to_cols_meta, own_tiles, sib_tiles, row_seg, 4, False, flops)
    col_got = [shifted(col_part[k], "x", k) for k in range(1, 4)]
    share = sum(
        v.astype(jnp.float32) for v in (row_part[0], col_part[0], *row_got, *col_got)
    ).astype(jnp.bfloat16)
    shares = [share] + [shifted(share, "h", k) for k in (1, 2, 3)]
    total = sum(v.astype(jnp.float32) for v in shares)
    sib_total = shifted(total, "c", 1)

    weight_mine = lax.dynamic_slice_in_dim(weight, (at_h * 2 + at_c) * 32, 32, 1)
    weight_mine = weight_mine.reshape(4, 2, 32, 32)
    weight_own = lax.dynamic_index_in_dim(weight_mine, at_c, 1, False).reshape(HALF, 32).T
    weight_sib = lax.dynamic_index_in_dim(weight_mine, 1 - at_c, 1, False).reshape(HALF, 32).T
    activation, grads = pl.pallas_call(
        dense_kernel,
        out_shape=[
            jax.ShapeDtypeStruct((32, NODE_DEV), jnp.bfloat16),
            jax.ShapeDtypeStruct((32, 32, FEAT), jnp.float32),
        ],
        in_specs=[VMEM] * 5,
        out_specs=[VMEM] * 2,
        compiler_params=params(16),
    )(total, sib_total, weight_own, weight_sib, cotangent)
    grad = lax.all_to_all(grads, ("x", "y", "l"), 0, 0, tiled=True).sum(0)
    own_grad, sib_grad = grad[:, :HALF], grad[:, HALF:]
    first = jnp.where(at_c == 0, own_grad, sib_grad).reshape(32, 4, 32)
    second = jnp.where(at_c == 0, sib_grad, own_grad).reshape(32, 4, 32)
    grad = jnp.stack([first, second], 2).reshape(32, FEAT)
    return activation, grad.T


def solution(mesh):
    fine = Mesh(mesh.devices.reshape(4, 4, 2, 4, 2), ("x", "y", "l", "h", "c"))
    depth, col = ("h", "c"), ("y", "l")
    placed = (
        P(depth, ("x", "y", "l")),
        P(),
        P("x", col, depth, None, None, None),
        P("x", col, depth, None, None),
        P("x", col, depth),
        P(depth, ("x", "y", "l")),
    )
    return jax.shard_map(
        body,
        mesh=fine,
        in_specs=placed,
        out_specs=(P(depth, ("x", "y", "l")), P(None, depth)),
        check_vma=False,
    )
```

time: 1120 us -> 122 us (0.11)
  waiting for transfers between devices: 919 us -> 45.6 us
  other arithmetic: 69.8 us -> 1.29 us
  local copies, waits for them, and re-layouts: 65.8 us -> 4.5 us
  starting transfers between devices: 0.46 us -> 53.8 us
  matrix products: 50.8 us -> 0 us
  Pallas kernels: 0 us -> 14.5 us
  between operations: 14.9 us -> 1.56 us
    all_gather x4 -> x0, waiting for transfers between devices: 349 us -> none  [the longest x2 223 us: collect(): lax.all_gather(piece[None], ('col', 'depth'), axis=0, tiled=True)]
    reduce_scatter x2 -> x0, waiting for transfers between devices: 319 us -> none  [the longest x1 241 us: settle(): lax.psum_scatter(row_partial.reshape(-1, feat_share, NODE_DEV), ('col', '...]
    psum x1 -> x0, waiting for transfers between devices: 249 us -> none  [body(): summed_grad = lax.psum(partial_grad, ('row', 'col', 'depth'))]
    scatter-add x8 -> x0, other arithmetic: 68 us -> none  [the longest x4 40.2 us: visiting(): row_acc = row_acc.at[row_piece, :, row_offset, :].add(to_rows)]
    dot_general x12 -> x0, matrix products: 50.8 us -> none  [the longest x4 18.5 us: visiting(): jnp.einsum('gfj,gij->gfi', from_cols, tile_values, preferred_element_type...]
    ppermute x0 -> x29, starting transfers between devices: none -> 43.4 us  [shifted(): lax.ppermute(value, axes, [(i, (i + step) % total) for i in range(total)])]
    ppermute x0 -> x29, waiting for transfers between devices: none -> 28.7 us  [shifted(): lax.ppermute(value, axes, [(i, (i + step) % total) for i in range(total)])]
    gather x8 -> x0, local copies, waits for them, and re-layouts: 23.3 us -> none  [the longest x4 14.8 us: visiting(): from_rows = row_view[row_piece, :, row_offset, :]]
  transfers between devices with their start and end apart: 7 -> 30, of which waited for: 7 -> 13; matrix products, arithmetic and copies ran while one was open for 2% -> 1% of each run, Pallas kernels for 0% -> 11%
where the time goes in v1:
time: 122 us; the launch traced here: 121 us
  starting transfers between devices  53.8 us (44%)
  waiting for transfers between devices  45.6 us (37%)
  Pallas kernels  14.5 us (12%)
  local copies, waits for them, and re-layouts  4.5 us (4%)
  between operations  1.56 us (1%)
  other arithmetic  1.29 us (1%)
    ppermute x29, starting transfers between devices, shifted(): lax.ppermute(value, axes, [(i, (i + step) % total) for i in range(total)])  43.4 us
    ppermute x29, waiting for transfers between devices, shifted(): lax.ppermute(value, axes, [(i, (i + step) % total) for i in range(total)])  28.7 us
    all_to_all x1, waiting for transfers between devices, body(): grad = lax.all_to_all(grads, ('x', 'y', 'l'), 0, 0, tiled=True).sum(0)  16.9 us
    pallas_call x2, Pallas kernels, agg(): pl.pallas_call(functools.partial(agg_kernel, pieces, outs, transpose), ou...  11.5 us
    all_to_all x1, starting transfers between devices, body(): grad = lax.all_to_all(grads, ('x', 'y', 'l'), 0, 0, tiled=True).sum(0)  10.4 us
    unnamed x16, local copies, waits for them, and re-layouts  3.12 us
  transfers between devices with their start and end apart: 30, of which 13 were waited for; matrix products, arithmetic and copies ran while one was open for 1% of the time, Pallas kernels for 11%

profile of v1, /device:TPU:8, one launch (start us, length us, event | category | flops | bytes accessed | tf_op | source)
XLA Modules:
  0.0 121.3 jit_solution(13875706390040240614)
XLA Ops:
  0.7 3.3 %collective-permute-start.2 = (bf16[32,512]{1,0:T(8,128)(2,1)}, bf16[32,512]{1,0:T(8,128)(2,1)S(1)}, u32[]{:S(2)}, u32[]{:S(2)}) collective-permute-start(bf16[32,512]{1,0:T(8,128)(2,1)} %own.1), channel_id=1, source_target_pairs={{0,2},{2,4},{4,6},{6,0},{1,3},{3,5},{5,7},{7,1},{8,10},{10,12},{12... | collective-permute-start | bytes 98312 | tf_op jit(solution)/shard_map/ppermute | solution.py:28
  4.1 5.4 %collective-permute-start.3 = (bf16[32,512]{1,0:T(8,128)(2,1)}, bf16[32,512]{1,0:T(8,128)(2,1)S(1)}, u32[]{:S(2)}, u32[]{:S(2)}) collective-permute-start(bf16[32,512]{1,0:T(8,128)(2,1)} %own.1), channel_id=1, source_target_pairs={{0,4},{2,6},{4,0},{6,2},{1,5},{3,7},{5,1},{7,3},{8,12},{10,14},{12... | collective-permute-start | bytes 98312 | tf_op jit(solution)/shard_map/ppermute | solution.py:28
  9.5 2.7 %collective-permute-start.4 = (bf16[32,512]{1,0:T(8,128)(2,1)}, bf16[32,512]{1,0:T(8,128)(2,1)S(1)}, u32[]{:S(2)}, u32[]{:S(2)}) collective-permute-start(bf16[32,512]{1,0:T(8,128)(2,1)} %own.1), channel_id=1, source_target_pairs={{0,6},{2,0},{4,2},{6,4},{1,7},{3,1},{5,3},{7,5},{8,14},{10,8},{12,... | collective-permute-start | bytes 98312 | tf_op jit(solution)/shard_map/ppermute | solution.py:28
  12.8 0.8 fusion.7
  13.6 0.9 collective-permute-done.4.r3
  14.6 0.6 copy-done.7
  15.2 1.5 %shard_map.77.refs_0_ = bf16[128,512]{1,0:T(8,128)(2,1)} custom-call(s32[1]{0:T(128)} %bitcast.4.place, bf16[32,512]{1,0:T(8,128)(2,1)} %own.1, bf16[32,512]{1,0:T(8,128)(2,1)} %copy-done.5, bf16[32,512]{1,0:T(8,128)(2,1)} %copy-done.6, bf16[32,512]{1,0:T(8,128)(2,1)} %copy-done.7), custom_call_target="tpu_custom_call" | custom-call | tf_op jit(solution)/shard_map/pallas_call | solution.py:148
  16.6 1.0 collective-permute-start.8
  17.6 1.6 %collective-permute-start.9 = (bf16[128,512]{1,0:T(8,128)(2,1)}, bf16[128,512]{1,0:T(8,128)(2,1)S(1)}, u32[]{:S(2)}, u32[]{:S(2)}) collective-permute-start(bf16[128,512]{1,0:T(8,128)(2,1)} %shard_map.77.refs_0_), channel_id=1, source_target_pairs={{0,16},{8,24},{16,32},{24,40},{32,48},{40,56},{48,0},{56,8},{1,17}... | collective-permute-start | bytes 393224 | tf_op jit(solution)/shard_map/ppermute | solution.py:28
  19.2 1.4 %collective-permute-start.10 = (bf16[128,512]{1,0:T(8,128)(2,1)}, bf16[128,512]{1,0:T(8,128)(2,1)S(1)}, u32[]{:S(2)}, u32[]{:S(2)}) collective-permute-start(bf16[128,512]{1,0:T(8,128)(2,1)} %shard_map.77.refs_0_), channel_id=1, source_target_pairs={{0,24},{8,32},{16,40},{24,48},{32,56},{40,0},{48,8},{56,16},{1,25}... | collective-permute-start | bytes 393224 | tf_op jit(solution)/shard_map/ppermute | solution.py:28
  20.7 1.2 collective-permute-done
  21.9 2.6 %collective-permute-start.11 = (bf16[128,512]{1,0:T(8,128)(2,1)}, bf16[128,512]{1,0:T(8,128)(2,1)S(1)}, u32[]{:S(2)}, u32[]{:S(2)}) collective-permute-start(bf16[128,512]{1,0:T(8,128)(2,1)} %shard_map.77.refs_0_), channel_id=1, source_target_pairs={{0,32},{8,40},{16,48},{24,56},{32,0},{40,8},{48,16},{56,24},{1,33}... | collective-permute-start | bytes 393224 | tf_op jit(solution)/shard_map/ppermute | solution.py:28
  24.5 1.3 %collective-permute-start.12 = (bf16[128,512]{1,0:T(8,128)(2,1)}, bf16[128,512]{1,0:T(8,128)(2,1)S(1)}, u32[]{:S(2)}, u32[]{:S(2)}) collective-permute-start(bf16[128,512]{1,0:T(8,128)(2,1)} %shard_map.77.refs_0_), channel_id=1, source_target_pairs={{0,40},{8,48},{16,56},{24,0},{32,8},{40,16},{48,24},{56,32},{1,41}... | collective-permute-start | bytes 393224 | tf_op jit(solution)/shard_map/ppermute | solution.py:28
  25.8 2.1 %collective-permute-done.9.refs_2_ = bf16[128,512]{1,0:T(8,128)(2,1)S(1)} collective-permute-done((bf16[128,512]{1,0:T(8,128)(2,1)}, bf16[128,512]{1,0:T(8,128)(2,1)S(1)}, u32[]{:S(2)}, u32[]{:S(2)}) %collective-permute-start.9) | collective-permute-done | bytes 131104 | tf_op jit(solution)/shard_map/ppermute | solution.py:28
  27.9 1.2 collective-permute-start.13
  29.1 0.8 collective-permute-start.14
  29.9 2.8 %collective-permute-done.11.refs_4_ = bf16[128,512]{1,0:T(8,128)(2,1)S(1)} collective-permute-done((bf16[128,512]{1,0:T(8,128)(2,1)}, bf16[128,512]{1,0:T(8,128)(2,1)S(1)}, u32[]{:S(2)}, u32[]{:S(2)}) %collective-permute-start.11) | collective-permute-done | bytes 131104 | tf_op jit(solution)/shard_map/ppermute | solution.py:28
  32.7 1.5 %collective-permute-start.5 = (bf16[128,512]{1,0:T(8,128)(2,1)}, bf16[128,512]{1,0:T(8,128)(2,1)S(1)}, u32[]{:S(2)}, u32[]{:S(2)}) collective-permute-start(bf16[128,512]{1,0:T(8,128)(2,1)} %shard_map.77.refs_0_), channel_id=1, source_target_pairs={{0,64},{64,128},{128,192},{192,0},{1,65},{65,129},{129,193},{193,1... | collective-permute-start | bytes 393224 | tf_op jit(solution)/shard_map/ppermute | solution.py:28
  34.2 2.7 %collective-permute-start.6 = (bf16[128,512]{1,0:T(8,128)(2,1)}, bf16[128,512]{1,0:T(8,128)(2,1)S(1)}, u32[]{:S(2)}, u32[]{:S(2)}) collective-permute-start(bf16[128,512]{1,0:T(8,128)(2,1)} %shard_map.77.refs_0_), channel_id=1, source_target_pairs={{0,128},{64,192},{128,0},{192,64},{1,129},{65,193},{129,1},{193,65... | collective-permute-start | bytes 393224 | tf_op jit(solution)/shard_map/ppermute | solution.py:28
  36.9 1.4 %collective-permute-start.7 = (bf16[128,512]{1,0:T(8,128)(2,1)}, bf16[128,512]{1,0:T(8,128)(2,1)S(1)}, u32[]{:S(2)}, u32[]{:S(2)}) collective-permute-start(bf16[128,512]{1,0:T(8,128)(2,1)} %shard_map.77.refs_0_), channel_id=1, source_target_pairs={{0,192},{64,0},{128,64},{192,128},{1,193},{65,1},{129,65},{193,129... | collective-permute-start | bytes 393224 | tf_op jit(solution)/shard_map/ppermute | solution.py:28
  38.4 1.6 %copy-done.1 = bf16[1,1,1,64,128,128]{5,4,3,2,1,0:T(8,128)(2,1)S(1)} copy-done((bf16[1,1,1,64,128,128]{5,4,3,2,1,0:T(8,128)(2,1)S(1)}, bf16[1,1,1,64,128,128]{5,4,3,2,1,0:T(8,128)(2,1)}, u32[]{:S(2)}) %copy-start.1) | copy-done | bytes 2097176
  40.0 0.9 copy-done.3
  40.9 5.3 %shard_map.79 = (bf16[128,512]{1,0:T(8,128)(2,1)S(1)}, bf16[128,512]{1,0:T(8,128)(2,1)S(1)}, bf16[128,512]{1,0:T(8,128)(2,1)S(1)}, bf16[128,512]{1,0:T(8,128)(2,1)S(1)}) custom-call(s32[6,64]{1,0:T(8,128)S(1)} %pad_add_fusion.meta, bf16[64,128,128]{2,1,0:T(8,128)(2,1)S(1)} %bitcast.45, bf16[64,128,128]{2,1,0:T(8,128)(2,1)S(1)} %collective-permute-done.1.sib_tiles, ...), custom_call_target="tpu_custom_call" | custom-call | flops 402653184 | bytes 6291456 | tf_op jit(solution)/shard_map/pallas_call | solution.py:77
  46.3 2.3 %collective-permute-start.23 = (bf16[128,512]{1,0:T(8,128)(2,1)S(1)}, bf16[128,512]{1,0:T(8,128)(2,1)S(1)}, u32[]{:S(2)}, u32[]{:S(2)}) collective-permute-start(bf16[128,512]{1,0:T(8,128)(2,1)S(1)} %get-tuple-element.26), channel_id=1, source_target_pairs={{0,128},{64,192},{128,0},{192,64},{1,129},{65,193},{129,1},{193,65... | collective-permute-start | bytes 393224 | tf_op jit(solution)/shard_map/ppermute | solution.py:28
  48.6 6.2 %shard_map.78 = (bf16[128,512]{1,0:T(8,128)(2,1)S(1)}, bf16[128,512]{1,0:T(8,128)(2,1)S(1)}, bf16[128,512]{1,0:T(8,128)(2,1)S(1)}, bf16[128,512]{1,0:T(8,128)(2,...) custom-call(s32[6,64]{1,0:T(8,128)S(1)} %concatenate.6.meta, ...), custom_call_target="tpu_custom_call" | custom-call | flops 402653184 | bytes 6291456 | tf_op jit(solution)/shard_map/pallas_call | solution.py:77
  54.8 2.3 %collective-permute-start.21 = (bf16[128,512]{1,0:T(8,128)(2,1)S(1)}, bf16[128,512]{1,0:T(8,128)(2,1)S(1)}, u32[]{:S(2)}, u32[]{:S(2)}) collective-permute-start(bf16[128,512]{1,0:T(8,128)(2,1)S(1)} %get-tuple-element.24), channel_id=1, source_target_pairs={{0,56},{8,0},{16,8},{24,16},{32,24},{40,32},{48,40},{56,48},{1,57}... | collective-permute-start | bytes 393224 | tf_op jit(solution)/shard_map/ppermute | solution.py:28
  57.1 0.4 collective-permute-start.20
  57.6 3.2 %collective-permute-start.18 = (bf16[128,512]{1,0:T(8,128)(2,1)S(1)}, bf16[128,512]{1,0:T(8,128)(2,1)S(1)}, u32[]{:S(2)}, u32[]{:S(2)}) collective-permute-start(bf16[128,512]{1,0:T(8,128)(2,1)S(1)} %get-tuple-element.21), channel_id=1, source_target_pairs={{0,32},{8,40},{16,48},{24,56},{32,0},{40,8},{48,16},{56,24},{1,33}... | collective-permute-start | bytes 393224 | tf_op jit(solution)/shard_map/ppermute | solution.py:28
  60.8 0.3 collective-permute-done.21
  61.1 1.8 %collective-permute-start.16 = (bf16[128,512]{1,0:T(8,128)(2,1)S(1)}, bf16[128,512]{1,0:T(8,128)(2,1)S(1)}, u32[]{:S(2)}, u32[]{:S(2)}) collective-permute-start(bf16[128,512]{1,0:T(8,128)(2,1)S(1)} %get-tuple-element.19), channel_id=1, source_target_pairs={{0,16},{8,24},{16,32},{24,40},{32,48},{40,56},{48,0},{56,8},{1,17}... | collective-permute-start | bytes 393224 | tf_op jit(solution)/shard_map/ppermute | solution.py:28
  62.8 6.3 %collective-permute-done.20 = bf16[128,512]{1,0:T(8,128)(2,1)S(1)} collective-permute-done((bf16[128,512]{1,0:T(8,128)(2,1)S(1)}, bf16[128,512]{1,0:T(8,128)(2,1)S(1)}, u32[]{:S(2)}, u32[]{:S(2)}) %collective-permute-start.20) | collective-permute-done | bytes 131104 | tf_op jit(solution)/shard_map/ppermute | solution.py:28
  69.2 0.7 collective-permute-done.16
  69.9 5.1 %collective-permute-done.15 = bf16[128,512]{1,0:T(8,128)(2,1)S(1)} collective-permute-done((bf16[128,512]{1,0:T(8,128)(2,1)S(1)}, bf16[128,512]{1,0:T(8,128)(2,1)S(1)}, u32[]{:S(2)}, u32[]{:S(2)}) %collective-permute-start.15) | collective-permute-done | bytes 131104 | tf_op jit(solution)/shard_map/ppermute | solution.py:28
  75.0 0.2 add_convert_fusion
  75.3 1.4 %collective-permute-start.27 = (bf16[128,512]{1,0:T(8,128)(2,1)S(1)}, bf16[128,512]{1,0:T(8,128)(2,1)S(1)}, u32[]{:S(2)}, u32[]{:S(2)}) collective-permute-start(bf16[128,512]{1,0:T(8,128)(2,1)S(1)} %add_convert_fusion), channel_id=1, source_target_pairs={{0,6},{2,0},{4,2},{6,4},{1,7},{3,1},{5,3},{7,5},{8,14},{10,8},{12,... | collective-permute-start | bytes 393224 | tf_op jit(solution)/shard_map/ppermute | solution.py:28
  76.6 2.0 %collective-permute-start.26 = (bf16[128,512]{1,0:T(8,128)(2,1)S(1)}, bf16[128,512]{1,0:T(8,128)(2,1)S(1)}, u32[]{:S(2)}, u32[]{:S(2)}) collective-permute-start(bf16[128,512]{1,0:T(8,128)(2,1)S(1)} %add_convert_fusion), channel_id=1, source_target_pairs={{0,4},{2,6},{4,0},{6,2},{1,5},{3,7},{5,1},{7,3},{8,12},{10,14},{12... | collective-permute-start | bytes 393224 | tf_op jit(solution)/shard_map/ppermute | solution.py:28
  78.6 2.8 %collective-permute-start.25 = (bf16[128,512]{1,0:T(8,128)(2,1)S(1)}, bf16[128,512]{1,0:T(8,128)(2,1)S(1)}, u32[]{:S(2)}, u32[]{:S(2)}) collective-permute-start(bf16[128,512]{1,0:T(8,128)(2,1)S(1)} %add_convert_fusion), channel_id=1, source_target_pairs={{0,2},{2,4},{4,6},{6,0},{1,3},{3,5},{5,7},{7,1},{8,10},{10,12},{12... | collective-permute-start | bytes 393224 | tf_op jit(solution)/shard_map/ppermute | solution.py:28
  81.4 3.4 %collective-permute-done.27 = bf16[128,512]{1,0:T(8,128)(2,1)S(1)} collective-permute-done((bf16[128,512]{1,0:T(8,128)(2,1)S(1)}, bf16[128,512]{1,0:T(8,128)(2,1)S(1)}, u32[]{:S(2)}, u32[]{:S(2)}) %collective-permute-start.27) | collective-permute-done | bytes 131104 | tf_op jit(solution)/shard_map/ppermute | solution.py:28
  84.8 1.5 %collective-permute-done.26 = bf16[128,512]{1,0:T(8,128)(2,1)S(1)} collective-permute-done((bf16[128,512]{1,0:T(8,128)(2,1)S(1)}, bf16[128,512]{1,0:T(8,128)(2,1)S(1)}, u32[]{:S(2)}, u32[]{:S(2)}) %collective-permute-start.26) | collective-permute-done | bytes 131104 | tf_op jit(solution)/shard_map/ppermute | solution.py:28
  86.3 3.1 %collective-permute-done.25 = bf16[128,512]{1,0:T(8,128)(2,1)S(1)} collective-permute-done((bf16[128,512]{1,0:T(8,128)(2,1)S(1)}, bf16[128,512]{1,0:T(8,128)(2,1)S(1)}, u32[]{:S(2)}, u32[]{:S(2)}) %collective-permute-start.25) | collective-permute-done | bytes 131104 | tf_op jit(solution)/shard_map/ppermute | solution.py:28
  89.9 1.2 %collective-permute-done.28.sib_ref = f32[128,512]{1,0:T(8,128)S(1)} collective-permute-done((f32[128,512]{1,0:T(8,128)S(1)}, f32[128,512]{1,0:T(8,128)S(1)}, u32[]{:S(2)}, u32[]{:S(2)}) %collective-permute-start.28) | collective-permute-done | bytes 262176 | tf_op jit(solution)/shard_map/ppermute | solution.py:28
  91.1 1.6 %shard_map.80 = (bf16[32,512]{1,0:T(8,128)(2,1)}, f32[32,32,256]{2,1,0:T(8,128)}) custom-call(f32[128,512]{1,0:T(8,128)S(1)} %convert_add_fusion.own_ref, f32[128,512]{1,0:T(8,128)S(1)} %collective-permute-done.28.sib_ref, bf16[32,128]{1,0:T(8,128)(2,1)S(1)} %bitcast.47, bf16[32,128]{1,0:T(8,128)(2,1)S(1)} %bitcast.48, bf16[32,512]{1,0:T(8,128)(2,1)S(1)} %copy-done.4), custom_call_target="tpu_custom_call" | custom-call | tf_op jit(solution)/shard_map/pallas_call | solution.py:173
  92.7 10.4 %all-to-all-start = ((f32[32,32,256]{2,1,0:T(8,128)}), f32[32,32,256]{2,1,0:T(8,128)S(1)}, u32[]{:S(2)}, u32[]{:S(2)}) async-start(f32[32,32,256]{2,1,0:T(8,128)} %get-tuple-element.29), calls=%async_computation | async-start | bytes 2097152 | tf_op jit(solution)/shard_map/all_to_all | solution.py:183
  103.1 16.9 %all-to-all-done = f32[32,32,256]{2,1,0:T(8,128)S(1)} async-done(((f32[32,32,256]{2,1,0:T(8,128)}), f32[32,32,256]{2,1,0:T(8,128)S(1)}, u32[]{:S(2)}, u32[]{:S(2)}) %all-to-all-start) | async-done | bytes 1048608 | tf_op jit(solution)/shard_map/all_to_all | solution.py:183
  120.1 0.1 stack_reshape.7
  120.2 0.1 stack_reshape.6
  120.4 0.2 pad_maximum_fusion
  120.5 0.8 reshape.366
  (53 shorter events, 0.9 us)
Async XLA Ops:
  0.6 88.9 %copy-start = (bf16[256,256]{1,0:T(8,128)(2,1)S(1)}, bf16[256,256]{1,0:T(8,128)(2,1)}, u32[]{:S(2)}) copy-start(bf16[256,256]{1,0:T(8,128)(2,1)} %param.7) | copy-start | bytes 393220
  0.6 37.7 %collective-permute-start.1 = (bf16[64,128,128]{2,1,0:T(8,128)(2,1)}, bf16[64,128,128]{2,1,0:T(8,128)(2,1)S(1)}, u32[]{:S(2)}, u32[]{:S(2)}) collective-permute-start(bf16[64,128,128]{2,1,0:T(8,128)(2,1)} %bitcast.44), channel_id=1, source_target_pairs={{0,1},{1,0},{2,3},{3,2},{4,5},{5,4},{6,7},{7,6},{8,9},{9,8},{10,11... | collective-permute-start | bytes 6291464 | tf_op jit(solution)/shard_map/ppermute | solution.py:28
  0.7 12.8 %collective-permute-start.2 = (bf16[32,512]{1,0:T(8,128)(2,1)}, bf16[32,512]{1,0:T(8,128)(2,1)S(1)}, u32[]{:S(2)}, u32[]{:S(2)}) collective-permute-start(bf16[32,512]{1,0:T(8,128)(2,1)} %own.1), channel_id=1, source_target_pairs={{0,2},{2,4},{4,6},{6,0},{1,3},{3,5},{5,7},{7,1},{8,10},{10,12},{12... | collective-permute-start | bytes 98312 | tf_op jit(solution)/shard_map/ppermute | solution.py:28
  4.1 9.5 %collective-permute-start.3 = (bf16[32,512]{1,0:T(8,128)(2,1)}, bf16[32,512]{1,0:T(8,128)(2,1)S(1)}, u32[]{:S(2)}, u32[]{:S(2)}) collective-permute-start(bf16[32,512]{1,0:T(8,128)(2,1)} %own.1), channel_id=1, source_target_pairs={{0,4},{2,6},{4,0},{6,2},{1,5},{3,7},{5,1},{7,3},{8,12},{10,14},{12... | collective-permute-start | bytes 98312 | tf_op jit(solution)/shard_map/ppermute | solution.py:28
  9.5 5.1 %collective-permute-start.4 = (bf16[32,512]{1,0:T(8,128)(2,1)}, bf16[32,512]{1,0:T(8,128)(2,1)S(1)}, u32[]{:S(2)}, u32[]{:S(2)}) collective-permute-start(bf16[32,512]{1,0:T(8,128)(2,1)} %own.1), channel_id=1, source_target_pairs={{0,6},{2,0},{4,2},{6,4},{1,7},{3,1},{5,3},{7,5},{8,14},{10,8},{12,... | collective-permute-start | bytes 98312 | tf_op jit(solution)/shard_map/ppermute | solution.py:28
  13.6 1.0 copy-start.5
  13.6 1.0 copy-start.6
  14.6 0.6 copy-start.7
  16.6 7.9 %collective-permute-start.8 = (bf16[128,512]{1,0:T(8,128)(2,1)}, bf16[128,512]{1,0:T(8,128)(2,1)S(1)}, u32[]{:S(2)}, u32[]{:S(2)}) collective-permute-start(bf16[128,512]{1,0:T(8,128)(2,1)} %shard_map.77.refs_0_), channel_id=1, source_target_pairs={{0,8},{8,16},{16,24},{24,32},{32,40},{40,48},{48,56},{56,0},{1,9},... | collective-permute-start | bytes 393224 | tf_op jit(solution)/shard_map/ppermute | solution.py:28
  17.6 10.3 %collective-permute-start.9 = (bf16[128,512]{1,0:T(8,128)(2,1)}, bf16[128,512]{1,0:T(8,128)(2,1)S(1)}, u32[]{:S(2)}, u32[]{:S(2)}) collective-permute-start(bf16[128,512]{1,0:T(8,128)(2,1)} %shard_map.77.refs_0_), channel_id=1, source_target_pairs={{0,16},{8,24},{16,32},{24,40},{32,48},{40,56},{48,0},{56,8},{1,17}... | collective-permute-start | bytes 393224 | tf_op jit(solution)/shard_map/ppermute | solution.py:28
  19.2 9.9 %collective-permute-start.10 = (bf16[128,512]{1,0:T(8,128)(2,1)}, bf16[128,512]{1,0:T(8,128)(2,1)S(1)}, u32[]{:S(2)}, u32[]{:S(2)}) collective-permute-start(bf16[128,512]{1,0:T(8,128)(2,1)} %shard_map.77.refs_0_), channel_id=1, source_target_pairs={{0,24},{8,32},{16,40},{24,48},{32,56},{40,0},{48,8},{56,16},{1,25}... | collective-permute-start | bytes 393224 | tf_op jit(solution)/shard_map/ppermute | solution.py:28
  20.6 1.2 %collective-permute-start = (s32[5,64]{1,0:T(8,128)S(1)}, s32[5,64]{1,0:T(8,128)S(1)}, u32[]{:S(2)}, u32[]{:S(2)}) collective-permute-start(s32[5,64]{1,0:T(8,128)S(1)} %stack.4), channel_id=1, source_target_pairs={{0,1},{1,0},{2,3},{3,2},{4,5},{5,4},{6,7},{7,6},{8,9},{9,8},{10,11... | collective-permute-start | bytes 3848 | tf_op jit(solution)/shard_map/ppermute | solution.py:28
  21.9 10.8 %collective-permute-start.11 = (bf16[128,512]{1,0:T(8,128)(2,1)}, bf16[128,512]{1,0:T(8,128)(2,1)S(1)}, u32[]{:S(2)}, u32[]{:S(2)}) collective-permute-start(bf16[128,512]{1,0:T(8,128)(2,1)} %shard_map.77.refs_0_), channel_id=1, source_target_pairs={{0,32},{8,40},{16,48},{24,56},{32,0},{40,8},{48,16},{56,24},{1,33}... | collective-permute-start | bytes 393224 | tf_op jit(solution)/shard_map/ppermute | solution.py:28
  24.5 9.7 %collective-permute-start.12 = (bf16[128,512]{1,0:T(8,128)(2,1)}, bf16[128,512]{1,0:T(8,128)(2,1)S(1)}, u32[]{:S(2)}, u32[]{:S(2)}) collective-permute-start(bf16[128,512]{1,0:T(8,128)(2,1)} %shard_map.77.refs_0_), channel_id=1, source_target_pairs={{0,40},{8,48},{16,56},{24,0},{32,8},{40,16},{48,24},{56,32},{1,41}... | collective-permute-start | bytes 393224 | tf_op jit(solution)/shard_map/ppermute | solution.py:28
  27.9 9.0 %collective-permute-start.13 = (bf16[128,512]{1,0:T(8,128)(2,1)}, bf16[128,512]{1,0:T(8,128)(2,1)S(1)}, u32[]{:S(2)}, u32[]{:S(2)}) collective-permute-start(bf16[128,512]{1,0:T(8,128)(2,1)} %shard_map.77.refs_0_), channel_id=1, source_target_pairs={{0,48},{8,56},{16,0},{24,8},{32,16},{40,24},{48,32},{56,40},{1,49}... | collective-permute-start | bytes 393224 | tf_op jit(solution)/shard_map/ppermute | solution.py:28
  29.1 9.3 %collective-permute-start.14 = (bf16[128,512]{1,0:T(8,128)(2,1)}, bf16[128,512]{1,0:T(8,128)(2,1)S(1)}, u32[]{:S(2)}, u32[]{:S(2)}) collective-permute-start(bf16[128,512]{1,0:T(8,128)(2,1)} %shard_map.77.refs_0_), channel_id=1, source_target_pairs={{0,56},{8,0},{16,8},{24,16},{32,24},{40,32},{48,40},{56,48},{1,57}... | collective-permute-start | bytes 393224 | tf_op jit(solution)/shard_map/ppermute | solution.py:28
  32.7 15.9 %collective-permute-start.5 = (bf16[128,512]{1,0:T(8,128)(2,1)}, bf16[128,512]{1,0:T(8,128)(2,1)S(1)}, u32[]{:S(2)}, u32[]{:S(2)}) collective-permute-start(bf16[128,512]{1,0:T(8,128)(2,1)} %shard_map.77.refs_0_), channel_id=1, source_target_pairs={{0,64},{64,128},{128,192},{192,0},{1,65},{65,129},{129,193},{193,1... | collective-permute-start | bytes 393224 | tf_op jit(solution)/shard_map/ppermute | solution.py:28
  34.2 14.4 %collective-permute-start.6 = (bf16[128,512]{1,0:T(8,128)(2,1)}, bf16[128,512]{1,0:T(8,128)(2,1)S(1)}, u32[]{:S(2)}, u32[]{:S(2)}) collective-permute-start(bf16[128,512]{1,0:T(8,128)(2,1)} %shard_map.77.refs_0_), channel_id=1, source_target_pairs={{0,128},{64,192},{128,0},{192,64},{1,129},{65,193},{129,1},{193,65... | collective-permute-start | bytes 393224 | tf_op jit(solution)/shard_map/ppermute | solution.py:28
  36.9 11.7 %collective-permute-start.7 = (bf16[128,512]{1,0:T(8,128)(2,1)}, bf16[128,512]{1,0:T(8,128)(2,1)S(1)}, u32[]{:S(2)}, u32[]{:S(2)}) collective-permute-start(bf16[128,512]{1,0:T(8,128)(2,1)} %shard_map.77.refs_0_), channel_id=1, source_target_pairs={{0,192},{64,0},{128,64},{192,128},{1,193},{65,1},{129,65},{193,129... | collective-permute-start | bytes 393224 | tf_op jit(solution)/shard_map/ppermute | solution.py:28
  38.4 1.6 %copy-start.1 = (bf16[1,1,1,64,128,128]{5,4,3,2,1,0:T(8,128)(2,1)S(1)}, bf16[1,1,1,64,128,128]{5,4,3,2,1,0:T(8,128)(2,1)}, u32[]{:S(2)}) copy-start(bf16[1,1,1,64,128,128]{5,4,3,2,1,0:T(8,128)(2,1)} %param.8) | copy-start | bytes 6291460
  40.0 0.9 copy-start.3
  40.9 7.7 %copy-start.2 = (bf16[1,1,1,64,128,128]{5,4,3,2,1,0:T(8,128)(2,1)S(1)}, bf16[1,1,1,64,128,128]{5,4,3,2,1,0:T(8,128)(2,1)}, u32[]{:S(2)}) copy-start(bf16[1,1,1,64,128,128]{5,4,3,2,1,0:T(8,128)(2,1)} %param.8) | copy-start | bytes 6291460
  46.2 11.4 %collective-permute-start.24 = (bf16[128,512]{1,0:T(8,128)(2,1)S(1)}, bf16[128,512]{1,0:T(8,128)(2,1)S(1)}, u32[]{:S(2)}, u32[]{:S(2)}) collective-permute-start(bf16[128,512]{1,0:T(8,128)(2,1)S(1)} %get-tuple-element.27), channel_id=1, source_target_pairs={{0,192},{64,0},{128,64},{192,128},{1,193},{65,1},{129,65},{193,129... | collective-permute-start | bytes 393224 | tf_op jit(solution)/shard_map/ppermute | solution.py:28
  46.3 11.3 %collective-permute-start.23 = (bf16[128,512]{1,0:T(8,128)(2,1)S(1)}, bf16[128,512]{1,0:T(8,128)(2,1)S(1)}, u32[]{:S(2)}, u32[]{:S(2)}) collective-permute-start(bf16[128,512]{1,0:T(8,128)(2,1)S(1)} %get-tuple-element.26), channel_id=1, source_target_pairs={{0,128},{64,192},{128,0},{192,64},{1,129},{65,193},{129,1},{193,65... | collective-permute-start | bytes 393224 | tf_op jit(solution)/shard_map/ppermute | solution.py:28
  48.6 12.2 %collective-permute-start.22 = (bf16[128,512]{1,0:T(8,128)(2,1)S(1)}, bf16[128,512]{1,0:T(8,128)(2,1)S(1)}, u32[]{:S(2)}, u32[]{:S(2)}) collective-permute-start(bf16[128,512]{1,0:T(8,128)(2,1)S(1)} %get-tuple-element.25), channel_id=1, source_target_pairs={{0,64},{64,128},{128,192},{192,0},{1,65},{65,129},{129,193},{193,1... | collective-permute-start | bytes 393224 | tf_op jit(solution)/shard_map/ppermute | solution.py:28
  54.8 36.3 %copy-start.4 = (bf16[32,512]{1,0:T(8,128)(2,1)S(1)}, bf16[32,512]{1,0:T(8,128)(2,1)}, u32[]{:S(2)}) copy-start(bf16[32,512]{1,0:T(8,128)(2,1)} %cotangent.1) | copy-start | bytes 98308
  54.8 6.3 %collective-permute-start.21 = (bf16[128,512]{1,0:T(8,128)(2,1)S(1)}, bf16[128,512]{1,0:T(8,128)(2,1)S(1)}, u32[]{:S(2)}, u32[]{:S(2)}) collective-permute-start(bf16[128,512]{1,0:T(8,128)(2,1)S(1)} %get-tuple-element.24), channel_id=1, source_target_pairs={{0,56},{8,0},{16,8},{24,16},{32,24},{40,32},{48,40},{56,48},{1,57}... | collective-permute-start | bytes 393224 | tf_op jit(solution)/shard_map/ppermute | solution.py:28
  57.1 12.0 %collective-permute-start.20 = (bf16[128,512]{1,0:T(8,128)(2,1)S(1)}, bf16[128,512]{1,0:T(8,128)(2,1)S(1)}, u32[]{:S(2)}, u32[]{:S(2)}) collective-permute-start(bf16[128,512]{1,0:T(8,128)(2,1)S(1)} %get-tuple-element.23), channel_id=1, source_target_pairs={{0,48},{8,56},{16,0},{24,8},{32,16},{40,24},{48,32},{56,40},{1,49}... | collective-permute-start | bytes 393224 | tf_op jit(solution)/shard_map/ppermute | solution.py:28
  57.6 11.6 %collective-permute-start.19 = (bf16[128,512]{1,0:T(8,128)(2,1)S(1)}, bf16[128,512]{1,0:T(8,128)(2,1)S(1)}, u32[]{:S(2)}, u32[]{:S(2)}) collective-permute-start(bf16[128,512]{1,0:T(8,128)(2,1)S(1)} %get-tuple-element.22), channel_id=1, source_target_pairs={{0,40},{8,48},{16,56},{24,0},{32,8},{40,16},{48,24},{56,32},{1,41}... | collective-permute-start | bytes 393224 | tf_op jit(solution)/shard_map/ppermute | solution.py:28
  57.6 11.6 %collective-permute-start.18 = (bf16[128,512]{1,0:T(8,128)(2,1)S(1)}, bf16[128,512]{1,0:T(8,128)(2,1)S(1)}, u32[]{:S(2)}, u32[]{:S(2)}) collective-permute-start(bf16[128,512]{1,0:T(8,128)(2,1)S(1)} %get-tuple-element.21), channel_id=1, source_target_pairs={{0,32},{8,40},{16,48},{24,56},{32,0},{40,8},{48,16},{56,24},{1,33}... | collective-permute-start | bytes 393224 | tf_op jit(solution)/shard_map/ppermute | solution.py:28
  60.8 8.4 %collective-permute-start.17 = (bf16[128,512]{1,0:T(8,128)(2,1)S(1)}, bf16[128,512]{1,0:T(8,128)(2,1)S(1)}, u32[]{:S(2)}, u32[]{:S(2)}) collective-permute-start(bf16[128,512]{1,0:T(8,128)(2,1)S(1)} %get-tuple-element.20), channel_id=1, source_target_pairs={{0,24},{8,32},{16,40},{24,48},{32,56},{40,0},{48,8},{56,16},{1,25}... | collective-permute-start | bytes 393224 | tf_op jit(solution)/shard_map/ppermute | solution.py:28
  61.1 8.9 %collective-permute-start.16 = (bf16[128,512]{1,0:T(8,128)(2,1)S(1)}, bf16[128,512]{1,0:T(8,128)(2,1)S(1)}, u32[]{:S(2)}, u32[]{:S(2)}) collective-permute-start(bf16[128,512]{1,0:T(8,128)(2,1)S(1)} %get-tuple-element.19), channel_id=1, source_target_pairs={{0,16},{8,24},{16,32},{24,40},{32,48},{40,56},{48,0},{56,8},{1,17}... | collective-permute-start | bytes 393224 | tf_op jit(solution)/shard_map/ppermute | solution.py:28
  69.2 5.9 %collective-permute-start.15 = (bf16[128,512]{1,0:T(8,128)(2,1)S(1)}, bf16[128,512]{1,0:T(8,128)(2,1)S(1)}, u32[]{:S(2)}, u32[]{:S(2)}) collective-permute-start(bf16[128,512]{1,0:T(8,128)(2,1)S(1)} %get-tuple-element.18), channel_id=1, source_target_pairs={{0,8},{8,16},{16,24},{24,32},{32,40},{40,48},{48,56},{56,0},{1,9},... | collective-permute-start | bytes 393224 | tf_op jit(solution)/shard_map/ppermute | solution.py:28
  75.3 9.6 %collective-permute-start.27 = (bf16[128,512]{1,0:T(8,128)(2,1)S(1)}, bf16[128,512]{1,0:T(8,128)(2,1)S(1)}, u32[]{:S(2)}, u32[]{:S(2)}) collective-permute-start(bf16[128,512]{1,0:T(8,128)(2,1)S(1)} %add_convert_fusion), channel_id=1, source_target_pairs={{0,6},{2,0},{4,2},{6,4},{1,7},{3,1},{5,3},{7,5},{8,14},{10,8},{12,... | collective-permute-start | bytes 393224 | tf_op jit(solution)/shard_map/ppermute | solution.py:28
  76.6 9.7 %collective-permute-start.26 = (bf16[128,512]{1,0:T(8,128)(2,1)S(1)}, bf16[128,512]{1,0:T(8,128)(2,1)S(1)}, u32[]{:S(2)}, u32[]{:S(2)}) collective-permute-start(bf16[128,512]{1,0:T(8,128)(2,1)S(1)} %add_convert_fusion), channel_id=1, source_target_pairs={{0,4},{2,6},{4,0},{6,2},{1,5},{3,7},{5,1},{7,3},{8,12},{10,14},{12... | collective-permute-start | bytes 393224 | tf_op jit(solution)/shard_map/ppermute | solution.py:28
  78.6 10.8 %collective-permute-start.25 = (bf16[128,512]{1,0:T(8,128)(2,1)S(1)}, bf16[128,512]{1,0:T(8,128)(2,1)S(1)}, u32[]{:S(2)}, u32[]{:S(2)}) collective-permute-start(bf16[128,512]{1,0:T(8,128)(2,1)S(1)} %add_convert_fusion), channel_id=1, source_target_pairs={{0,2},{2,4},{4,6},{6,0},{1,3},{3,5},{5,7},{7,1},{8,10},{10,12},{12... | collective-permute-start | bytes 393224 | tf_op jit(solution)/shard_map/ppermute | solution.py:28
  89.5 1.6 %collective-permute-start.28 = (f32[128,512]{1,0:T(8,128)S(1)}, f32[128,512]{1,0:T(8,128)S(1)}, u32[]{:S(2)}, u32[]{:S(2)}) collective-permute-start(f32[128,512]{1,0:T(8,128)S(1)} %convert_add_fusion.own_ref), channel_id=1, source_target_pairs={{0,1},{1,0},{2,3},{3,2},{4,5},{5,4},{6,7},{7,6},{8,9},{9,8},{10,11... | collective-permute-start | bytes 786440 | tf_op jit(solution)/shard_map/ppermute | solution.py:28
  92.7 27.3 %all-to-all-start = ((f32[32,32,256]{2,1,0:T(8,128)}), f32[32,32,256]{2,1,0:T(8,128)S(1)}, u32[]{:S(2)}, u32[]{:S(2)}) async-start(f32[32,32,256]{2,1,0:T(8,128)} %get-tuple-element.29), calls=%async_computation | async-start | bytes 2097152 | tf_op jit(solution)/shard_map/all_to_all | solution.py:183

commit v2 on v1

v2 whole, which is shorter than its diff:
```python
import functools

import jax
import jax.numpy as jnp
from jax import lax
from jax.experimental import pallas as pl
from jax.experimental.pallas import tpu as pltpu
from jax.sharding import Mesh, PartitionSpec as P

FEAT = 256
TILE = 128
NODE_DEV = 512
PER_PIECE = NODE_DEV // TILE
HALF = FEAT // 2
GROUP = 32
MIB = 1 << 20
EARLY = 1
PACK = 0
FIN = 0
FLA = 20000000000
FLB = 20000000000

VMEM = pl.BlockSpec(memory_space=pltpu.VMEM)
SMEM = pl.BlockSpec(memory_space=pltpu.SMEM)
ANY = pl.BlockSpec(memory_space=pl.ANY)
HBM = pl.BlockSpec(memory_space=pltpu.HBM)
PIECE = (HALF, NODE_DEV)


def shifted(value, axes, step):
    total = lax.axis_size(axes)
    return lax.ppermute(value, axes, [(i, (i + step) % total) for i in range(total)])


def order_kernel(own, r1, r2, r3, field, arrive):
    place = lax.axis_index("h")
    copies = []
    for back, ref in enumerate((own, r1, r2, r3)):
        slot = lax.rem(place + 4 - back, 4)
        rows = pl.ds(pl.multiple_of(slot * 32, 32), 32)
        copies.append(pltpu.make_async_copy(ref, field.at[rows, :], arrive.at[back]))
    for copy in copies:
        copy.start()
    for copy in copies:
        copy.wait()


def pack_kernel(own, other, both):
    place = lax.axis_index("l")
    both[place] = own[...]
    both[1 - place] = other[...]


def agg_kernel(to_rows, own_meta, sib_meta, own_tiles, sib_tiles, *refs):
    place, place_y = lax.axis_index("x"), lax.axis_index("y")
    if to_rows:
        sources = [refs[-piece % 4] for piece in range(4)]
        result, field, acc, held, staged, tile_sem, field_sem, out_sem = refs[4:]
        outs = 8
    else:
        sources = [refs[-(piece // 2) % 4].at[piece % 2] for piece in range(8)]
        results = refs[4:8]
        field, acc, held, tile_sem, field_sem = refs[8:]
        outs = 4

    sides = ((0, own_meta, own_tiles), (1, sib_meta, sib_tiles))

    def tile_copy(side, turn, tiles):
        return pltpu.make_async_copy(
            tiles.at[pl.ds(turn * GROUP, GROUP)], held.at[side, turn], tile_sem.at[side, turn]
        )

    fills = []
    for piece, source in enumerate(sources):
        for part in range(PER_PIECE):
            lanes = pl.ds(part * TILE, TILE)
            fills.append(
                pltpu.make_async_copy(
                    source.at[:, lanes],
                    field.at[piece * PER_PIECE + part],
                    field_sem.at[piece * PER_PIECE + part],
                )
            )
    for side, meta, tiles in sides:
        tile_copy(side, 0, tiles).start()
    for copy in fills:
        copy.start()
    for side, meta, tiles in sides:

        @pl.when(meta[2, 0] > GROUP)
        def _(side=side, tiles=tiles):
            tile_copy(side, 1, tiles).start()

    acc[...] = jnp.zeros_like(acc)
    for copy in fills:
        copy.wait()
    contract = (((1,), (1,)), ((), ())) if to_rows else (((1,), (0,)), ((), ()))
    for side, meta, tiles in sides:
        used = meta[2, 0]

        def row_of(slot, meta=meta):
            return meta[0, slot]

        def near_row_of(slot, meta=meta):
            return (meta[0, slot] - 2 * PER_PIECE * place_y) & (8 * PER_PIECE - 1)

        def col_of(slot, meta=meta):
            block = meta[1, slot]
            return ((block // PER_PIECE - place) & 3) * PER_PIECE + (block & (PER_PIECE - 1))

        ends = (col_of, row_of) if to_rows else (near_row_of, col_of)

        def visiting(turn, carry, side=side, used=used, tiles=tiles, ends=ends):
            source, target = ends
            tile_copy(side, turn, tiles).wait()
            terms = []
            for member in range(GROUP):
                terms.append(
                    lax.dot_general(
                        field[source(turn * GROUP + member)],
                        held[side, turn, member],
                        contract,
                        preferred_element_type=jnp.float32,
                    )
                )
            for member in range(GROUP):
                slot = turn * GROUP + member
                acc[jnp.where(slot < used, target(slot), outs * PER_PIECE)] += terms[member]
            return carry

        lax.fori_loop(0, (used + GROUP - 1) // GROUP, visiting, 0)
    leaving = []
    for piece in range(outs):
        done = staged.at[piece] if to_rows else results[piece]
        for part in range(PER_PIECE):
            done[:, part * TILE : (part + 1) * TILE] = acc[piece * PER_PIECE + part].astype(
                jnp.bfloat16
            )
        if to_rows:
            leaving.append(pltpu.make_async_copy(done, result.at[piece], out_sem.at[piece]))
            leaving[-1].start()
    for copy in leaving:
        copy.wait()


def agg(to_rows, meta, tiles, sources, flops):
    pieces, outs = (4, 8) if to_rows else (8, 4)
    scratch = [
        pltpu.VMEM((pieces * PER_PIECE, HALF, TILE), jnp.bfloat16),
        pltpu.VMEM((outs * PER_PIECE + 1, HALF, TILE), jnp.float32),
        pltpu.VMEM((2, 64 // GROUP, GROUP, TILE, TILE), jnp.bfloat16),
    ]
    sems = [
        pltpu.SemaphoreType.DMA((2, 64 // GROUP)),
        pltpu.SemaphoreType.DMA((pieces * PER_PIECE,)),
    ]
    if to_rows:
        scratch += [pltpu.VMEM((outs,) + PIECE, jnp.bfloat16)]
        sems += [pltpu.SemaphoreType.DMA((outs,))]
        out_shape, out_specs = jax.ShapeDtypeStruct((outs,) + PIECE, jnp.bfloat16), HBM
    else:
        out_shape, out_specs = [jax.ShapeDtypeStruct(PIECE, jnp.bfloat16)] * outs, [VMEM] * outs
    return pl.pallas_call(
        functools.partial(agg_kernel, to_rows),
        out_shape=out_shape,
        in_specs=[SMEM] * 2 + [HBM] * 2 + [ANY] * len(sources),
        out_specs=out_specs,
        scratch_shapes=scratch + sems,
        compiler_params=pltpu.CompilerParams(vmem_limit_bytes=28 * MIB),
        cost_estimate=pl.CostEstimate(flops=flops, bytes_accessed=6 * MIB, transcendentals=0),
        name="to_rows" if to_rows else "to_cols",
    )(*meta, *tiles, *sources)


def split(value):
    high = value.astype(jnp.bfloat16)
    low = (value - high.astype(jnp.float32)).astype(jnp.bfloat16)
    return high, low


def dense_kernel(own_ref, sib_ref, weight_own, weight_sib, cotangent, activation, grads):
    own = split(own_ref[...])
    sib = split(sib_ref[...])
    preact = 0.0
    for weight, field in ((weight_own[...], own), (weight_sib[...], sib)):
        for part in field[::-1]:
            preact += jnp.dot(weight, part, preferred_element_type=jnp.float32)
    sigmoid = jax.nn.sigmoid(preact)
    activation[...] = (preact * sigmoid).astype(jnp.bfloat16)
    slope = (
        cotangent[...].astype(jnp.float32) * sigmoid * (1.0 + preact * (1.0 - sigmoid))
    ).astype(jnp.bfloat16)
    for side, field in enumerate((own, sib)):
        total = 0.0
        for part in field[::-1]:
            total += lax.dot_general(
                slope, part, (((1,), (1,)), ((), ())), preferred_element_type=jnp.float32
            )
        grads[:, side * HALF : (side + 1) * HALF] = total


def finish_kernel(terms, grad):
    place = lax.axis_index("c")
    total = terms[0].astype(jnp.float32)
    for turn in range(1, terms.shape[0]):
        total += terms[turn].astype(jnp.float32)
    total = total.T
    for side in range(2):
        core = place if side == 0 else 1 - place
        for step in range(4):
            rows = pl.ds(pl.multiple_of(step * 64 + core * 32, 32), 32)
            grad[rows, :] = total[side * HALF + step * 32 : side * HALF + (step + 1) * 32, :]


def body(features, weight, tiles, pairs, counts, cotangent):
    at_h, at_c = lax.axis_index("h"), lax.axis_index("c")
    slot_total = tiles.shape[3]
    own_tiles = tiles.reshape(slot_total, TILE, TILE)
    own_meta = jnp.concatenate(
        [pairs.reshape(2, slot_total), jnp.broadcast_to(counts.reshape(1, 1), (1, slot_total))]
    )
    sib_meta = shifted(own_meta, "c", 1)
    both_tiles = (own_tiles, shifted(own_tiles, "c", 1))

    from_h = [shifted(features, "h", k) for k in (1, 2, 3)]
    if EARLY:
        from_h, sib_meta = lax.optimization_barrier((from_h, sib_meta))
    meta = (own_meta, sib_meta)
    field = pl.pallas_call(
        order_kernel,
        out_shape=jax.ShapeDtypeStruct(PIECE, jnp.bfloat16),
        in_specs=[ANY] * 4,
        out_specs=VMEM,
        scratch_shapes=[pltpu.SemaphoreType.DMA((4,))],
        compiler_params=pltpu.CompilerParams(vmem_limit_bytes=2 * MIB),
        name="order",
    )(features, *from_h)
    other = shifted(field, "l", 1)
    col_seg = [field] + [shifted(field, "x", k) for k in range(1, 4)]
    if PACK == 0:
        near = pl.pallas_call(
            pack_kernel,
            out_shape=jax.ShapeDtypeStruct((2,) + PIECE, jnp.bfloat16),
            in_specs=[VMEM] * 2,
            out_specs=VMEM,
            compiler_params=pltpu.CompilerParams(vmem_limit_bytes=2 * MIB),
            name="pack",
        )(field, other)
    else:
        first = lax.axis_index("l") == 0
        near = jnp.stack([jnp.where(first, field, other), jnp.where(first, other, field)])
    row_seg = [near] + [shifted(near, "y", k) for k in range(1, 4)]
    row_part = agg(True, meta, both_tiles, col_seg, FLA)
    row_got = list(lax.all_to_all(row_part, ("y", "l"), 0, 0, tiled=True))
    col_part = agg(False, meta, both_tiles, row_seg, FLB)
    col_got = [col_part[0]] + [shifted(col_part[k], "x", k) for k in range(1, 4)]
    share = sum(v.astype(jnp.float32) for v in (*row_got, *col_got)).astype(jnp.bfloat16)
    shares = [share] + [shifted(share, "h", k) for k in (1, 2, 3)]
    total = sum(v.astype(jnp.float32) for v in shares)
    sib_total = shifted(total, "c", 1)

    weight_mine = lax.dynamic_slice_in_dim(weight, (at_h * 2 + at_c) * 32, 32, 1)
    weight_mine = weight_mine.reshape(4, 2, 32, 32)
    weight_own = lax.dynamic_index_in_dim(weight_mine, at_c, 1, False).reshape(HALF, 32).T
    weight_sib = lax.dynamic_index_in_dim(weight_mine, 1 - at_c, 1, False).reshape(HALF, 32).T
    activation, grads = pl.pallas_call(
        dense_kernel,
        out_shape=[
            jax.ShapeDtypeStruct((32, NODE_DEV), jnp.bfloat16),
            jax.ShapeDtypeStruct((32, FEAT), jnp.float32),
        ],
        in_specs=[VMEM] * 5,
        out_specs=[VMEM] * 2,
        compiler_params=pltpu.CompilerParams(vmem_limit_bytes=16 * MIB),
        name="dense",
    )(total, sib_total, weight_own, weight_sib, cotangent)
    pair = (grads + shifted(grads, "l", 1)).astype(jnp.bfloat16)
    many = jnp.broadcast_to(pair[None], (16, 32, FEAT))
    terms = lax.all_to_all(many, ("x", "y"), 0, 0, tiled=True)
    grad = pl.pallas_call(
        finish_kernel,
        out_shape=jax.ShapeDtypeStruct((FEAT, 32), jnp.float32),
        in_specs=[VMEM],
        out_specs=VMEM,
        compiler_params=pltpu.CompilerParams(vmem_limit_bytes=2 * MIB),
        name="finish",
    )(terms)
    return activation, grad


def solution(mesh):
    fine = Mesh(mesh.devices.reshape(4, 4, 2, 4, 2), ("x", "y", "l", "h", "c"))
    depth, col = ("h", "c"), ("y", "l")
    placed = (
        P(depth, ("x", "y", "l")),
        P(),
        P("x", col, depth, None, None, None),
        P("x", col, depth, None, None),
        P("x", col, depth),
        P(depth, ("x", "y", "l")),
    )
    return jax.shard_map(
        body,
        mesh=fine,
        in_specs=placed,
        out_specs=(P(depth, ("x", "y", "l")), P(None, depth)),
        check_vma=False,
    )
```

time: 122 us -> 92.8 us (0.76)
  waiting for transfers between devices: 45.6 us -> 19.2 us
  blocking collectives: 0 us -> 12.2 us
  starting transfers between devices: 53.8 us -> 42.8 us
  Pallas kernels: 14.5 us -> 7.73 us
  local copies, waits for them, and re-layouts: 4.5 us -> 6.94 us
    all_to_all x1, waiting for transfers between devices: 16.9 us -> 0.01 us  [body(): row_got = list(lax.all_to_all(row_part, ('y', 'l'), 0, 0, tiled=True))]
    all_to_all x0 -> x1, blocking collectives: none -> 12.2 us  [body(): terms = lax.all_to_all(many, ('x', 'y'), 0, 0, tiled=True)]
    ppermute x29 -> x20, waiting for transfers between devices: 28.7 us -> 19.2 us  [shifted(): lax.ppermute(value, axes, [(i, (i + step) % total) for i in range(total)])]
    pallas_call x3 -> x5, Pallas kernels: 12.9 us -> 6.87 us  [the longest x2 6.53 us: agg(): pl.pallas_call(functools.partial(agg_kernel, to_rows), out_shape=out_shap...]
    ppermute x29 -> x20, starting transfers between devices: 43.4 us -> 37.6 us  [shifted(): lax.ppermute(value, axes, [(i, (i + step) % total) for i in range(total)])]
    all_to_all x1, starting transfers between devices: 10.4 us -> 5.2 us  [body(): row_got = list(lax.all_to_all(row_part, ('y', 'l'), 0, 0, tiled=True))]
    unnamed x16 -> x15, local copies, waits for them, and re-layouts: 3.12 us -> 5.98 us
    convert_element_type x1 -> x2, other arithmetic: 0.21 us -> 1.5 us  [the longest x1 1.49 us: body(): sum((v.astype(jnp.float32) for v in (*row_got, *col_got)))]
  transfers between devices with their start and end apart: 30 -> 21, of which waited for: 13 -> 10; matrix products, arithmetic and copies ran while one was open for 1% -> 1% of each run, Pallas kernels for 11% -> 7%
where the time goes in v2:
time: 92.8 us; the launch traced here: 92 us
  starting transfers between devices  42.8 us (46%)
  waiting for transfers between devices  19.2 us (21%)
  blocking collectives  12.2 us (13%)
  Pallas kernels  7.73 us (8%)
  local copies, waits for them, and re-layouts  6.94 us (7%)
  other arithmetic  1.56 us (2%)
  between operations  1.46 us (2%)
    ppermute x20, starting transfers between devices, shifted(): lax.ppermute(value, axes, [(i, (i + step) % total) for i in range(total)])  37.6 us
    ppermute x20, waiting for transfers between devices, shifted(): lax.ppermute(value, axes, [(i, (i + step) % total) for i in range(total)])  19.2 us
    all_to_all x1, blocking collectives, body(): terms = lax.all_to_all(many, ('x', 'y'), 0, 0, tiled=True)  12.2 us
    pallas_call x2, Pallas kernels, agg(): pl.pallas_call(functools.partial(agg_kernel, to_rows), out_shape=out_shap...  6.53 us
    unnamed x15, local copies, waits for them, and re-layouts  5.98 us
    all_to_all x1, starting transfers between devices, body(): row_got = list(lax.all_to_all(row_part, ('y', 'l'), 0, 0, tiled=True))  5.2 us
  transfers between devices with their start and end apart: 21, of which 10 were waited for; matrix products, arithmetic and copies ran while one was open for 1% of the time, Pallas kernels for 7%

profile of v2, /device:TPU:8, one launch (start us, length us, event | category | flops | bytes accessed | tf_op | source)
XLA Modules:
  0.0 92.0 jit_solution(211665294376161785)
XLA Ops:
  0.6 0.0 copy-start
  0.6 0.1 collective-permute-start.4
  0.7 3.3 %collective-permute-start = (bf16[32,512]{1,0:T(8,128)(2,1)}, bf16[32,512]{1,0:T(8,128)(2,1)S(1)}, u32[]{:S(2)}, u32[]{:S(2)}) collective-permute-start(bf16[32,512]{1,0:T(8,128)(2,1)} %own.1), channel_id=1, source_target_pairs={{0,2},{2,4},{4,6},{6,0},{1,3},{3,5},{5,7},{7,1},{8,10},{10,12},{12... | collective-permute-start | bytes 98312 | tf_op jit(solution)/shard_map/ppermute | solution.py:32
  4.1 5.4 %collective-permute-start.1 = (bf16[32,512]{1,0:T(8,128)(2,1)}, bf16[32,512]{1,0:T(8,128)(2,1)S(1)}, u32[]{:S(2)}, u32[]{:S(2)}) collective-permute-start(bf16[32,512]{1,0:T(8,128)(2,1)} %own.1), channel_id=1, source_target_pairs={{0,4},{2,6},{4,0},{6,2},{1,5},{3,7},{5,1},{7,3},{8,12},{10,14},{12... | collective-permute-start | bytes 98312 | tf_op jit(solution)/shard_map/ppermute | solution.py:32
  9.5 2.7 %collective-permute-start.2 = (bf16[32,512]{1,0:T(8,128)(2,1)}, bf16[32,512]{1,0:T(8,128)(2,1)S(1)}, u32[]{:S(2)}, u32[]{:S(2)}) collective-permute-start(bf16[32,512]{1,0:T(8,128)(2,1)} %own.1), channel_id=1, source_target_pairs={{0,6},{2,0},{4,2},{6,4},{1,7},{3,1},{5,3},{7,5},{8,14},{10,8},{12,... | collective-permute-start | bytes 98312 | tf_op jit(solution)/shard_map/ppermute | solution.py:32
  12.8 0.7 concatenate.3.own_meta
  13.5 1.2 %collective-permute-done.3.sib_meta = s32[3,64]{1,0:T(4,128)S(1)} collective-permute-done((s32[3,64]{1,0:T(4,128)S(1)}, s32[3,64]{1,0:T(4,128)S(1)}, u32[]{:S(2)}, u32[]{:S(2)}) %collective-permute-start.3) | collective-permute-done | bytes 800 | tf_op jit(solution)/shard_map/ppermute | solution.py:32
  14.7 0.7 copy-done.2
  15.4 0.2 order.1.refs_0_.own
  15.6 1.1 %collective-permute-start.8 = (bf16[128,512]{1,0:T(8,128)(2,1)S(1)}, bf16[128,512]{1,0:T(8,128)(2,1)S(1)}, u32[]{:S(2)}, u32[]{:S(2)}) collective-permute-start(bf16[128,512]{1,0:T(8,128)(2,1)S(1)} %order.1.refs_0_.own), channel_id=1, source_target_pairs={{0,8},{8,0},{1,9},{9,1},{2,10},{10,2},{3,11},{11,3},{4,12},{12,4},... | collective-permute-start | bytes 393224 | tf_op jit(solution)/shard_map/ppermute | solution.py:32
  16.7 1.5 %collective-permute-start.5 = (bf16[128,512]{1,0:T(8,128)(2,1)S(1)}, bf16[128,512]{1,0:T(8,128)(2,1)S(1)}, u32[]{:S(2)}, u32[]{:S(2)}) collective-permute-start(bf16[128,512]{1,0:T(8,128)(2,1)S(1)} %order.1.refs_0_.own), channel_id=1, source_target_pairs={{0,64},{64,128},{128,192},{192,0},{1,65},{65,129},{129,193},{193,1... | collective-permute-start | bytes 393224 | tf_op jit(solution)/shard_map/ppermute | solution.py:32
  18.2 2.7 %collective-permute-start.6 = (bf16[128,512]{1,0:T(8,128)(2,1)S(1)}, bf16[128,512]{1,0:T(8,128)(2,1)S(1)}, u32[]{:S(2)}, u32[]{:S(2)}) collective-permute-start(bf16[128,512]{1,0:T(8,128)(2,1)S(1)} %order.1.refs_0_.own), channel_id=1, source_target_pairs={{0,128},{64,192},{128,0},{192,64},{1,129},{65,193},{129,1},{193,65... | collective-permute-start | bytes 393224 | tf_op jit(solution)/shard_map/ppermute | solution.py:32
  20.9 1.4 %collective-permute-start.7 = (bf16[128,512]{1,0:T(8,128)(2,1)S(1)}, bf16[128,512]{1,0:T(8,128)(2,1)S(1)}, u32[]{:S(2)}, u32[]{:S(2)}) collective-permute-start(bf16[128,512]{1,0:T(8,128)(2,1)S(1)} %order.1.refs_0_.own), channel_id=1, source_target_pairs={{0,192},{64,0},{128,64},{192,128},{1,193},{65,1},{129,65},{193,129... | collective-permute-start | bytes 393224 | tf_op jit(solution)/shard_map/ppermute | solution.py:32
  22.4 2.4 %collective-permute-start.10 = (bf16[2,128,512]{2,1,0:T(8,128)(2,1)S(1)}, bf16[2,128,512]{2,1,0:T(8,128)(2,1)S(1)}, u32[]{:S(2)}, u32[]{:S(2)}) collective-permute-start(bf16[2,128,512]{2,1,0:T(8,128)(2,1)S(1)} %pack.1.refs_0_), channel_id=1, source_target_pairs={{0,32},{16,48},{32,0},{48,16},{1,33},{17,49},{33,1},{49,17},{2,34}... | collective-permute-start | bytes 786440 | tf_op jit(solution)/shard_map/ppermute | solution.py:32
  24.8 1.3 %collective-permute-start.11 = (bf16[2,128,512]{2,1,0:T(8,128)(2,1)S(1)}, bf16[2,128,512]{2,1,0:T(8,128)(2,1)S(1)}, u32[]{:S(2)}, u32[]{:S(2)}) collective-permute-start(bf16[2,128,512]{2,1,0:T(8,128)(2,1)S(1)} %pack.1.refs_0_), channel_id=1, source_target_pairs={{0,48},{16,0},{32,16},{48,32},{1,49},{17,1},{33,17},{49,33},{2,50}... | collective-permute-start | bytes 786440 | tf_op jit(solution)/shard_map/ppermute | solution.py:32
  26.1 0.9 collective-permute-done.6.refs_2_
  27.0 1.6 %collective-permute-start.9 = (bf16[2,128,512]{2,1,0:T(8,128)(2,1)S(1)}, bf16[2,128,512]{2,1,0:T(8,128)(2,1)S(1)}, u32[]{:S(2)}, u32[]{:S(2)}) collective-permute-start(bf16[2,128,512]{2,1,0:T(8,128)(2,1)S(1)} %pack.1.refs_0_), channel_id=1, source_target_pairs={{0,16},{16,32},{32,48},{48,0},{1,17},{17,33},{33,49},{49,1},{2,18}... | collective-permute-start | bytes 786440 | tf_op jit(solution)/shard_map/ppermute | solution.py:32
  28.6 1.6 %copy-done.3 = bf16[1,1,1,64,128,128]{5,4,3,2,1,0:T(8,128)(2,1)S(1)} copy-done((bf16[1,1,1,64,128,128]{5,4,3,2,1,0:T(8,128)(2,1)S(1)}, bf16[1,1,1,64,128,128]{5,4,3,2,1,0:T(8,128)(2,1)}, u32[]{:S(2)}) %copy-start.3) | copy-done | bytes 2097176
  30.2 4.0 %to_rows.1 = bf16[8,128,512]{2,1,0:T(8,128)(2,1)} custom-call(s32[3,64]{1,0:T(4,128)S(1)} %concatenate.3.own_meta, s32[3,64]{1,0:T(4,128)S(1)} %collective-permute-done.3.sib_meta, bf16[64,128,128]{2,1,0:T(8,128)(2,1)S(1)} %bitcast.26, bf16[64,128,128]{2,1,0:T(8,128)(2,1)S(1)} %collective-permute-done.4.sib_tiles, bf16[128,512]{1,0:T(8,128)(2,1)S(1)} %order.1.refs_0_.own, ...), custom_call_target="tpu_custom_call" | custom-call | flops 20000000000 | bytes 6291456 | tf_op jit(solution)/shard_map/to_rows/pallas_call | solution.py:163
  34.2 1.3 %copy-done.5 = bf16[64,128,128]{2,1,0:T(8,128)(2,1)} copy-done((bf16[64,128,128]{2,1,0:T(8,128)(2,1)}, bf16[64,128,128]{2,1,0:T(8,128)(2,1)S(1)}, u32[]{:S(2)}) %copy-start.5) | copy-done | bytes 2097176
  35.6 5.2 %all-to-all-start = ((bf16[8,128,512]{2,1,0:T(8,128)(2,1)}), bf16[8,128,512]{2,1,0:T(8,128)(2,1)}, u32[]{:S(2)}, u32[]{:S(2)}) async-start(bf16[8,128,512]{2,1,0:T(8,128)(2,1)} %to_rows.1), calls=%async_computation | async-start | bytes 2097152 | tf_op jit(solution)/shard_map/all_to_all | solution.py:254
  40.8 1.6 %copy-done.6 = bf16[64,128,128]{2,1,0:T(8,128)(2,1)S(1)} copy-done((bf16[64,128,128]{2,1,0:T(8,128)(2,1)S(1)}, bf16[64,128,128]{2,1,0:T(8,128)(2,1)}, u32[]{:S(2)}) %copy-start.6) | copy-done | bytes 2097176
  42.4 2.5 %to_cols.1 = (bf16[128,512]{1,0:T(8,128)(2,1)S(1)}, bf16[128,512]{1,0:T(8,128)(2,1)S(1)}, bf16[128,512]{1,0:T(8,128)(2,1)S(1)}, bf16[128,512]{1,0:T(8,128)(2,1)S(1)}) custom-call(s32[3,64]{1,0:T(4,128)S(1)} %concatenate.3.own_meta, s32[3,64]{1,0:T(4,128)S(1)} %collective-permute-done.3.sib_meta, bf16[64,128,128]{2,1,0:T(8,128)(2,1)S(1)} %bitcast.27, ...), custom_call_target="tpu_custom_call" | custom-call | flops 20000000000 | bytes 6291456 | tf_op jit(solution)/shard_map/to_cols/pallas_call | solution.py:163
  44.9 1.3 %collective-permute-start.12 = (bf16[128,512]{1,0:T(8,128)(2,1)S(1)}, bf16[128,512]{1,0:T(8,128)(2,1)S(1)}, u32[]{:S(2)}, u32[]{:S(2)}) collective-permute-start(bf16[128,512]{1,0:T(8,128)(2,1)S(1)} %get-tuple-element.17), channel_id=1, source_target_pairs={{0,64},{64,128},{128,192},{192,0},{1,65},{65,129},{129,193},{193,1... | collective-permute-start | bytes 393224 | tf_op jit(solution)/shard_map/ppermute | solution.py:32
  46.2 2.3 %collective-permute-start.13 = (bf16[128,512]{1,0:T(8,128)(2,1)S(1)}, bf16[128,512]{1,0:T(8,128)(2,1)S(1)}, u32[]{:S(2)}, u32[]{:S(2)}) collective-permute-start(bf16[128,512]{1,0:T(8,128)(2,1)S(1)} %get-tuple-element.18), channel_id=1, source_target_pairs={{0,128},{64,192},{128,0},{192,64},{1,129},{65,193},{129,1},{193,65... | collective-permute-start | bytes 393224 | tf_op jit(solution)/shard_map/ppermute | solution.py:32
  48.5 1.6 %collective-permute-start.14 = (bf16[128,512]{1,0:T(8,128)(2,1)S(1)}, bf16[128,512]{1,0:T(8,128)(2,1)S(1)}, u32[]{:S(2)}, u32[]{:S(2)}) collective-permute-start(bf16[128,512]{1,0:T(8,128)(2,1)S(1)} %get-tuple-element.19), channel_id=1, source_target_pairs={{0,192},{64,0},{128,64},{192,128},{1,193},{65,1},{129,65},{193,129... | collective-permute-start | bytes 393224 | tf_op jit(solution)/shard_map/ppermute | solution.py:32
  50.1 1.9 %collective-permute-done.12 = bf16[128,512]{1,0:T(8,128)(2,1)S(1)} collective-permute-done((bf16[128,512]{1,0:T(8,128)(2,1)S(1)}, bf16[128,512]{1,0:T(8,128)(2,1)S(1)}, u32[]{:S(2)}, u32[]{:S(2)}) %collective-permute-start.12) | collective-permute-done | bytes 131104 | tf_op jit(solution)/shard_map/ppermute | solution.py:32
  52.0 1.4 %collective-permute-done.13 = bf16[128,512]{1,0:T(8,128)(2,1)S(1)} collective-permute-done((bf16[128,512]{1,0:T(8,128)(2,1)S(1)}, bf16[128,512]{1,0:T(8,128)(2,1)S(1)}, u32[]{:S(2)}, u32[]{:S(2)}) %collective-permute-start.13) | collective-permute-done | bytes 131104 | tf_op jit(solution)/shard_map/ppermute | solution.py:32
  53.4 0.3 collective-permute-done.14
  53.6 1.5 %fusion.3 = bf16[128,512]{1,0:T(8,128)(2,1)S(1)} fusion(bf16[128,512]{1,0:T(8,128)(2,1)S(1)} %collective-permute-done.14, bf16[128,512]{1,0:T(8,128)(2,1)S(1)} %collective-permute-done.13, bf16[128,512]{1,0:T(8,128)(2,1)S(1)} %collective-permute-done.12, bf16[128,512]{1,0:T(8,128)(2,1)S(1)} %get-tuple-element.16, bf16[8,128,512]{2,1,0:T(8,128)(2,1)} %all-to-all-done), kind=kLoop, calls=%fused_computation.4 | loop fusion | flops 1572864 | bytes 1703936 | tf_op jit(solution)/shard_map/convert_element_type | solution.py:257
  55.1 1.9 %collective-permute-start.15 = (bf16[128,512]{1,0:T(8,128)(2,1)S(1)}, bf16[128,512]{1,0:T(8,128)(2,1)S(1)}, u32[]{:S(2)}, u32[]{:S(2)}) collective-permute-start(bf16[128,512]{1,0:T(8,128)(2,1)S(1)} %fusion.3), channel_id=1, source_target_pairs={{0,2},{2,4},{4,6},{6,0},{1,3},{3,5},{5,7},{7,1},{8,10},{10,12},{12... | collective-permute-start | bytes 393224 | tf_op jit(solution)/shard_map/ppermute | solution.py:32
  57.1 3.9 %collective-permute-start.16 = (bf16[128,512]{1,0:T(8,128)(2,1)S(1)}, bf16[128,512]{1,0:T(8,128)(2,1)S(1)}, u32[]{:S(2)}, u32[]{:S(2)}) collective-permute-start(bf16[128,512]{1,0:T(8,128)(2,1)S(1)} %fusion.3), channel_id=1, source_target_pairs={{0,4},{2,6},{4,0},{6,2},{1,5},{3,7},{5,1},{7,3},{8,12},{10,14},{12... | collective-permute-start | bytes 393224 | tf_op jit(solution)/shard_map/ppermute | solution.py:32
  60.9 2.1 %collective-permute-start.17 = (bf16[128,512]{1,0:T(8,128)(2,1)S(1)}, bf16[128,512]{1,0:T(8,128)(2,1)S(1)}, u32[]{:S(2)}, u32[]{:S(2)}) collective-permute-start(bf16[128,512]{1,0:T(8,128)(2,1)S(1)} %fusion.3), channel_id=1, source_target_pairs={{0,6},{2,0},{4,2},{6,4},{1,7},{3,1},{5,3},{7,5},{8,14},{10,8},{12,... | collective-permute-start | bytes 393224 | tf_op jit(solution)/shard_map/ppermute | solution.py:32
  63.0 1.9 %collective-permute-done.15 = bf16[128,512]{1,0:T(8,128)(2,1)S(1)} collective-permute-done((bf16[128,512]{1,0:T(8,128)(2,1)S(1)}, bf16[128,512]{1,0:T(8,128)(2,1)S(1)}, u32[]{:S(2)}, u32[]{:S(2)}) %collective-permute-start.15) | collective-permute-done | bytes 131104 | tf_op jit(solution)/shard_map/ppermute | solution.py:32
  64.9 3.2 %collective-permute-done.16 = bf16[128,512]{1,0:T(8,128)(2,1)S(1)} collective-permute-done((bf16[128,512]{1,0:T(8,128)(2,1)S(1)}, bf16[128,512]{1,0:T(8,128)(2,1)S(1)}, u32[]{:S(2)}, u32[]{:S(2)}) %collective-permute-start.16) | collective-permute-done | bytes 131104 | tf_op jit(solution)/shard_map/ppermute | solution.py:32
  68.1 4.3 %collective-permute-done.17 = bf16[128,512]{1,0:T(8,128)(2,1)S(1)} collective-permute-done((bf16[128,512]{1,0:T(8,128)(2,1)S(1)}, bf16[128,512]{1,0:T(8,128)(2,1)S(1)}, u32[]{:S(2)}, u32[]{:S(2)}) %collective-permute-start.17) | collective-permute-done | bytes 131104 | tf_op jit(solution)/shard_map/ppermute | solution.py:32
  72.4 0.1 convert_add_fusion.own_ref
  72.5 0.1 collective-permute-start.18
  72.6 0.1 constant_dynamic-slice_fusion.2
  72.7 0.1 copy.18
  72.8 0.1 copy.19
  72.9 1.2 %collective-permute-done.18.sib_ref = f32[128,512]{1,0:T(8,128)S(1)} collective-permute-done((f32[128,512]{1,0:T(8,128)S(1)}, f32[128,512]{1,0:T(8,128)S(1)}, u32[]{:S(2)}, u32[]{:S(2)}) %collective-permute-start.18) | collective-permute-done | bytes 262176 | tf_op jit(solution)/shard_map/ppermute | solution.py:32
  74.1 0.9 dense.1
  75.0 0.9 %collective-permute-start.19 = (f32[32,256]{1,0:T(8,128)S(1)}, f32[32,256]{1,0:T(8,128)S(1)}, u32[]{:S(2)}, u32[]{:S(2)}) collective-permute-start(f32[32,256]{1,0:T(8,128)S(1)} %get-tuple-element.21), channel_id=1, source_target_pairs={{0,8},{8,0},{1,9},{9,1},{2,10},{10,2},{3,11},{11,3},{4,12},{12,4},... | collective-permute-start | bytes 98312 | tf_op jit(solution)/shard_map/ppermute | solution.py:32
  75.9 3.0 %collective-permute-done.19 = f32[32,256]{1,0:T(8,128)S(1)} collective-permute-done((f32[32,256]{1,0:T(8,128)S(1)}, f32[32,256]{1,0:T(8,128)S(1)}, u32[]{:S(2)}, u32[]{:S(2)}) %collective-permute-start.19) | collective-permute-done | bytes 32800 | tf_op jit(solution)/shard_map/ppermute | solution.py:32
  78.9 12.2 %all_to_all.10.terms = bf16[16,32,256]{2,1,0:T(8,128)(2,1)S(1)} all-to-all(bf16[16,32,256]{2,1,0:T(8,128)(2,1)S(1)} %broadcast_in_dim.5), channel_id=1, replica_groups=mesh['x'=4,'y'=4,'l'=2,'h'=4,'c'=2] {'x','y'}, dimensions={0} | all-to-all | bytes 524288 | tf_op jit(solution)/shard_map/all_to_all | solution.py:279
  91.1 0.1 finish.1
  91.3 0.7 copy.12
  (25 shorter events, 0.1 us)
Async XLA Ops:
  0.6 72.0 %copy-start = (bf16[256,256]{1,0:T(8,128)(2,1)S(1)}, bf16[256,256]{1,0:T(8,128)(2,1)}, u32[]{:S(2)}) copy-start(bf16[256,256]{1,0:T(8,128)(2,1)} %param.7) | copy-start | bytes 393220
  0.6 27.9 %collective-permute-start.4 = (bf16[64,128,128]{2,1,0:T(8,128)(2,1)}, bf16[64,128,128]{2,1,0:T(8,128)(2,1)S(1)}, u32[]{:S(2)}, u32[]{:S(2)}) collective-permute-start(bf16[64,128,128]{2,1,0:T(8,128)(2,1)} %bitcast.25), channel_id=1, source_target_pairs={{0,1},{1,0},{2,3},{3,2},{4,5},{5,4},{6,7},{7,6},{8,9},{9,8},{10,11... | collective-permute-start | bytes 6291464 | tf_op jit(solution)/shard_map/ppermute | solution.py:32
  0.7 13.9 %collective-permute-start = (bf16[32,512]{1,0:T(8,128)(2,1)}, bf16[32,512]{1,0:T(8,128)(2,1)S(1)}, u32[]{:S(2)}, u32[]{:S(2)}) collective-permute-start(bf16[32,512]{1,0:T(8,128)(2,1)} %own.1), channel_id=1, source_target_pairs={{0,2},{2,4},{4,6},{6,0},{1,3},{3,5},{5,7},{7,1},{8,10},{10,12},{12... | collective-permute-start | bytes 98312 | tf_op jit(solution)/shard_map/ppermute | solution.py:32
  4.1 10.6 %collective-permute-start.1 = (bf16[32,512]{1,0:T(8,128)(2,1)}, bf16[32,512]{1,0:T(8,128)(2,1)S(1)}, u32[]{:S(2)}, u32[]{:S(2)}) collective-permute-start(bf16[32,512]{1,0:T(8,128)(2,1)} %own.1), channel_id=1, source_target_pairs={{0,4},{2,6},{4,0},{6,2},{1,5},{3,7},{5,1},{7,3},{8,12},{10,14},{12... | collective-permute-start | bytes 98312 | tf_op jit(solution)/shard_map/ppermute | solution.py:32
  9.5 5.2 %collective-permute-start.2 = (bf16[32,512]{1,0:T(8,128)(2,1)}, bf16[32,512]{1,0:T(8,128)(2,1)S(1)}, u32[]{:S(2)}, u32[]{:S(2)}) collective-permute-start(bf16[32,512]{1,0:T(8,128)(2,1)} %own.1), channel_id=1, source_target_pairs={{0,6},{2,0},{4,2},{6,4},{1,7},{3,1},{5,3},{7,5},{8,14},{10,8},{12,... | collective-permute-start | bytes 98312 | tf_op jit(solution)/shard_map/ppermute | solution.py:32
  13.5 1.2 %collective-permute-start.3 = (s32[3,64]{1,0:T(4,128)S(1)}, s32[3,64]{1,0:T(4,128)S(1)}, u32[]{:S(2)}, u32[]{:S(2)}) collective-permute-start(s32[3,64]{1,0:T(4,128)S(1)} %concatenate.3.own_meta), channel_id=1, source_target_pairs={{0,1},{1,0},{2,3},{3,2},{4,5},{5,4},{6,7},{7,6},{8,9},{9,8},{10,11... | collective-permute-start | bytes 2312 | tf_op jit(solution)/shard_map/ppermute | solution.py:32
  14.7 0.8 copy-start.2
  15.6 6.8 %collective-permute-start.8 = (bf16[128,512]{1,0:T(8,128)(2,1)S(1)}, bf16[128,512]{1,0:T(8,128)(2,1)S(1)}, u32[]{:S(2)}, u32[]{:S(2)}) collective-permute-start(bf16[128,512]{1,0:T(8,128)(2,1)S(1)} %order.1.refs_0_.own), channel_id=1, source_target_pairs={{0,8},{8,0},{1,9},{9,1},{2,10},{10,2},{3,11},{11,3},{4,12},{12,4},... | collective-permute-start | bytes 393224 | tf_op jit(solution)/shard_map/ppermute | solution.py:32
  16.7 8.1 %collective-permute-start.5 = (bf16[128,512]{1,0:T(8,128)(2,1)S(1)}, bf16[128,512]{1,0:T(8,128)(2,1)S(1)}, u32[]{:S(2)}, u32[]{:S(2)}) collective-permute-start(bf16[128,512]{1,0:T(8,128)(2,1)S(1)} %order.1.refs_0_.own), channel_id=1, source_target_pairs={{0,64},{64,128},{128,192},{192,0},{1,65},{65,129},{129,193},{193,1... | collective-permute-start | bytes 393224 | tf_op jit(solution)/shard_map/ppermute | solution.py:32
  18.2 8.8 %collective-permute-start.6 = (bf16[128,512]{1,0:T(8,128)(2,1)S(1)}, bf16[128,512]{1,0:T(8,128)(2,1)S(1)}, u32[]{:S(2)}, u32[]{:S(2)}) collective-permute-start(bf16[128,512]{1,0:T(8,128)(2,1)S(1)} %order.1.refs_0_.own), channel_id=1, source_target_pairs={{0,128},{64,192},{128,0},{192,64},{1,129},{65,193},{129,1},{193,65... | collective-permute-start | bytes 393224 | tf_op jit(solution)/shard_map/ppermute | solution.py:32
  20.9 7.7 %collective-permute-start.7 = (bf16[128,512]{1,0:T(8,128)(2,1)S(1)}, bf16[128,512]{1,0:T(8,128)(2,1)S(1)}, u32[]{:S(2)}, u32[]{:S(2)}) collective-permute-start(bf16[128,512]{1,0:T(8,128)(2,1)S(1)} %order.1.refs_0_.own), channel_id=1, source_target_pairs={{0,192},{64,0},{128,64},{192,128},{1,193},{65,1},{129,65},{193,129... | collective-permute-start | bytes 393224 | tf_op jit(solution)/shard_map/ppermute | solution.py:32
  22.4 18.4 %collective-permute-start.10 = (bf16[2,128,512]{2,1,0:T(8,128)(2,1)S(1)}, bf16[2,128,512]{2,1,0:T(8,128)(2,1)S(1)}, u32[]{:S(2)}, u32[]{:S(2)}) collective-permute-start(bf16[2,128,512]{2,1,0:T(8,128)(2,1)S(1)} %pack.1.refs_0_), channel_id=1, source_target_pairs={{0,32},{16,48},{32,0},{48,16},{1,33},{17,49},{33,1},{49,17},{2,34}... | collective-permute-start | bytes 786440 | tf_op jit(solution)/shard_map/ppermute | solution.py:32
  24.8 16.0 %collective-permute-start.11 = (bf16[2,128,512]{2,1,0:T(8,128)(2,1)S(1)}, bf16[2,128,512]{2,1,0:T(8,128)(2,1)S(1)}, u32[]{:S(2)}, u32[]{:S(2)}) collective-permute-start(bf16[2,128,512]{2,1,0:T(8,128)(2,1)S(1)} %pack.1.refs_0_), channel_id=1, source_target_pairs={{0,48},{16,0},{32,16},{48,32},{1,49},{17,1},{33,17},{49,33},{2,50}... | collective-permute-start | bytes 786440 | tf_op jit(solution)/shard_map/ppermute | solution.py:32
  27.0 13.8 %collective-permute-start.9 = (bf16[2,128,512]{2,1,0:T(8,128)(2,1)S(1)}, bf16[2,128,512]{2,1,0:T(8,128)(2,1)S(1)}, u32[]{:S(2)}, u32[]{:S(2)}) collective-permute-start(bf16[2,128,512]{2,1,0:T(8,128)(2,1)S(1)} %pack.1.refs_0_), channel_id=1, source_target_pairs={{0,16},{16,32},{32,48},{48,0},{1,17},{17,33},{33,49},{49,1},{2,18}... | collective-permute-start | bytes 786440 | tf_op jit(solution)/shard_map/ppermute | solution.py:32
  28.6 1.6 %copy-start.3 = (bf16[1,1,1,64,128,128]{5,4,3,2,1,0:T(8,128)(2,1)S(1)}, bf16[1,1,1,64,128,128]{5,4,3,2,1,0:T(8,128)(2,1)}, u32[]{:S(2)}) copy-start(bf16[1,1,1,64,128,128]{5,4,3,2,1,0:T(8,128)(2,1)} %param.8) | copy-start | bytes 6291460
  34.2 1.3 %copy-start.5 = (bf16[64,128,128]{2,1,0:T(8,128)(2,1)}, bf16[64,128,128]{2,1,0:T(8,128)(2,1)S(1)}, u32[]{:S(2)}) copy-start(bf16[64,128,128]{2,1,0:T(8,128)(2,1)S(1)} %collective-permute-done.4.sib_tiles) | copy-start | bytes 6291460
  35.6 5.2 %copy-start.4 = (bf16[1,1,1,64,128,128]{5,4,3,2,1,0:T(8,128)(2,1)S(1)}, bf16[1,1,1,64,128,128]{5,4,3,2,1,0:T(8,128)(2,1)}, u32[]{:S(2)}) copy-start(bf16[1,1,1,64,128,128]{5,4,3,2,1,0:T(8,128)(2,1)} %param.8) | copy-start | bytes 6291460
  35.6 18.1 %all-to-all-start = ((bf16[8,128,512]{2,1,0:T(8,128)(2,1)}), bf16[8,128,512]{2,1,0:T(8,128)(2,1)}, u32[]{:S(2)}, u32[]{:S(2)}) async-start(bf16[8,128,512]{2,1,0:T(8,128)(2,1)} %to_rows.1), calls=%async_computation | async-start | bytes 2097152 | tf_op jit(solution)/shard_map/all_to_all | solution.py:254
  40.8 1.6 %copy-start.6 = (bf16[64,128,128]{2,1,0:T(8,128)(2,1)S(1)}, bf16[64,128,128]{2,1,0:T(8,128)(2,1)}, u32[]{:S(2)}) copy-start(bf16[64,128,128]{2,1,0:T(8,128)(2,1)} %copy-done.5) | copy-start | bytes 6291460
  44.9 29.2 %copy-start.1 = (bf16[32,512]{1,0:T(8,128)(2,1)S(1)}, bf16[32,512]{1,0:T(8,128)(2,1)}, u32[]{:S(2)}) copy-start(bf16[32,512]{1,0:T(8,128)(2,1)} %cotangent.1) | copy-start | bytes 98308
  44.9 7.0 %collective-permute-start.12 = (bf16[128,512]{1,0:T(8,128)(2,1)S(1)}, bf16[128,512]{1,0:T(8,128)(2,1)S(1)}, u32[]{:S(2)}, u32[]{:S(2)}) collective-permute-start(bf16[128,512]{1,0:T(8,128)(2,1)S(1)} %get-tuple-element.17), channel_id=1, source_target_pairs={{0,64},{64,128},{128,192},{192,0},{1,65},{65,129},{129,193},{193,1... | collective-permute-start | bytes 393224 | tf_op jit(solution)/shard_map/ppermute | solution.py:32
  46.2 7.2 %collective-permute-start.13 = (bf16[128,512]{1,0:T(8,128)(2,1)S(1)}, bf16[128,512]{1,0:T(8,128)(2,1)S(1)}, u32[]{:S(2)}, u32[]{:S(2)}) collective-permute-start(bf16[128,512]{1,0:T(8,128)(2,1)S(1)} %get-tuple-element.18), channel_id=1, source_target_pairs={{0,128},{64,192},{128,0},{192,64},{1,129},{65,193},{129,1},{193,65... | collective-permute-start | bytes 393224 | tf_op jit(solution)/shard_map/ppermute | solution.py:32
  48.5 5.1 %collective-permute-start.14 = (bf16[128,512]{1,0:T(8,128)(2,1)S(1)}, bf16[128,512]{1,0:T(8,128)(2,1)S(1)}, u32[]{:S(2)}, u32[]{:S(2)}) collective-permute-start(bf16[128,512]{1,0:T(8,128)(2,1)S(1)} %get-tuple-element.19), channel_id=1, source_target_pairs={{0,192},{64,0},{128,64},{192,128},{1,193},{65,1},{129,65},{193,129... | collective-permute-start | bytes 393224 | tf_op jit(solution)/shard_map/ppermute | solution.py:32
  55.1 9.8 %collective-permute-start.15 = (bf16[128,512]{1,0:T(8,128)(2,1)S(1)}, bf16[128,512]{1,0:T(8,128)(2,1)S(1)}, u32[]{:S(2)}, u32[]{:S(2)}) collective-permute-start(bf16[128,512]{1,0:T(8,128)(2,1)S(1)} %fusion.3), channel_id=1, source_target_pairs={{0,2},{2,4},{4,6},{6,0},{1,3},{3,5},{5,7},{7,1},{8,10},{10,12},{12... | collective-permute-start | bytes 393224 | tf_op jit(solution)/shard_map/ppermute | solution.py:32
  57.1 11.0 %collective-permute-start.16 = (bf16[128,512]{1,0:T(8,128)(2,1)S(1)}, bf16[128,512]{1,0:T(8,128)(2,1)S(1)}, u32[]{:S(2)}, u32[]{:S(2)}) collective-permute-start(bf16[128,512]{1,0:T(8,128)(2,1)S(1)} %fusion.3), channel_id=1, source_target_pairs={{0,4},{2,6},{4,0},{6,2},{1,5},{3,7},{5,1},{7,3},{8,12},{10,14},{12... | collective-permute-start | bytes 393224 | tf_op jit(solution)/shard_map/ppermute | solution.py:32
  60.9 11.5 %collective-permute-start.17 = (bf16[128,512]{1,0:T(8,128)(2,1)S(1)}, bf16[128,512]{1,0:T(8,128)(2,1)S(1)}, u32[]{:S(2)}, u32[]{:S(2)}) collective-permute-start(bf16[128,512]{1,0:T(8,128)(2,1)S(1)} %fusion.3), channel_id=1, source_target_pairs={{0,6},{2,0},{4,2},{6,4},{1,7},{3,1},{5,3},{7,5},{8,14},{10,8},{12,... | collective-permute-start | bytes 393224 | tf_op jit(solution)/shard_map/ppermute | solution.py:32
  72.5 1.6 %collective-permute-start.18 = (f32[128,512]{1,0:T(8,128)S(1)}, f32[128,512]{1,0:T(8,128)S(1)}, u32[]{:S(2)}, u32[]{:S(2)}) collective-permute-start(f32[128,512]{1,0:T(8,128)S(1)} %convert_add_fusion.own_ref), channel_id=1, source_target_pairs={{0,1},{1,0},{2,3},{3,2},{4,5},{5,4},{6,7},{7,6},{8,9},{9,8},{10,11... | collective-permute-start | bytes 786440 | tf_op jit(solution)/shard_map/ppermute | solution.py:32
  75.0 3.9 %collective-permute-start.19 = (f32[32,256]{1,0:T(8,128)S(1)}, f32[32,256]{1,0:T(8,128)S(1)}, u32[]{:S(2)}, u32[]{:S(2)}) collective-permute-start(f32[32,256]{1,0:T(8,128)S(1)} %get-tuple-element.21), channel_id=1, source_target_pairs={{0,8},{8,0},{1,9},{9,1},{2,10},{10,2},{3,11},{11,3},{4,12},{12,4},... | collective-permute-start | bytes 98312 | tf_op jit(solution)/shard_map/ppermute | solution.py:32

commit v3 on v2

--- a/solution.py
+++ b/solution.py
@@ -12,13 +12,11 @@
 NODE_DEV = 512
 PER_PIECE = NODE_DEV // TILE
 HALF = FEAT // 2
+SLOTS = 64
 GROUP = 32
 MIB = 1 << 20
-EARLY = 1
-PACK = 0
-FIN = 0
-FLA = 20000000000
-FLB = 20000000000
+AGG_FLOPS = 20_000_000_000
+AGG_VMEM = 52
 
 VMEM = pl.BlockSpec(memory_space=pltpu.VMEM)
 SMEM = pl.BlockSpec(memory_space=pltpu.SMEM)
@@ -27,9 +25,21 @@
 PIECE = (HALF, NODE_DEV)
 
 
-def shifted(value, axes, step):
-    total = lax.axis_size(axes)
-    return lax.ppermute(value, axes, [(i, (i + step) % total) for i in range(total)])
+def limit(mib):
+    return pltpu.CompilerParams(vmem_limit_bytes=mib * MIB)
+
+
+def shifted(value, axis, step):
+    total = lax.axis_size(axis)
+    return lax.ppermute(value, axis, [(i, (i + step) % total) for i in range(total)])
+
+
+def ring(values, axis):
+    got = [None] * 4
+    for step in (2, 1, 3):
+        value = values[step] if isinstance(values, (list, tuple)) else values
+        got[step] = shifted(value, axis, step)
+    return got[1:]
 
 
 def order_kernel(own, r1, r2, r3, field, arrive):
@@ -54,13 +64,12 @@
 def agg_kernel(to_rows, own_meta, sib_meta, own_tiles, sib_tiles, *refs):
     place, place_y = lax.axis_index("x"), lax.axis_index("y")
     if to_rows:
-        sources = [refs[-piece % 4] for piece in range(4)]
-        result, field, acc, held, staged, tile_sem, field_sem, out_sem = refs[4:]
+        sources, refs = [refs[-piece % 4] for piece in range(4)], refs[4:]
+        result, field, acc, held, staged, tile_sem, out_sem = refs
         outs = 8
     else:
         sources = [refs[-(piece // 2) % 4].at[piece % 2] for piece in range(8)]
-        results = refs[4:8]
-        field, acc, held, tile_sem, field_sem = refs[8:]
+        results, (field, acc, held, tile_sem) = refs[4:8], refs[8:]
         outs = 4
 
     sides = ((0, own_meta, own_tiles), (1, sib_meta, sib_tiles))
@@ -70,30 +79,17 @@
             tiles.at[pl.ds(turn * GROUP, GROUP)], held.at[side, turn], tile_sem.at[side, turn]
         )
 
-    fills = []
+    for side, meta, tiles in sides:
+        for turn in range(SLOTS // GROUP):
+
+            @pl.when(meta[2, 0] > turn * GROUP)
+            def _(side=side, turn=turn, tiles=tiles):
+                tile_copy(side, turn, tiles).start()
+
     for piece, source in enumerate(sources):
         for part in range(PER_PIECE):
-            lanes = pl.ds(part * TILE, TILE)
-            fills.append(
-                pltpu.make_async_copy(
-                    source.at[:, lanes],
-                    field.at[piece * PER_PIECE + part],
-                    field_sem.at[piece * PER_PIECE + part],
-                )
-            )
-    for side, meta, tiles in sides:
-        tile_copy(side, 0, tiles).start()
-    for copy in fills:
-        copy.start()
-    for side, meta, tiles in sides:
-
-        @pl.when(meta[2, 0] > GROUP)
-        def _(side=side, tiles=tiles):
-            tile_copy(side, 1, tiles).start()
-
+            field[piece * PER_PIECE + part] = source[:, part * TILE : (part + 1) * TILE]
     acc[...] = jnp.zeros_like(acc)
-    for copy in fills:
-        copy.wait()
     contract = (((1,), (1,)), ((), ())) if to_rows else (((1,), (0,)), ((), ()))
     for side, meta, tiles in sides:
         used = meta[2, 0]
@@ -143,17 +139,14 @@
         copy.wait()
 
 
-def agg(to_rows, meta, tiles, sources, flops):
+def agg(to_rows, meta, tiles, sources):
     pieces, outs = (4, 8) if to_rows else (8, 4)
     scratch = [
         pltpu.VMEM((pieces * PER_PIECE, HALF, TILE), jnp.bfloat16),
         pltpu.VMEM((outs * PER_PIECE + 1, HALF, TILE), jnp.float32),
-        pltpu.VMEM((2, 64 // GROUP, GROUP, TILE, TILE), jnp.bfloat16),
+        pltpu.VMEM((2, SLOTS // GROUP, GROUP, TILE, TILE), jnp.bfloat16),
     ]
-    sems = [
-        pltpu.SemaphoreType.DMA((2, 64 // GROUP)),
-        pltpu.SemaphoreType.DMA((pieces * PER_PIECE,)),
-    ]
+    sems = [pltpu.SemaphoreType.DMA((2, SLOTS // GROUP))]
     if to_rows:
         scratch += [pltpu.VMEM((outs,) + PIECE, jnp.bfloat16)]
         sems += [pltpu.SemaphoreType.DMA((outs,))]
@@ -163,11 +156,11 @@
     return pl.pallas_call(
         functools.partial(agg_kernel, to_rows),
         out_shape=out_shape,
-        in_specs=[SMEM] * 2 + [HBM] * 2 + [ANY] * len(sources),
+        in_specs=[SMEM] * 2 + [HBM] * 2 + [VMEM] * len(sources),
         out_specs=out_specs,
         scratch_shapes=scratch + sems,
-        compiler_params=pltpu.CompilerParams(vmem_limit_bytes=28 * MIB),
-        cost_estimate=pl.CostEstimate(flops=flops, bytes_accessed=6 * MIB, transcendentals=0),
+        compiler_params=limit(AGG_VMEM),
+        cost_estimate=pl.CostEstimate(flops=AGG_FLOPS, bytes_accessed=6 * MIB, transcendentals=0),
         name="to_rows" if to_rows else "to_cols",
     )(*meta, *tiles, *sources)
 
@@ -204,59 +197,56 @@
     total = terms[0].astype(jnp.float32)
     for turn in range(1, terms.shape[0]):
         total += terms[turn].astype(jnp.float32)
-    total = total.T
-    for side in range(2):
-        core = place if side == 0 else 1 - place
-        for step in range(4):
-            rows = pl.ds(pl.multiple_of(step * 64 + core * 32, 32), 32)
-            grad[rows, :] = total[side * HALF + step * 32 : side * HALF + (step + 1) * 32, :]
+    sides = [
+        [total[:, side * HALF + step * 32 : side * HALF + (step + 1) * 32] for step in range(4)]
+        for side in range(2)
+    ]
+    first, second = (
+        jnp.concatenate([sides[(side + core) % 2][step] for step in range(4) for side in range(2)], 1)
+        for core in range(2)
+    )
+    grad[...] = jnp.where(place == 0, first, second)
 
 
 def body(features, weight, tiles, pairs, counts, cotangent):
     at_h, at_c = lax.axis_index("h"), lax.axis_index("c")
-    slot_total = tiles.shape[3]
-    own_tiles = tiles.reshape(slot_total, TILE, TILE)
+    own_tiles = tiles.reshape(SLOTS, TILE, TILE)
     own_meta = jnp.concatenate(
-        [pairs.reshape(2, slot_total), jnp.broadcast_to(counts.reshape(1, 1), (1, slot_total))]
+        [pairs.reshape(2, SLOTS), jnp.broadcast_to(counts.reshape(1, 1), (1, SLOTS))]
     )
     sib_meta = shifted(own_meta, "c", 1)
-    both_tiles = (own_tiles, shifted(own_tiles, "c", 1))
-
-    from_h = [shifted(features, "h", k) for k in (1, 2, 3)]
-    if EARLY:
-        from_h, sib_meta = lax.optimization_barrier((from_h, sib_meta))
-    meta = (own_meta, sib_meta)
+    sib_tiles = shifted(own_tiles, "c", 1)
+
+    from_h = ring(features, "h")
+    from_h, sib_meta, sib_tiles = lax.optimization_barrier((from_h, sib_meta, sib_tiles))
+    meta, both_tiles = (own_meta, sib_meta), (own_tiles, sib_tiles)
+    own_features = jnp.where(counts.reshape(()) >= 0, features, jnp.zeros_like(features))
     field = pl.pallas_call(
         order_kernel,
         out_shape=jax.ShapeDtypeStruct(PIECE, jnp.bfloat16),
         in_specs=[ANY] * 4,
         out_specs=VMEM,
         scratch_shapes=[pltpu.SemaphoreType.DMA((4,))],
-        compiler_params=pltpu.CompilerParams(vmem_limit_bytes=2 * MIB),
+        compiler_params=limit(2),
         name="order",
-    )(features, *from_h)
+    )(own_features, *from_h)
     other = shifted(field, "l", 1)
-    col_seg = [field] + [shifted(field, "x", k) for k in range(1, 4)]
-    if PACK == 0:
-        near = pl.pallas_call(
-            pack_kernel,
-            out_shape=jax.ShapeDtypeStruct((2,) + PIECE, jnp.bfloat16),
-            in_specs=[VMEM] * 2,
-            out_specs=VMEM,
-            compiler_params=pltpu.CompilerParams(vmem_limit_bytes=2 * MIB),
-            name="pack",
-        )(field, other)
-    else:
-        first = lax.axis_index("l") == 0
-        near = jnp.stack([jnp.where(first, field, other), jnp.where(first, other, field)])
-    row_seg = [near] + [shifted(near, "y", k) for k in range(1, 4)]
-    row_part = agg(True, meta, both_tiles, col_seg, FLA)
+    col_seg = [field] + ring(field, "x")
+    near = pl.pallas_call(
+        pack_kernel,
+        out_shape=jax.ShapeDtypeStruct((2,) + PIECE, jnp.bfloat16),
+        in_specs=[VMEM] * 2,
+        out_specs=VMEM,
+        compiler_params=limit(4),
+        name="pack",
+    )(field, other)
+    row_seg = [near] + ring(near, "y")
+    row_part = agg(True, meta, both_tiles, col_seg)
     row_got = list(lax.all_to_all(row_part, ("y", "l"), 0, 0, tiled=True))
-    col_part = agg(False, meta, both_tiles, row_seg, FLB)
-    col_got = [col_part[0]] + [shifted(col_part[k], "x", k) for k in range(1, 4)]
+    col_part = agg(False, meta, both_tiles, row_seg)
+    col_got = [col_part[0]] + ring(col_part, "x")
     share = sum(v.astype(jnp.float32) for v in (*row_got, *col_got)).astype(jnp.bfloat16)
-    shares = [share] + [shifted(share, "h", k) for k in (1, 2, 3)]
-    total = sum(v.astype(jnp.float32) for v in shares)
+    total = sum(v.astype(jnp.float32) for v in [share] + ring(share, "h"))
     sib_total = shifted(total, "c", 1)
 
     weight_mine = lax.dynamic_slice_in_dim(weight, (at_h * 2 + at_c) * 32, 32, 1)
@@ -271,7 +261,7 @@
         ],
         in_specs=[VMEM] * 5,
         out_specs=[VMEM] * 2,
-        compiler_params=pltpu.CompilerParams(vmem_limit_bytes=16 * MIB),
+        compiler_params=limit(16),
         name="dense",
     )(total, sib_total, weight_own, weight_sib, cotangent)
     pair = (grads + shifted(grads, "l", 1)).astype(jnp.bfloat16)
@@ -279,13 +269,13 @@
     terms = lax.all_to_all(many, ("x", "y"), 0, 0, tiled=True)
     grad = pl.pallas_call(
         finish_kernel,
-        out_shape=jax.ShapeDtypeStruct((FEAT, 32), jnp.float32),
+        out_shape=jax.ShapeDtypeStruct((32, FEAT), jnp.float32),
         in_specs=[VMEM],
         out_specs=VMEM,
-        compiler_params=pltpu.CompilerParams(vmem_limit_bytes=2 * MIB),
+        compiler_params=limit(2),
         name="finish",
     )(terms)
-    return activation, grad
+    return activation, grad.T
 
 
 def solution(mesh):

time: 92.8 us -> 87.6 us (0.944)
  local copies, waits for them, and re-layouts: 6.94 us -> 0.99 us
  Pallas kernels: 7.73 us -> 9.49 us
  starting transfers between devices: 42.8 us -> 41.3 us
  blocking collectives: 12.2 us -> 13.5 us
    unnamed x15 -> x6, local copies, waits for them, and re-layouts: 5.98 us -> 0.02 us
    ppermute x20, starting transfers between devices: 37.6 us -> 35.7 us  [shifted(): lax.ppermute(value, axis, [(i, (i + step) % total) for i in range(total)])]
    convert_element_type x1, other arithmetic: 1.49 us -> 0.21 us  [body(): sum((v.astype(jnp.float32) for v in (*row_got, *col_got)))]
    all_to_all x1, blocking collectives: 12.2 us -> 13.5 us  [body(): terms = lax.all_to_all(many, ('x', 'y'), 0, 0, tiled=True)]
    pallas_call x2, Pallas kernels: 6.53 us -> 7.63 us  [agg(): pl.pallas_call(functools.partial(agg_kernel, to_rows), out_shape=out_shap...]
  transfers between devices with their start and end apart: 21 -> 21, of which waited for: 10 -> 9; matrix products, arithmetic and copies ran while one was open for 1% -> 2% of each run, Pallas kernels for 7% -> 9%
where the time goes in v3:
time: 87.6 us; the launch traced here: 87.1 us
  starting transfers between devices  41.3 us (47%)
  waiting for transfers between devices  19.3 us (22%)
  blocking collectives  13.5 us (15%)
  Pallas kernels  9.49 us (11%)
  between operations  1.44 us (2%)
  other arithmetic  1.04 us (1%)
  local copies, waits for them, and re-layouts  0.99 us (1%)
    ppermute x20, starting transfers between devices, shifted(): lax.ppermute(value, axis, [(i, (i + step) % total) for i in range(total)])  35.7 us
    ppermute x20, waiting for transfers between devices, shifted(): lax.ppermute(value, axis, [(i, (i + step) % total) for i in range(total)])  19.3 us
    all_to_all x1, blocking collectives, body(): terms = lax.all_to_all(many, ('x', 'y'), 0, 0, tiled=True)  13.5 us
    pallas_call x2, Pallas kernels, agg(): pl.pallas_call(functools.partial(agg_kernel, to_rows), out_shape=out_shap...  7.63 us
    all_to_all x1, starting transfers between devices, body(): row_got = list(lax.all_to_all(row_part, ('y', 'l'), 0, 0, tiled=True))  5.63 us
  transfers between devices with their start and end apart: 21, of which 9 were waited for; matrix products, arithmetic and copies ran while one was open for 2% of the time, Pallas kernels for 9%

profile of v3, /device:TPU:8, one launch (start us, length us, event | category | flops | bytes accessed | tf_op | source)
XLA Modules:
  0.0 87.1 jit_solution(4606738808467434529)
XLA Ops:
  0.6 0.0 copy-start
  0.6 0.1 collective-permute-start.4
  0.7 3.3 %collective-permute-start = (bf16[32,512]{1,0:T(8,128)(2,1)}, bf16[32,512]{1,0:T(8,128)(2,1)S(1)}, u32[]{:S(2)}, u32[]{:S(2)}) collective-permute-start(bf16[32,512]{1,0:T(8,128)(2,1)} %param.6), channel_id=1, source_target_pairs={{0,2},{2,4},{4,6},{6,0},{1,3},{3,5},{5,7},{7,1},{8,10},{10,12},{12... | collective-permute-start | bytes 98312 | tf_op jit(solution)/shard_map/ppermute | solution.py:34
  4.1 5.4 %collective-permute-start.1 = (bf16[32,512]{1,0:T(8,128)(2,1)}, bf16[32,512]{1,0:T(8,128)(2,1)S(1)}, u32[]{:S(2)}, u32[]{:S(2)}) collective-permute-start(bf16[32,512]{1,0:T(8,128)(2,1)} %param.6), channel_id=1, source_target_pairs={{0,4},{2,6},{4,0},{6,2},{1,5},{3,7},{5,1},{7,3},{8,12},{10,14},{12... | collective-permute-start | bytes 98312 | tf_op jit(solution)/shard_map/ppermute | solution.py:34
  9.5 2.7 %collective-permute-start.2 = (bf16[32,512]{1,0:T(8,128)(2,1)}, bf16[32,512]{1,0:T(8,128)(2,1)S(1)}, u32[]{:S(2)}, u32[]{:S(2)}) collective-permute-start(bf16[32,512]{1,0:T(8,128)(2,1)} %param.6), channel_id=1, source_target_pairs={{0,6},{2,0},{4,2},{6,4},{1,7},{3,1},{5,3},{7,5},{8,14},{10,8},{12,... | collective-permute-start | bytes 98312 | tf_op jit(solution)/shard_map/ppermute | solution.py:34
  12.8 0.7 concatenate.3.own_meta
  13.5 0.0 collective-permute-start.3
  13.5 0.8 broadcast_select_fusion.own
  14.3 0.4 collective-permute-done.3.sib_meta
  14.7 0.0 collective-permute-done.2.r3
  14.7 0.0 collective-permute-done.4.sib_tiles
  14.7 0.2 order.1.refs_0_.own
  14.9 1.1 %collective-permute-start.8 = (bf16[128,512]{1,0:T(8,128)(2,1)S(1)}, bf16[128,512]{1,0:T(8,128)(2,1)S(1)}, u32[]{:S(2)}, u32[]{:S(2)}) collective-permute-start(bf16[128,512]{1,0:T(8,128)(2,1)S(1)} %order.1.refs_0_.own), channel_id=1, source_target_pairs={{0,8},{8,0},{1,9},{9,1},{2,10},{10,2},{3,11},{11,3},{4,12},{12,4},... | collective-permute-start | bytes 393224 | tf_op jit(solution)/shard_map/ppermute | solution.py:34
  16.0 1.5 %collective-permute-start.5 = (bf16[128,512]{1,0:T(8,128)(2,1)S(1)}, bf16[128,512]{1,0:T(8,128)(2,1)S(1)}, u32[]{:S(2)}, u32[]{:S(2)}) collective-permute-start(bf16[128,512]{1,0:T(8,128)(2,1)S(1)} %order.1.refs_0_.own), channel_id=1, source_target_pairs={{0,64},{64,128},{128,192},{192,0},{1,65},{65,129},{129,193},{193,1... | collective-permute-start | bytes 393224 | tf_op jit(solution)/shard_map/ppermute | solution.py:34
  17.5 2.7 %collective-permute-start.6 = (bf16[128,512]{1,0:T(8,128)(2,1)S(1)}, bf16[128,512]{1,0:T(8,128)(2,1)S(1)}, u32[]{:S(2)}, u32[]{:S(2)}) collective-permute-start(bf16[128,512]{1,0:T(8,128)(2,1)S(1)} %order.1.refs_0_.own), channel_id=1, source_target_pairs={{0,128},{64,192},{128,0},{192,64},{1,129},{65,193},{129,1},{193,65... | collective-permute-start | bytes 393224 | tf_op jit(solution)/shard_map/ppermute | solution.py:34
  20.2 1.4 %collective-permute-start.7 = (bf16[128,512]{1,0:T(8,128)(2,1)S(1)}, bf16[128,512]{1,0:T(8,128)(2,1)S(1)}, u32[]{:S(2)}, u32[]{:S(2)}) collective-permute-start(bf16[128,512]{1,0:T(8,128)(2,1)S(1)} %order.1.refs_0_.own), channel_id=1, source_target_pairs={{0,192},{64,0},{128,64},{192,128},{1,193},{65,1},{129,65},{193,129... | collective-permute-start | bytes 393224 | tf_op jit(solution)/shard_map/ppermute | solution.py:34
  21.7 1.7 %collective-permute-start.9 = (bf16[2,128,512]{2,1,0:T(8,128)(2,1)S(1)}, bf16[2,128,512]{2,1,0:T(8,128)(2,1)S(1)}, u32[]{:S(2)}, u32[]{:S(2)}) collective-permute-start(bf16[2,128,512]{2,1,0:T(8,128)(2,1)S(1)} %pack.1.refs_0_), channel_id=1, source_target_pairs={{0,16},{16,32},{32,48},{48,0},{1,17},{17,33},{33,49},{49,1},{2,18}... | collective-permute-start | bytes 786440 | tf_op jit(solution)/shard_map/ppermute | solution.py:34
  23.4 0.9 %collective-permute-start.10 = (bf16[2,128,512]{2,1,0:T(8,128)(2,1)S(1)}, bf16[2,128,512]{2,1,0:T(8,128)(2,1)S(1)}, u32[]{:S(2)}, u32[]{:S(2)}) collective-permute-start(bf16[2,128,512]{2,1,0:T(8,128)(2,1)S(1)} %pack.1.refs_0_), channel_id=1, source_target_pairs={{0,32},{16,48},{32,0},{48,16},{1,33},{17,49},{33,1},{49,17},{2,34}... | collective-permute-start | bytes 786440 | tf_op jit(solution)/shard_map/ppermute | solution.py:34
  24.3 2.4 %collective-permute-start.11 = (bf16[2,128,512]{2,1,0:T(8,128)(2,1)S(1)}, bf16[2,128,512]{2,1,0:T(8,128)(2,1)S(1)}, u32[]{:S(2)}, u32[]{:S(2)}) collective-permute-start(bf16[2,128,512]{2,1,0:T(8,128)(2,1)S(1)} %pack.1.refs_0_), channel_id=1, source_target_pairs={{0,48},{16,0},{32,16},{48,32},{1,49},{17,1},{33,17},{49,33},{2,50}... | collective-permute-start | bytes 786440 | tf_op jit(solution)/shard_map/ppermute | solution.py:34
  26.7 0.0 collective-permute-done.6.refs_2_
  26.7 4.7 %to_rows.1 = bf16[8,128,512]{2,1,0:T(8,128)(2,1)} custom-call(s32[3,64]{1,0:T(4,128)S(1)} %concatenate.3.own_meta, s32[3,64]{1,0:T(4,128)S(1)} %collective-permute-done.3.sib_meta, bf16[64,128,128]{2,1,0:T(8,128)(2,1)} %bitcast.33, bf16[64,128,128]{2,1,0:T(8,128)(2,1)} %copy-done.2, bf16[128,512]{1,0:T(8,128)(2,1)S(1)} %order.1.refs_0_.own, ...), custom_call_target="tpu_custom_call" | custom-call | flops 20000000000 | bytes 6291456 | tf_op jit(solution)/shard_map/to_rows/pallas_call | solution.py:156
  31.4 5.6 %all-to-all-start = ((bf16[8,128,512]{2,1,0:T(8,128)(2,1)}), bf16[8,128,512]{2,1,0:T(8,128)(2,1)S(1)}, u32[]{:S(2)}, u32[]{:S(2)}) async-start(bf16[8,128,512]{2,1,0:T(8,128)(2,1)} %to_rows.1), calls=%async_computation | async-start | bytes 2097152 | tf_op jit(solution)/shard_map/all_to_all | solution.py:245
  37.1 3.0 %to_cols.1 = (bf16[128,512]{1,0:T(8,128)(2,1)S(1)}, bf16[128,512]{1,0:T(8,128)(2,1)S(1)}, bf16[128,512]{1,0:T(8,128)(2,1)S(1)}, bf16[128,512]{1,0:T(8,128)(2,1)S(1)}) custom-call(s32[3,64]{1,0:T(4,128)S(1)} %concatenate.3.own_meta, s32[3,64]{1,0:T(4,128)S(1)} %collective-permute-done.3.sib_meta, bf16[64,128,128]{2,1,0:T(8,128)(2,1)} %bitcast.34, ...), custom_call_target="tpu_custom_call" | custom-call | flops 20000000000 | bytes 6291456 | tf_op jit(solution)/shard_map/to_cols/pallas_call | solution.py:156
  40.0 0.0 copy-start.1
  40.0 2.4 %collective-permute-start.14 = (bf16[128,512]{1,0:T(8,128)(2,1)S(1)}, bf16[128,512]{1,0:T(8,128)(2,1)S(1)}, u32[]{:S(2)}, u32[]{:S(2)}) collective-permute-start(bf16[128,512]{1,0:T(8,128)(2,1)S(1)} %get-tuple-element.21), channel_id=1, source_target_pairs={{0,192},{64,0},{128,64},{192,128},{1,193},{65,1},{129,65},{193,129... | collective-permute-start | bytes 393224 | tf_op jit(solution)/shard_map/ppermute | solution.py:34
  42.4 1.7 %collective-permute-start.13 = (bf16[128,512]{1,0:T(8,128)(2,1)S(1)}, bf16[128,512]{1,0:T(8,128)(2,1)S(1)}, u32[]{:S(2)}, u32[]{:S(2)}) collective-permute-start(bf16[128,512]{1,0:T(8,128)(2,1)S(1)} %get-tuple-element.20), channel_id=1, source_target_pairs={{0,128},{64,192},{128,0},{192,64},{1,129},{65,193},{129,1},{193,65... | collective-permute-start | bytes 393224 | tf_op jit(solution)/shard_map/ppermute | solution.py:34
  44.1 1.1 %collective-permute-start.12 = (bf16[128,512]{1,0:T(8,128)(2,1)S(1)}, bf16[128,512]{1,0:T(8,128)(2,1)S(1)}, u32[]{:S(2)}, u32[]{:S(2)}) collective-permute-start(bf16[128,512]{1,0:T(8,128)(2,1)S(1)} %get-tuple-element.19), channel_id=1, source_target_pairs={{0,64},{64,128},{128,192},{192,0},{1,65},{65,129},{129,193},{193,1... | collective-permute-start | bytes 393224 | tf_op jit(solution)/shard_map/ppermute | solution.py:34
  45.3 1.2 %collective-permute-done.14 = bf16[128,512]{1,0:T(8,128)(2,1)S(1)} collective-permute-done((bf16[128,512]{1,0:T(8,128)(2,1)S(1)}, bf16[128,512]{1,0:T(8,128)(2,1)S(1)}, u32[]{:S(2)}, u32[]{:S(2)}) %collective-permute-start.14) | collective-permute-done | bytes 131104 | tf_op jit(solution)/shard_map/ppermute | solution.py:34
  46.4 2.7 %collective-permute-done.13 = bf16[128,512]{1,0:T(8,128)(2,1)S(1)} collective-permute-done((bf16[128,512]{1,0:T(8,128)(2,1)S(1)}, bf16[128,512]{1,0:T(8,128)(2,1)S(1)}, u32[]{:S(2)}, u32[]{:S(2)}) %collective-permute-start.13) | collective-permute-done | bytes 131104 | tf_op jit(solution)/shard_map/ppermute | solution.py:34
  49.1 1.4 %collective-permute-done.12 = bf16[128,512]{1,0:T(8,128)(2,1)S(1)} collective-permute-done((bf16[128,512]{1,0:T(8,128)(2,1)S(1)}, bf16[128,512]{1,0:T(8,128)(2,1)S(1)}, u32[]{:S(2)}, u32[]{:S(2)}) %collective-permute-start.12) | collective-permute-done | bytes 131104 | tf_op jit(solution)/shard_map/ppermute | solution.py:34
  50.5 0.2 fusion.3
  50.7 3.5 %collective-permute-start.17 = (bf16[128,512]{1,0:T(8,128)(2,1)S(1)}, bf16[128,512]{1,0:T(8,128)(2,1)S(1)}, u32[]{:S(2)}, u32[]{:S(2)}) collective-permute-start(bf16[128,512]{1,0:T(8,128)(2,1)S(1)} %fusion.3), channel_id=1, source_target_pairs={{0,6},{2,0},{4,2},{6,4},{1,7},{3,1},{5,3},{7,5},{8,14},{10,8},{12,... | collective-permute-start | bytes 393224 | tf_op jit(solution)/shard_map/ppermute | solution.py:34
  54.2 1.2 %collective-permute-start.16 = (bf16[128,512]{1,0:T(8,128)(2,1)S(1)}, bf16[128,512]{1,0:T(8,128)(2,1)S(1)}, u32[]{:S(2)}, u32[]{:S(2)}) collective-permute-start(bf16[128,512]{1,0:T(8,128)(2,1)S(1)} %fusion.3), channel_id=1, source_target_pairs={{0,4},{2,6},{4,0},{6,2},{1,5},{3,7},{5,1},{7,3},{8,12},{10,14},{12... | collective-permute-start | bytes 393224 | tf_op jit(solution)/shard_map/ppermute | solution.py:34
  55.4 1.3 %collective-permute-start.15 = (bf16[128,512]{1,0:T(8,128)(2,1)S(1)}, bf16[128,512]{1,0:T(8,128)(2,1)S(1)}, u32[]{:S(2)}, u32[]{:S(2)}) collective-permute-start(bf16[128,512]{1,0:T(8,128)(2,1)S(1)} %fusion.3), channel_id=1, source_target_pairs={{0,2},{2,4},{4,6},{6,0},{1,3},{3,5},{5,7},{7,1},{8,10},{10,12},{12... | collective-permute-start | bytes 393224 | tf_op jit(solution)/shard_map/ppermute | solution.py:34
  56.6 5.3 %collective-permute-done.17 = bf16[128,512]{1,0:T(8,128)(2,1)S(1)} collective-permute-done((bf16[128,512]{1,0:T(8,128)(2,1)S(1)}, bf16[128,512]{1,0:T(8,128)(2,1)S(1)}, u32[]{:S(2)}, u32[]{:S(2)}) %collective-permute-start.17) | collective-permute-done | bytes 131104 | tf_op jit(solution)/shard_map/ppermute | solution.py:34
  62.0 2.0 %collective-permute-done.16 = bf16[128,512]{1,0:T(8,128)(2,1)S(1)} collective-permute-done((bf16[128,512]{1,0:T(8,128)(2,1)S(1)}, bf16[128,512]{1,0:T(8,128)(2,1)S(1)}, u32[]{:S(2)}, u32[]{:S(2)}) %collective-permute-start.16) | collective-permute-done | bytes 131104 | tf_op jit(solution)/shard_map/ppermute | solution.py:34
  63.9 2.4 %collective-permute-done.15 = bf16[128,512]{1,0:T(8,128)(2,1)S(1)} collective-permute-done((bf16[128,512]{1,0:T(8,128)(2,1)S(1)}, bf16[128,512]{1,0:T(8,128)(2,1)S(1)}, u32[]{:S(2)}, u32[]{:S(2)}) %collective-permute-start.15) | collective-permute-done | bytes 131104 | tf_op jit(solution)/shard_map/ppermute | solution.py:34
  66.4 0.1 convert_add_fusion.own_ref
  66.4 0.1 collective-permute-start.18
  66.5 0.1 constant_dynamic-slice_fusion.2
  66.7 0.1 copy.15
  66.7 0.1 copy.16
  66.8 1.2 %collective-permute-done.18.sib_ref = f32[128,512]{1,0:T(8,128)S(1)} collective-permute-done((f32[128,512]{1,0:T(8,128)S(1)}, f32[128,512]{1,0:T(8,128)S(1)}, u32[]{:S(2)}, u32[]{:S(2)}) %collective-permute-start.18) | collective-permute-done | bytes 262176 | tf_op jit(solution)/shard_map/ppermute | solution.py:34
  68.0 0.9 dense.1
  68.9 1.2 %collective-permute-start.19 = (f32[32,256]{1,0:T(8,128)S(1)}, f32[32,256]{1,0:T(8,128)S(1)}, u32[]{:S(2)}, u32[]{:S(2)}) collective-permute-start(f32[32,256]{1,0:T(8,128)S(1)} %get-tuple-element.23), channel_id=1, source_target_pairs={{0,8},{8,0},{1,9},{9,1},{2,10},{10,2},{3,11},{11,3},{4,12},{12,4},... | collective-permute-start | bytes 98312 | tf_op jit(solution)/shard_map/ppermute | solution.py:34
  70.1 2.7 %collective-permute-done.19 = f32[32,256]{1,0:T(8,128)S(1)} collective-permute-done((f32[32,256]{1,0:T(8,128)S(1)}, f32[32,256]{1,0:T(8,128)S(1)}, u32[]{:S(2)}, u32[]{:S(2)}) %collective-permute-start.19) | collective-permute-done | bytes 32800 | tf_op jit(solution)/shard_map/ppermute | solution.py:34
  72.9 13.5 %all_to_all.10.terms = bf16[16,32,256]{2,1,0:T(8,128)(2,1)S(1)} all-to-all(bf16[16,32,256]{2,1,0:T(8,128)(2,1)S(1)} %broadcast_in_dim.16), channel_id=1, replica_groups=mesh['x'=4,'y'=4,'l'=2,'h'=4,'c'=2] {'x','y'}, dimensions={0} | all-to-all | bytes 524288 | tf_op jit(solution)/shard_map/all_to_all | solution.py:269
  86.3 0.7 finish.1
  (17 shorter events, 0.1 us)
Async XLA Ops:
  0.6 65.9 %copy-start = (bf16[256,256]{1,0:T(8,128)(2,1)S(1)}, bf16[256,256]{1,0:T(8,128)(2,1)}, u32[]{:S(2)}) copy-start(bf16[256,256]{1,0:T(8,128)(2,1)} %param.7) | copy-start | bytes 393220
  0.6 14.0 %collective-permute-start.4 = (bf16[64,128,128]{2,1,0:T(8,128)(2,1)}, bf16[64,128,128]{2,1,0:T(8,128)(2,1)S(1)}, u32[]{:S(2)}, u32[]{:S(2)}) collective-permute-start(bf16[64,128,128]{2,1,0:T(8,128)(2,1)} %bitcast.32), channel_id=1, source_target_pairs={{0,1},{1,0},{2,3},{3,2},{4,5},{5,4},{6,7},{7,6},{8,9},{9,8},{10,11... | collective-permute-start | bytes 6291464 | tf_op jit(solution)/shard_map/ppermute | solution.py:34
  0.7 13.9 %collective-permute-start = (bf16[32,512]{1,0:T(8,128)(2,1)}, bf16[32,512]{1,0:T(8,128)(2,1)S(1)}, u32[]{:S(2)}, u32[]{:S(2)}) collective-permute-start(bf16[32,512]{1,0:T(8,128)(2,1)} %param.6), channel_id=1, source_target_pairs={{0,2},{2,4},{4,6},{6,0},{1,3},{3,5},{5,7},{7,1},{8,10},{10,12},{12... | collective-permute-start | bytes 98312 | tf_op jit(solution)/shard_map/ppermute | solution.py:34
  4.1 10.6 %collective-permute-start.1 = (bf16[32,512]{1,0:T(8,128)(2,1)}, bf16[32,512]{1,0:T(8,128)(2,1)S(1)}, u32[]{:S(2)}, u32[]{:S(2)}) collective-permute-start(bf16[32,512]{1,0:T(8,128)(2,1)} %param.6), channel_id=1, source_target_pairs={{0,4},{2,6},{4,0},{6,2},{1,5},{3,7},{5,1},{7,3},{8,12},{10,14},{12... | collective-permute-start | bytes 98312 | tf_op jit(solution)/shard_map/ppermute | solution.py:34
  9.5 5.2 %collective-permute-start.2 = (bf16[32,512]{1,0:T(8,128)(2,1)}, bf16[32,512]{1,0:T(8,128)(2,1)S(1)}, u32[]{:S(2)}, u32[]{:S(2)}) collective-permute-start(bf16[32,512]{1,0:T(8,128)(2,1)} %param.6), channel_id=1, source_target_pairs={{0,6},{2,0},{4,2},{6,4},{1,7},{3,1},{5,3},{7,5},{8,14},{10,8},{12,... | collective-permute-start | bytes 98312 | tf_op jit(solution)/shard_map/ppermute | solution.py:34
  13.5 1.2 %collective-permute-start.3 = (s32[3,64]{1,0:T(4,128)S(1)}, s32[3,64]{1,0:T(4,128)S(1)}, u32[]{:S(2)}, u32[]{:S(2)}) collective-permute-start(s32[3,64]{1,0:T(4,128)S(1)} %concatenate.3.own_meta), channel_id=1, source_target_pairs={{0,1},{1,0},{2,3},{3,2},{4,5},{5,4},{6,7},{7,6},{8,9},{9,8},{10,11... | collective-permute-start | bytes 2312 | tf_op jit(solution)/shard_map/ppermute | solution.py:34
  14.7 12.1 %copy-start.2 = (bf16[64,128,128]{2,1,0:T(8,128)(2,1)}, bf16[64,128,128]{2,1,0:T(8,128)(2,1)S(1)}, u32[]{:S(2)}) copy-start(bf16[64,128,128]{2,1,0:T(8,128)(2,1)S(1)} %collective-permute-done.4.sib_tiles) | copy-start | bytes 6291460
  14.9 6.8 %collective-permute-start.8 = (bf16[128,512]{1,0:T(8,128)(2,1)S(1)}, bf16[128,512]{1,0:T(8,128)(2,1)S(1)}, u32[]{:S(2)}, u32[]{:S(2)}) collective-permute-start(bf16[128,512]{1,0:T(8,128)(2,1)S(1)} %order.1.refs_0_.own), channel_id=1, source_target_pairs={{0,8},{8,0},{1,9},{9,1},{2,10},{10,2},{3,11},{11,3},{4,12},{12,4},... | collective-permute-start | bytes 393224 | tf_op jit(solution)/shard_map/ppermute | solution.py:34
  16.0 8.3 %collective-permute-start.5 = (bf16[128,512]{1,0:T(8,128)(2,1)S(1)}, bf16[128,512]{1,0:T(8,128)(2,1)S(1)}, u32[]{:S(2)}, u32[]{:S(2)}) collective-permute-start(bf16[128,512]{1,0:T(8,128)(2,1)S(1)} %order.1.refs_0_.own), channel_id=1, source_target_pairs={{0,64},{64,128},{128,192},{192,0},{1,65},{65,129},{129,193},{193,1... | collective-permute-start | bytes 393224 | tf_op jit(solution)/shard_map/ppermute | solution.py:34
  17.5 9.2 %collective-permute-start.6 = (bf16[128,512]{1,0:T(8,128)(2,1)S(1)}, bf16[128,512]{1,0:T(8,128)(2,1)S(1)}, u32[]{:S(2)}, u32[]{:S(2)}) collective-permute-start(bf16[128,512]{1,0:T(8,128)(2,1)S(1)} %order.1.refs_0_.own), channel_id=1, source_target_pairs={{0,128},{64,192},{128,0},{192,64},{1,129},{65,193},{129,1},{193,65... | collective-permute-start | bytes 393224 | tf_op jit(solution)/shard_map/ppermute | solution.py:34
  20.2 6.5 %collective-permute-start.7 = (bf16[128,512]{1,0:T(8,128)(2,1)S(1)}, bf16[128,512]{1,0:T(8,128)(2,1)S(1)}, u32[]{:S(2)}, u32[]{:S(2)}) collective-permute-start(bf16[128,512]{1,0:T(8,128)(2,1)S(1)} %order.1.refs_0_.own), channel_id=1, source_target_pairs={{0,192},{64,0},{128,64},{192,128},{1,193},{65,1},{129,65},{193,129... | collective-permute-start | bytes 393224 | tf_op jit(solution)/shard_map/ppermute | solution.py:34
  21.7 15.3 %collective-permute-start.9 = (bf16[2,128,512]{2,1,0:T(8,128)(2,1)S(1)}, bf16[2,128,512]{2,1,0:T(8,128)(2,1)S(1)}, u32[]{:S(2)}, u32[]{:S(2)}) collective-permute-start(bf16[2,128,512]{2,1,0:T(8,128)(2,1)S(1)} %pack.1.refs_0_), channel_id=1, source_target_pairs={{0,16},{16,32},{32,48},{48,0},{1,17},{17,33},{33,49},{49,1},{2,18}... | collective-permute-start | bytes 786440 | tf_op jit(solution)/shard_map/ppermute | solution.py:34
  23.4 13.7 %collective-permute-start.10 = (bf16[2,128,512]{2,1,0:T(8,128)(2,1)S(1)}, bf16[2,128,512]{2,1,0:T(8,128)(2,1)S(1)}, u32[]{:S(2)}, u32[]{:S(2)}) collective-permute-start(bf16[2,128,512]{2,1,0:T(8,128)(2,1)S(1)} %pack.1.refs_0_), channel_id=1, source_target_pairs={{0,32},{16,48},{32,0},{48,16},{1,33},{17,49},{33,1},{49,17},{2,34}... | collective-permute-start | bytes 786440 | tf_op jit(solution)/shard_map/ppermute | solution.py:34
  24.3 12.7 %collective-permute-start.11 = (bf16[2,128,512]{2,1,0:T(8,128)(2,1)S(1)}, bf16[2,128,512]{2,1,0:T(8,128)(2,1)S(1)}, u32[]{:S(2)}, u32[]{:S(2)}) collective-permute-start(bf16[2,128,512]{2,1,0:T(8,128)(2,1)S(1)} %pack.1.refs_0_), channel_id=1, source_target_pairs={{0,48},{16,0},{32,16},{48,32},{1,49},{17,1},{33,17},{49,33},{2,50}... | collective-permute-start | bytes 786440 | tf_op jit(solution)/shard_map/ppermute | solution.py:34
  31.4 19.1 %all-to-all-start = ((bf16[8,128,512]{2,1,0:T(8,128)(2,1)}), bf16[8,128,512]{2,1,0:T(8,128)(2,1)S(1)}, u32[]{:S(2)}, u32[]{:S(2)}) async-start(bf16[8,128,512]{2,1,0:T(8,128)(2,1)} %to_rows.1), calls=%async_computation | async-start | bytes 2097152 | tf_op jit(solution)/shard_map/all_to_all | solution.py:245
  40.0 28.0 %copy-start.1 = (bf16[32,512]{1,0:T(8,128)(2,1)S(1)}, bf16[32,512]{1,0:T(8,128)(2,1)}, u32[]{:S(2)}) copy-start(bf16[32,512]{1,0:T(8,128)(2,1)} %cotangent.1) | copy-start | bytes 98308
  40.0 6.4 %collective-permute-start.14 = (bf16[128,512]{1,0:T(8,128)(2,1)S(1)}, bf16[128,512]{1,0:T(8,128)(2,1)S(1)}, u32[]{:S(2)}, u32[]{:S(2)}) collective-permute-start(bf16[128,512]{1,0:T(8,128)(2,1)S(1)} %get-tuple-element.21), channel_id=1, source_target_pairs={{0,192},{64,0},{128,64},{192,128},{1,193},{65,1},{129,65},{193,129... | collective-permute-start | bytes 393224 | tf_op jit(solution)/shard_map/ppermute | solution.py:34
  42.4 6.7 %collective-permute-start.13 = (bf16[128,512]{1,0:T(8,128)(2,1)S(1)}, bf16[128,512]{1,0:T(8,128)(2,1)S(1)}, u32[]{:S(2)}, u32[]{:S(2)}) collective-permute-start(bf16[128,512]{1,0:T(8,128)(2,1)S(1)} %get-tuple-element.20), channel_id=1, source_target_pairs={{0,128},{64,192},{128,0},{192,64},{1,129},{65,193},{129,1},{193,65... | collective-permute-start | bytes 393224 | tf_op jit(solution)/shard_map/ppermute | solution.py:34
  44.1 6.4 %collective-permute-start.12 = (bf16[128,512]{1,0:T(8,128)(2,1)S(1)}, bf16[128,512]{1,0:T(8,128)(2,1)S(1)}, u32[]{:S(2)}, u32[]{:S(2)}) collective-permute-start(bf16[128,512]{1,0:T(8,128)(2,1)S(1)} %get-tuple-element.19), channel_id=1, source_target_pairs={{0,64},{64,128},{128,192},{192,0},{1,65},{65,129},{129,193},{193,1... | collective-permute-start | bytes 393224 | tf_op jit(solution)/shard_map/ppermute | solution.py:34
  50.7 11.2 %collective-permute-start.17 = (bf16[128,512]{1,0:T(8,128)(2,1)S(1)}, bf16[128,512]{1,0:T(8,128)(2,1)S(1)}, u32[]{:S(2)}, u32[]{:S(2)}) collective-permute-start(bf16[128,512]{1,0:T(8,128)(2,1)S(1)} %fusion.3), channel_id=1, source_target_pairs={{0,6},{2,0},{4,2},{6,4},{1,7},{3,1},{5,3},{7,5},{8,14},{10,8},{12,... | collective-permute-start | bytes 393224 | tf_op jit(solution)/shard_map/ppermute | solution.py:34
  54.2 9.7 %collective-permute-start.16 = (bf16[128,512]{1,0:T(8,128)(2,1)S(1)}, bf16[128,512]{1,0:T(8,128)(2,1)S(1)}, u32[]{:S(2)}, u32[]{:S(2)}) collective-permute-start(bf16[128,512]{1,0:T(8,128)(2,1)S(1)} %fusion.3), channel_id=1, source_target_pairs={{0,4},{2,6},{4,0},{6,2},{1,5},{3,7},{5,1},{7,3},{8,12},{10,14},{12... | collective-permute-start | bytes 393224 | tf_op jit(solution)/shard_map/ppermute | solution.py:34
  55.4 11.0 %collective-permute-start.15 = (bf16[128,512]{1,0:T(8,128)(2,1)S(1)}, bf16[128,512]{1,0:T(8,128)(2,1)S(1)}, u32[]{:S(2)}, u32[]{:S(2)}) collective-permute-start(bf16[128,512]{1,0:T(8,128)(2,1)S(1)} %fusion.3), channel_id=1, source_target_pairs={{0,2},{2,4},{4,6},{6,0},{1,3},{3,5},{5,7},{7,1},{8,10},{10,12},{12... | collective-permute-start | bytes 393224 | tf_op jit(solution)/shard_map/ppermute | solution.py:34
  66.4 1.6 %collective-permute-start.18 = (f32[128,512]{1,0:T(8,128)S(1)}, f32[128,512]{1,0:T(8,128)S(1)}, u32[]{:S(2)}, u32[]{:S(2)}) collective-permute-start(f32[128,512]{1,0:T(8,128)S(1)} %convert_add_fusion.own_ref), channel_id=1, source_target_pairs={{0,1},{1,0},{2,3},{3,2},{4,5},{5,4},{6,7},{7,6},{8,9},{9,8},{10,11... | collective-permute-start | bytes 786440 | tf_op jit(solution)/shard_map/ppermute | solution.py:34
  68.9 3.9 %collective-permute-start.19 = (f32[32,256]{1,0:T(8,128)S(1)}, f32[32,256]{1,0:T(8,128)S(1)}, u32[]{:S(2)}, u32[]{:S(2)}) collective-permute-start(f32[32,256]{1,0:T(8,128)S(1)} %get-tuple-element.23), channel_id=1, source_target_pairs={{0,8},{8,0},{1,9},{9,1},{2,10},{10,2},{3,11},{11,3},{4,12},{12,4},... | collective-permute-start | bytes 98312 | tf_op jit(solution)/shard_map/ppermute | solution.py:34

commit v4 on v3

--- a/solution.py
+++ b/solution.py
@@ -40,6 +40,10 @@
         value = values[step] if isinstance(values, (list, tuple)) else values
         got[step] = shifted(value, axis, step)
     return got[1:]
+
+
+def swaps(value, axis):
+    return [lax.ppermute(value, axis, [(i, i ^ bits) for i in range(4)]) for bits in (2, 1, 3)]
 
 
 def order_kernel(own, r1, r2, r3, field, arrive):
@@ -246,7 +250,7 @@
     col_part = agg(False, meta, both_tiles, row_seg)
     col_got = [col_part[0]] + ring(col_part, "x")
     share = sum(v.astype(jnp.float32) for v in (*row_got, *col_got)).astype(jnp.bfloat16)
-    total = sum(v.astype(jnp.float32) for v in [share] + ring(share, "h"))
+    total = sum(v.astype(jnp.float32) for v in [share] + swaps(share, "h"))
     sib_total = shifted(total, "c", 1)
 
     weight_mine = lax.dynamic_slice_in_dim(weight, (at_h * 2 + at_c) * 32, 32, 1)

time: 87.6 us -> 86.3 us (0.985)
  starting transfers between devices: 41.3 us -> 39.5 us
  waiting for transfers between devices: 19.3 us -> 20.8 us
    ppermute x0 -> x3, waiting for transfers between devices: none -> 8.68 us  [swaps(): lax.ppermute(value, axis, [(i, i ^ bits) for i in range(4)])]
    ppermute x20 -> x17, starting transfers between devices: 35.7 us -> 27.2 us  [shifted(): lax.ppermute(value, axis, [(i, (i + step) % total) for i in range(total)])]
    ppermute x20 -> x17, waiting for transfers between devices: 19.3 us -> 12.1 us  [shifted(): lax.ppermute(value, axis, [(i, (i + step) % total) for i in range(total)])]
    ppermute x0 -> x3, starting transfers between devices: none -> 6.58 us  [swaps(): lax.ppermute(value, axis, [(i, i ^ bits) for i in range(4)])]
where the time goes in v4:
time: 86.3 us
  starting transfers between devices  39.5 us (46%)
  waiting for transfers between devices  20.8 us (24%)
  blocking collectives  13 us (15%)
  Pallas kernels  9.49 us (11%)
  between operations  1.44 us (2%)
  other arithmetic  1.04 us (1%)
  local copies, waits for them, and re-layouts  0.99 us (1%)
    ppermute x17, starting transfers between devices, shifted(): lax.ppermute(value, axis, [(i, (i + step) % total) for i in range(total)])  27.2 us
    all_to_all x1, blocking collectives, body(): terms = lax.all_to_all(many, ('x', 'y'), 0, 0, tiled=True)  13 us
    ppermute x17, waiting for transfers between devices, shifted(): lax.ppermute(value, axis, [(i, (i + step) % total) for i in range(total)])  12.1 us
    ppermute x3, waiting for transfers between devices, swaps(): lax.ppermute(value, axis, [(i, i ^ bits) for i in range(4)])  8.68 us
    pallas_call x2, Pallas kernels, agg(): pl.pallas_call(functools.partial(agg_kernel, to_rows), out_shape=out_shap...  7.63 us
    ppermute x3, starting transfers between devices, swaps(): lax.ppermute(value, axis, [(i, i ^ bits) for i in range(4)])  6.58 us
    all_to_all x1, starting transfers between devices, body(): row_got = list(lax.all_to_all(row_part, ('y', 'l'), 0, 0, tiled=True))  5.68 us
  transfers between devices with their start and end apart: 21, of which 9 were waited for; matrix products, arithmetic and copies ran while one was open for 2% of the time, Pallas kernels for 9%

profile of v4, /device:TPU:8, one launch (start us, length us, event | category | flops | bytes accessed | tf_op | source)
XLA Modules:
  0.0 86.3 jit_solution(17277637629386139341)
XLA Ops:
  0.6 0.0 copy-start
  0.6 0.1 collective-permute-start.4
  0.7 3.3 %collective-permute-start = (bf16[32,512]{1,0:T(8,128)(2,1)}, bf16[32,512]{1,0:T(8,128)(2,1)S(1)}, u32[]{:S(2)}, u32[]{:S(2)}) collective-permute-start(bf16[32,512]{1,0:T(8,128)(2,1)} %param.6), channel_id=1, source_target_pairs={{0,2},{2,4},{4,6},{6,0},{1,3},{3,5},{5,7},{7,1},{8,10},{10,12},{12... | collective-permute-start | bytes 98312 | tf_op jit(solution)/shard_map/ppermute | solution.py:34
  4.1 5.4 %collective-permute-start.1 = (bf16[32,512]{1,0:T(8,128)(2,1)}, bf16[32,512]{1,0:T(8,128)(2,1)S(1)}, u32[]{:S(2)}, u32[]{:S(2)}) collective-permute-start(bf16[32,512]{1,0:T(8,128)(2,1)} %param.6), channel_id=1, source_target_pairs={{0,4},{2,6},{4,0},{6,2},{1,5},{3,7},{5,1},{7,3},{8,12},{10,14},{12... | collective-permute-start | bytes 98312 | tf_op jit(solution)/shard_map/ppermute | solution.py:34
  9.5 2.7 %collective-permute-start.2 = (bf16[32,512]{1,0:T(8,128)(2,1)}, bf16[32,512]{1,0:T(8,128)(2,1)S(1)}, u32[]{:S(2)}, u32[]{:S(2)}) collective-permute-start(bf16[32,512]{1,0:T(8,128)(2,1)} %param.6), channel_id=1, source_target_pairs={{0,6},{2,0},{4,2},{6,4},{1,7},{3,1},{5,3},{7,5},{8,14},{10,8},{12,... | collective-permute-start | bytes 98312 | tf_op jit(solution)/shard_map/ppermute | solution.py:34
  12.8 0.7 concatenate.3.own_meta
  13.5 0.8 broadcast_select_fusion.own
  14.3 0.4 collective-permute-done.3.sib_meta
  14.6 0.0 collective-permute-done.r1
  14.7 0.0 collective-permute-done.1.r2
  14.7 0.2 order.1.refs_0_.own
  14.9 1.1 %collective-permute-start.8 = (bf16[128,512]{1,0:T(8,128)(2,1)S(1)}, bf16[128,512]{1,0:T(8,128)(2,1)S(1)}, u32[]{:S(2)}, u32[]{:S(2)}) collective-permute-start(bf16[128,512]{1,0:T(8,128)(2,1)S(1)} %order.1.refs_0_.own), channel_id=1, source_target_pairs={{0,8},{8,0},{1,9},{9,1},{2,10},{10,2},{3,11},{11,3},{4,12},{12,4},... | collective-permute-start | bytes 393224 | tf_op jit(solution)/shard_map/ppermute | solution.py:34
  16.0 1.5 %collective-permute-start.5 = (bf16[128,512]{1,0:T(8,128)(2,1)S(1)}, bf16[128,512]{1,0:T(8,128)(2,1)S(1)}, u32[]{:S(2)}, u32[]{:S(2)}) collective-permute-start(bf16[128,512]{1,0:T(8,128)(2,1)S(1)} %order.1.refs_0_.own), channel_id=1, source_target_pairs={{0,64},{64,128},{128,192},{192,0},{1,65},{65,129},{129,193},{193,1... | collective-permute-start | bytes 393224 | tf_op jit(solution)/shard_map/ppermute | solution.py:34
  17.5 2.7 %collective-permute-start.6 = (bf16[128,512]{1,0:T(8,128)(2,1)S(1)}, bf16[128,512]{1,0:T(8,128)(2,1)S(1)}, u32[]{:S(2)}, u32[]{:S(2)}) collective-permute-start(bf16[128,512]{1,0:T(8,128)(2,1)S(1)} %order.1.refs_0_.own), channel_id=1, source_target_pairs={{0,128},{64,192},{128,0},{192,64},{1,129},{65,193},{129,1},{193,65... | collective-permute-start | bytes 393224 | tf_op jit(solution)/shard_map/ppermute | solution.py:34
  20.2 1.4 %collective-permute-start.7 = (bf16[128,512]{1,0:T(8,128)(2,1)S(1)}, bf16[128,512]{1,0:T(8,128)(2,1)S(1)}, u32[]{:S(2)}, u32[]{:S(2)}) collective-permute-start(bf16[128,512]{1,0:T(8,128)(2,1)S(1)} %order.1.refs_0_.own), channel_id=1, source_target_pairs={{0,192},{64,0},{128,64},{192,128},{1,193},{65,1},{129,65},{193,129... | collective-permute-start | bytes 393224 | tf_op jit(solution)/shard_map/ppermute | solution.py:34
  21.7 0.0 collective-permute-done.8.other
  21.7 1.7 %collective-permute-start.9 = (bf16[2,128,512]{2,1,0:T(8,128)(2,1)S(1)}, bf16[2,128,512]{2,1,0:T(8,128)(2,1)S(1)}, u32[]{:S(2)}, u32[]{:S(2)}) collective-permute-start(bf16[2,128,512]{2,1,0:T(8,128)(2,1)S(1)} %pack.1.refs_0_), channel_id=1, source_target_pairs={{0,16},{16,32},{32,48},{48,0},{1,17},{17,33},{33,49},{49,1},{2,18}... | collective-permute-start | bytes 786440 | tf_op jit(solution)/shard_map/ppermute | solution.py:34
  23.4 0.9 %collective-permute-start.10 = (bf16[2,128,512]{2,1,0:T(8,128)(2,1)S(1)}, bf16[2,128,512]{2,1,0:T(8,128)(2,1)S(1)}, u32[]{:S(2)}, u32[]{:S(2)}) collective-permute-start(bf16[2,128,512]{2,1,0:T(8,128)(2,1)S(1)} %pack.1.refs_0_), channel_id=1, source_target_pairs={{0,32},{16,48},{32,0},{48,16},{1,33},{17,49},{33,1},{49,17},{2,34}... | collective-permute-start | bytes 786440 | tf_op jit(solution)/shard_map/ppermute | solution.py:34
  24.3 0.0 collective-permute-done.5.refs_1_
  24.3 2.4 %collective-permute-start.11 = (bf16[2,128,512]{2,1,0:T(8,128)(2,1)S(1)}, bf16[2,128,512]{2,1,0:T(8,128)(2,1)S(1)}, u32[]{:S(2)}, u32[]{:S(2)}) collective-permute-start(bf16[2,128,512]{2,1,0:T(8,128)(2,1)S(1)} %pack.1.refs_0_), channel_id=1, source_target_pairs={{0,48},{16,0},{32,16},{48,32},{1,49},{17,1},{33,17},{49,33},{2,50}... | collective-permute-start | bytes 786440 | tf_op jit(solution)/shard_map/ppermute | solution.py:34
  26.7 4.7 %to_rows.1 = bf16[8,128,512]{2,1,0:T(8,128)(2,1)} custom-call(s32[3,64]{1,0:T(4,128)S(1)} %concatenate.3.own_meta, s32[3,64]{1,0:T(4,128)S(1)} %collective-permute-done.3.sib_meta, bf16[64,128,128]{2,1,0:T(8,128)(2,1)} %bitcast.33, bf16[64,128,128]{2,1,0:T(8,128)(2,1)} %copy-done.2, bf16[128,512]{1,0:T(8,128)(2,1)S(1)} %order.1.refs_0_.own, ...), custom_call_target="tpu_custom_call" | custom-call | flops 20000000000 | bytes 6291456 | tf_op jit(solution)/shard_map/to_rows/pallas_call | solution.py:160
  31.4 5.7 %all-to-all-start = ((bf16[8,128,512]{2,1,0:T(8,128)(2,1)}), bf16[8,128,512]{2,1,0:T(8,128)(2,1)S(1)}, u32[]{:S(2)}, u32[]{:S(2)}) async-start(bf16[8,128,512]{2,1,0:T(8,128)(2,1)} %to_rows.1), calls=%async_computation | async-start | bytes 2097152 | tf_op jit(solution)/shard_map/all_to_all | solution.py:249
  37.1 0.0 collective-permute-done.9.refs_1_
  37.1 3.0 %to_cols.1 = (bf16[128,512]{1,0:T(8,128)(2,1)S(1)}, bf16[128,512]{1,0:T(8,128)(2,1)S(1)}, bf16[128,512]{1,0:T(8,128)(2,1)S(1)}, bf16[128,512]{1,0:T(8,128)(2,1)S(1)}) custom-call(s32[3,64]{1,0:T(4,128)S(1)} %concatenate.3.own_meta, s32[3,64]{1,0:T(4,128)S(1)} %collective-permute-done.3.sib_meta, bf16[64,128,128]{2,1,0:T(8,128)(2,1)} %bitcast.34, ...), custom_call_target="tpu_custom_call" | custom-call | flops 20000000000 | bytes 6291456 | tf_op jit(solution)/shard_map/to_cols/pallas_call | solution.py:160
  40.1 0.0 copy-start.1
  40.1 2.3 %collective-permute-start.14 = (bf16[128,512]{1,0:T(8,128)(2,1)S(1)}, bf16[128,512]{1,0:T(8,128)(2,1)S(1)}, u32[]{:S(2)}, u32[]{:S(2)}) collective-permute-start(bf16[128,512]{1,0:T(8,128)(2,1)S(1)} %get-tuple-element.21), channel_id=1, source_target_pairs={{0,192},{64,0},{128,64},{192,128},{1,193},{65,1},{129,65},{193,129... | collective-permute-start | bytes 393224 | tf_op jit(solution)/shard_map/ppermute | solution.py:34
  42.4 1.3 %collective-permute-start.13 = (bf16[128,512]{1,0:T(8,128)(2,1)S(1)}, bf16[128,512]{1,0:T(8,128)(2,1)S(1)}, u32[]{:S(2)}, u32[]{:S(2)}) collective-permute-start(bf16[128,512]{1,0:T(8,128)(2,1)S(1)} %get-tuple-element.20), channel_id=1, source_target_pairs={{0,128},{64,192},{128,0},{192,64},{1,129},{65,193},{129,1},{193,65... | collective-permute-start | bytes 393224 | tf_op jit(solution)/shard_map/ppermute | solution.py:34
  43.7 0.2 collective-permute-start.12
  44.0 2.9 %collective-permute-done.14 = bf16[128,512]{1,0:T(8,128)(2,1)S(1)} collective-permute-done((bf16[128,512]{1,0:T(8,128)(2,1)S(1)}, bf16[128,512]{1,0:T(8,128)(2,1)S(1)}, u32[]{:S(2)}, u32[]{:S(2)}) %collective-permute-start.14) | collective-permute-done | bytes 131104 | tf_op jit(solution)/shard_map/ppermute | solution.py:34
  46.8 2.3 %collective-permute-done.13 = bf16[128,512]{1,0:T(8,128)(2,1)S(1)} collective-permute-done((bf16[128,512]{1,0:T(8,128)(2,1)S(1)}, bf16[128,512]{1,0:T(8,128)(2,1)S(1)}, u32[]{:S(2)}, u32[]{:S(2)}) %collective-permute-start.13) | collective-permute-done | bytes 131104 | tf_op jit(solution)/shard_map/ppermute | solution.py:34
  49.2 1.3 %collective-permute-done.12 = bf16[128,512]{1,0:T(8,128)(2,1)S(1)} collective-permute-done((bf16[128,512]{1,0:T(8,128)(2,1)S(1)}, bf16[128,512]{1,0:T(8,128)(2,1)S(1)}, u32[]{:S(2)}, u32[]{:S(2)}) %collective-permute-start.12) | collective-permute-done | bytes 131104 | tf_op jit(solution)/shard_map/ppermute | solution.py:34
  50.5 0.2 fusion.3
  50.7 3.2 %collective-permute-start.17 = (bf16[128,512]{1,0:T(8,128)(2,1)S(1)}, bf16[128,512]{1,0:T(8,128)(2,1)S(1)}, u32[]{:S(2)}, u32[]{:S(2)}) collective-permute-start(bf16[128,512]{1,0:T(8,128)(2,1)S(1)} %fusion.3), channel_id=1, source_target_pairs={{0,6},{2,4},{4,2},{6,0},{1,7},{3,5},{5,3},{7,1},{8,14},{10,12},{12... | collective-permute-start | bytes 393224 | tf_op jit(solution)/shard_map/ppermute | solution.py:46
  53.9 0.1 collective-permute-start.16
  54.0 3.3 %collective-permute-start.15 = (bf16[128,512]{1,0:T(8,128)(2,1)S(1)}, bf16[128,512]{1,0:T(8,128)(2,1)S(1)}, u32[]{:S(2)}, u32[]{:S(2)}) collective-permute-start(bf16[128,512]{1,0:T(8,128)(2,1)S(1)} %fusion.3), channel_id=1, source_target_pairs={{0,4},{2,6},{4,0},{6,2},{1,5},{3,7},{5,1},{7,3},{8,12},{10,14},{12... | collective-permute-start | bytes 393224 | tf_op jit(solution)/shard_map/ppermute | solution.py:46
  57.3 5.5 %collective-permute-done.17 = bf16[128,512]{1,0:T(8,128)(2,1)S(1)} collective-permute-done((bf16[128,512]{1,0:T(8,128)(2,1)S(1)}, bf16[128,512]{1,0:T(8,128)(2,1)S(1)}, u32[]{:S(2)}, u32[]{:S(2)}) %collective-permute-start.17) | collective-permute-done | bytes 131104 | tf_op jit(solution)/shard_map/ppermute | solution.py:46
  62.8 3.1 %collective-permute-done.16 = bf16[128,512]{1,0:T(8,128)(2,1)S(1)} collective-permute-done((bf16[128,512]{1,0:T(8,128)(2,1)S(1)}, bf16[128,512]{1,0:T(8,128)(2,1)S(1)}, u32[]{:S(2)}, u32[]{:S(2)}) %collective-permute-start.16) | collective-permute-done | bytes 131104 | tf_op jit(solution)/shard_map/ppermute | solution.py:46
  65.9 0.1 collective-permute-done.15
  66.0 0.1 convert_add_fusion.own_ref
  66.1 0.1 collective-permute-start.18
  66.2 0.1 constant_dynamic-slice_fusion.2
  66.3 0.1 copy.15
  66.4 0.1 copy.16
  66.5 1.2 %collective-permute-done.18.sib_ref = f32[128,512]{1,0:T(8,128)S(1)} collective-permute-done((f32[128,512]{1,0:T(8,128)S(1)}, f32[128,512]{1,0:T(8,128)S(1)}, u32[]{:S(2)}, u32[]{:S(2)}) %collective-permute-start.18) | collective-permute-done | bytes 262176 | tf_op jit(solution)/shard_map/ppermute | solution.py:34
  67.7 0.9 dense.1
  68.6 3.9 %collective-permute-done.19 = f32[32,256]{1,0:T(8,128)S(1)} collective-permute-done((f32[32,256]{1,0:T(8,128)S(1)}, f32[32,256]{1,0:T(8,128)S(1)}, u32[]{:S(2)}, u32[]{:S(2)}) %collective-permute-start.19) | collective-permute-done | bytes 32800 | tf_op jit(solution)/shard_map/ppermute | solution.py:34
  72.5 13.0 %all_to_all.10.terms = bf16[16,32,256]{2,1,0:T(8,128)(2,1)S(1)} all-to-all(bf16[16,32,256]{2,1,0:T(8,128)(2,1)S(1)} %broadcast_in_dim.16), channel_id=1, replica_groups=mesh['x'=4,'y'=4,'l'=2,'h'=4,'c'=2] {'x','y'}, dimensions={0} | all-to-all | bytes 524288 | tf_op jit(solution)/shard_map/all_to_all | solution.py:273
  85.5 0.7 finish.1
  (17 shorter events, 0.1 us)
Async XLA Ops:
  0.6 65.5 %copy-start = (bf16[256,256]{1,0:T(8,128)(2,1)S(1)}, bf16[256,256]{1,0:T(8,128)(2,1)}, u32[]{:S(2)}) copy-start(bf16[256,256]{1,0:T(8,128)(2,1)} %param.7) | copy-start | bytes 393220
  0.6 14.0 %collective-permute-start.4 = (bf16[64,128,128]{2,1,0:T(8,128)(2,1)}, bf16[64,128,128]{2,1,0:T(8,128)(2,1)S(1)}, u32[]{:S(2)}, u32[]{:S(2)}) collective-permute-start(bf16[64,128,128]{2,1,0:T(8,128)(2,1)} %bitcast.32), channel_id=1, source_target_pairs={{0,1},{1,0},{2,3},{3,2},{4,5},{5,4},{6,7},{7,6},{8,9},{9,8},{10,11... | collective-permute-start | bytes 6291464 | tf_op jit(solution)/shard_map/ppermute | solution.py:34
  0.7 13.9 %collective-permute-start = (bf16[32,512]{1,0:T(8,128)(2,1)}, bf16[32,512]{1,0:T(8,128)(2,1)S(1)}, u32[]{:S(2)}, u32[]{:S(2)}) collective-permute-start(bf16[32,512]{1,0:T(8,128)(2,1)} %param.6), channel_id=1, source_target_pairs={{0,2},{2,4},{4,6},{6,0},{1,3},{3,5},{5,7},{7,1},{8,10},{10,12},{12... | collective-permute-start | bytes 98312 | tf_op jit(solution)/shard_map/ppermute | solution.py:34
  4.1 10.6 %collective-permute-start.1 = (bf16[32,512]{1,0:T(8,128)(2,1)}, bf16[32,512]{1,0:T(8,128)(2,1)S(1)}, u32[]{:S(2)}, u32[]{:S(2)}) collective-permute-start(bf16[32,512]{1,0:T(8,128)(2,1)} %param.6), channel_id=1, source_target_pairs={{0,4},{2,6},{4,0},{6,2},{1,5},{3,7},{5,1},{7,3},{8,12},{10,14},{12... | collective-permute-start | bytes 98312 | tf_op jit(solution)/shard_map/ppermute | solution.py:34
  9.5 5.2 %collective-permute-start.2 = (bf16[32,512]{1,0:T(8,128)(2,1)}, bf16[32,512]{1,0:T(8,128)(2,1)S(1)}, u32[]{:S(2)}, u32[]{:S(2)}) collective-permute-start(bf16[32,512]{1,0:T(8,128)(2,1)} %param.6), channel_id=1, source_target_pairs={{0,6},{2,0},{4,2},{6,4},{1,7},{3,1},{5,3},{7,5},{8,14},{10,8},{12,... | collective-permute-start | bytes 98312 | tf_op jit(solution)/shard_map/ppermute | solution.py:34
  13.5 1.2 %collective-permute-start.3 = (s32[3,64]{1,0:T(4,128)S(1)}, s32[3,64]{1,0:T(4,128)S(1)}, u32[]{:S(2)}, u32[]{:S(2)}) collective-permute-start(s32[3,64]{1,0:T(4,128)S(1)} %concatenate.3.own_meta), channel_id=1, source_target_pairs={{0,1},{1,0},{2,3},{3,2},{4,5},{5,4},{6,7},{7,6},{8,9},{9,8},{10,11... | collective-permute-start | bytes 2312 | tf_op jit(solution)/shard_map/ppermute | solution.py:34
  14.7 12.1 %copy-start.2 = (bf16[64,128,128]{2,1,0:T(8,128)(2,1)}, bf16[64,128,128]{2,1,0:T(8,128)(2,1)S(1)}, u32[]{:S(2)}) copy-start(bf16[64,128,128]{2,1,0:T(8,128)(2,1)S(1)} %collective-permute-done.4.sib_tiles) | copy-start | bytes 6291460
  14.9 6.8 %collective-permute-start.8 = (bf16[128,512]{1,0:T(8,128)(2,1)S(1)}, bf16[128,512]{1,0:T(8,128)(2,1)S(1)}, u32[]{:S(2)}, u32[]{:S(2)}) collective-permute-start(bf16[128,512]{1,0:T(8,128)(2,1)S(1)} %order.1.refs_0_.own), channel_id=1, source_target_pairs={{0,8},{8,0},{1,9},{9,1},{2,10},{10,2},{3,11},{11,3},{4,12},{12,4},... | collective-permute-start | bytes 393224 | tf_op jit(solution)/shard_map/ppermute | solution.py:34
  16.0 8.3 %collective-permute-start.5 = (bf16[128,512]{1,0:T(8,128)(2,1)S(1)}, bf16[128,512]{1,0:T(8,128)(2,1)S(1)}, u32[]{:S(2)}, u32[]{:S(2)}) collective-permute-start(bf16[128,512]{1,0:T(8,128)(2,1)S(1)} %order.1.refs_0_.own), channel_id=1, source_target_pairs={{0,64},{64,128},{128,192},{192,0},{1,65},{65,129},{129,193},{193,1... | collective-permute-start | bytes 393224 | tf_op jit(solution)/shard_map/ppermute | solution.py:34
  17.5 9.2 %collective-permute-start.6 = (bf16[128,512]{1,0:T(8,128)(2,1)S(1)}, bf16[128,512]{1,0:T(8,128)(2,1)S(1)}, u32[]{:S(2)}, u32[]{:S(2)}) collective-permute-start(bf16[128,512]{1,0:T(8,128)(2,1)S(1)} %order.1.refs_0_.own), channel_id=1, source_target_pairs={{0,128},{64,192},{128,0},{192,64},{1,129},{65,193},{129,1},{193,65... | collective-permute-start | bytes 393224 | tf_op jit(solution)/shard_map/ppermute | solution.py:34
  20.2 6.5 %collective-permute-start.7 = (bf16[128,512]{1,0:T(8,128)(2,1)S(1)}, bf16[128,512]{1,0:T(8,128)(2,1)S(1)}, u32[]{:S(2)}, u32[]{:S(2)}) collective-permute-start(bf16[128,512]{1,0:T(8,128)(2,1)S(1)} %order.1.refs_0_.own), channel_id=1, source_target_pairs={{0,192},{64,0},{128,64},{192,128},{1,193},{65,1},{129,65},{193,129... | collective-permute-start | bytes 393224 | tf_op jit(solution)/shard_map/ppermute | solution.py:34
  21.7 15.4 %collective-permute-start.9 = (bf16[2,128,512]{2,1,0:T(8,128)(2,1)S(1)}, bf16[2,128,512]{2,1,0:T(8,128)(2,1)S(1)}, u32[]{:S(2)}, u32[]{:S(2)}) collective-permute-start(bf16[2,128,512]{2,1,0:T(8,128)(2,1)S(1)} %pack.1.refs_0_), channel_id=1, source_target_pairs={{0,16},{16,32},{32,48},{48,0},{1,17},{17,33},{33,49},{49,1},{2,18}... | collective-permute-start | bytes 786440 | tf_op jit(solution)/shard_map/ppermute | solution.py:34
  23.4 13.7 %collective-permute-start.10 = (bf16[2,128,512]{2,1,0:T(8,128)(2,1)S(1)}, bf16[2,128,512]{2,1,0:T(8,128)(2,1)S(1)}, u32[]{:S(2)}, u32[]{:S(2)}) collective-permute-start(bf16[2,128,512]{2,1,0:T(8,128)(2,1)S(1)} %pack.1.refs_0_), channel_id=1, source_target_pairs={{0,32},{16,48},{32,0},{48,16},{1,33},{17,49},{33,1},{49,17},{2,34}... | collective-permute-start | bytes 786440 | tf_op jit(solution)/shard_map/ppermute | solution.py:34
  24.3 12.8 %collective-permute-start.11 = (bf16[2,128,512]{2,1,0:T(8,128)(2,1)S(1)}, bf16[2,128,512]{2,1,0:T(8,128)(2,1)S(1)}, u32[]{:S(2)}, u32[]{:S(2)}) collective-permute-start(bf16[2,128,512]{2,1,0:T(8,128)(2,1)S(1)} %pack.1.refs_0_), channel_id=1, source_target_pairs={{0,48},{16,0},{32,16},{48,32},{1,49},{17,1},{33,17},{49,33},{2,50}... | collective-permute-start | bytes 786440 | tf_op jit(solution)/shard_map/ppermute | solution.py:34
  31.4 19.1 %all-to-all-start = ((bf16[8,128,512]{2,1,0:T(8,128)(2,1)}), bf16[8,128,512]{2,1,0:T(8,128)(2,1)S(1)}, u32[]{:S(2)}, u32[]{:S(2)}) async-start(bf16[8,128,512]{2,1,0:T(8,128)(2,1)} %to_rows.1), calls=%async_computation | async-start | bytes 2097152 | tf_op jit(solution)/shard_map/all_to_all | solution.py:249
  40.1 27.6 %copy-start.1 = (bf16[32,512]{1,0:T(8,128)(2,1)S(1)}, bf16[32,512]{1,0:T(8,128)(2,1)}, u32[]{:S(2)}) copy-start(bf16[32,512]{1,0:T(8,128)(2,1)} %cotangent.1) | copy-start | bytes 98308
  40.1 6.8 %collective-permute-start.14 = (bf16[128,512]{1,0:T(8,128)(2,1)S(1)}, bf16[128,512]{1,0:T(8,128)(2,1)S(1)}, u32[]{:S(2)}, u32[]{:S(2)}) collective-permute-start(bf16[128,512]{1,0:T(8,128)(2,1)S(1)} %get-tuple-element.21), channel_id=1, source_target_pairs={{0,192},{64,0},{128,64},{192,128},{1,193},{65,1},{129,65},{193,129... | collective-permute-start | bytes 393224 | tf_op jit(solution)/shard_map/ppermute | solution.py:34
  42.4 6.8 %collective-permute-start.13 = (bf16[128,512]{1,0:T(8,128)(2,1)S(1)}, bf16[128,512]{1,0:T(8,128)(2,1)S(1)}, u32[]{:S(2)}, u32[]{:S(2)}) collective-permute-start(bf16[128,512]{1,0:T(8,128)(2,1)S(1)} %get-tuple-element.20), channel_id=1, source_target_pairs={{0,128},{64,192},{128,0},{192,64},{1,129},{65,193},{129,1},{193,65... | collective-permute-start | bytes 393224 | tf_op jit(solution)/shard_map/ppermute | solution.py:34
  43.7 6.8 %collective-permute-start.12 = (bf16[128,512]{1,0:T(8,128)(2,1)S(1)}, bf16[128,512]{1,0:T(8,128)(2,1)S(1)}, u32[]{:S(2)}, u32[]{:S(2)}) collective-permute-start(bf16[128,512]{1,0:T(8,128)(2,1)S(1)} %get-tuple-element.19), channel_id=1, source_target_pairs={{0,64},{64,128},{128,192},{192,0},{1,65},{65,129},{129,193},{193,1... | collective-permute-start | bytes 393224 | tf_op jit(solution)/shard_map/ppermute | solution.py:34
  50.7 12.1 %collective-permute-start.17 = (bf16[128,512]{1,0:T(8,128)(2,1)S(1)}, bf16[128,512]{1,0:T(8,128)(2,1)S(1)}, u32[]{:S(2)}, u32[]{:S(2)}) collective-permute-start(bf16[128,512]{1,0:T(8,128)(2,1)S(1)} %fusion.3), channel_id=1, source_target_pairs={{0,6},{2,4},{4,2},{6,0},{1,7},{3,5},{5,3},{7,1},{8,14},{10,12},{12... | collective-permute-start | bytes 393224 | tf_op jit(solution)/shard_map/ppermute | solution.py:46
  53.9 12.0 %collective-permute-start.16 = (bf16[128,512]{1,0:T(8,128)(2,1)S(1)}, bf16[128,512]{1,0:T(8,128)(2,1)S(1)}, u32[]{:S(2)}, u32[]{:S(2)}) collective-permute-start(bf16[128,512]{1,0:T(8,128)(2,1)S(1)} %fusion.3), channel_id=1, source_target_pairs={{0,2},{2,0},{4,6},{6,4},{1,3},{3,1},{5,7},{7,5},{8,10},{10,8},{12,... | collective-permute-start | bytes 393224 | tf_op jit(solution)/shard_map/ppermute | solution.py:46
  54.0 12.0 %collective-permute-start.15 = (bf16[128,512]{1,0:T(8,128)(2,1)S(1)}, bf16[128,512]{1,0:T(8,128)(2,1)S(1)}, u32[]{:S(2)}, u32[]{:S(2)}) collective-permute-start(bf16[128,512]{1,0:T(8,128)(2,1)S(1)} %fusion.3), channel_id=1, source_target_pairs={{0,4},{2,6},{4,0},{6,2},{1,5},{3,7},{5,1},{7,3},{8,12},{10,14},{12... | collective-permute-start | bytes 393224 | tf_op jit(solution)/shard_map/ppermute | solution.py:46
  66.1 1.6 %collective-permute-start.18 = (f32[128,512]{1,0:T(8,128)S(1)}, f32[128,512]{1,0:T(8,128)S(1)}, u32[]{:S(2)}, u32[]{:S(2)}) collective-permute-start(f32[128,512]{1,0:T(8,128)S(1)} %convert_add_fusion.own_ref), channel_id=1, source_target_pairs={{0,1},{1,0},{2,3},{3,2},{4,5},{5,4},{6,7},{7,6},{8,9},{9,8},{10,11... | collective-permute-start | bytes 786440 | tf_op jit(solution)/shard_map/ppermute | solution.py:34
  68.5 3.9 %collective-permute-start.19 = (f32[32,256]{1,0:T(8,128)S(1)}, f32[32,256]{1,0:T(8,128)S(1)}, u32[]{:S(2)}, u32[]{:S(2)}) collective-permute-start(f32[32,256]{1,0:T(8,128)S(1)} %get-tuple-element.23), channel_id=1, source_target_pairs={{0,8},{8,0},{1,9},{9,1},{2,10},{10,2},{3,11},{11,3},{4,12},{12,4},... | collective-permute-start | bytes 98312 | tf_op jit(solution)/shard_map/ppermute | solution.py:34

commit v5 on v4

--- a/solution.py
+++ b/solution.py
@@ -175,41 +175,33 @@
     return high, low
 
 
-def dense_kernel(own_ref, sib_ref, weight_own, weight_sib, cotangent, activation, grads):
-    own = split(own_ref[...])
-    sib = split(sib_ref[...])
-    preact = 0.0
-    for weight, field in ((weight_own[...], own), (weight_sib[...], sib)):
-        for part in field[::-1]:
-            preact += jnp.dot(weight, part, preferred_element_type=jnp.float32)
+def dense_kernel(own_ref, sib_ref, weight, cotangent, activation, grads, field):
+    place = lax.axis_index("c")
+    for core, ref in ((place, own_ref), (1 - place, sib_ref)):
+        for step in range(4):
+            rows = pl.ds(pl.multiple_of(step * 64 + core * 32, 32), 32)
+            field[rows, :] = ref[step * 32 : (step + 1) * 32, :]
+    high, low = split(field[...])
+    preact = jnp.dot(weight[...], low, preferred_element_type=jnp.float32)
+    preact += jnp.dot(weight[...], high, preferred_element_type=jnp.float32)
     sigmoid = jax.nn.sigmoid(preact)
     activation[...] = (preact * sigmoid).astype(jnp.bfloat16)
     slope = (
         cotangent[...].astype(jnp.float32) * sigmoid * (1.0 + preact * (1.0 - sigmoid))
     ).astype(jnp.bfloat16)
-    for side, field in enumerate((own, sib)):
-        total = 0.0
-        for part in field[::-1]:
-            total += lax.dot_general(
-                slope, part, (((1,), (1,)), ((), ())), preferred_element_type=jnp.float32
-            )
-        grads[:, side * HALF : (side + 1) * HALF] = total
+    total = 0.0
+    for part in (low, high):
+        total += lax.dot_general(
+            slope, part, (((1,), (1,)), ((), ())), preferred_element_type=jnp.float32
+        )
+    grads[...] = total
 
 
 def finish_kernel(terms, grad):
-    place = lax.axis_index("c")
     total = terms[0].astype(jnp.float32)
     for turn in range(1, terms.shape[0]):
         total += terms[turn].astype(jnp.float32)
-    sides = [
-        [total[:, side * HALF + step * 32 : side * HALF + (step + 1) * 32] for step in range(4)]
-        for side in range(2)
-    ]
-    first, second = (
-        jnp.concatenate([sides[(side + core) % 2][step] for step in range(4) for side in range(2)], 1)
-        for core in range(2)
-    )
-    grad[...] = jnp.where(place == 0, first, second)
+    grad[...] = total
 
 
 def body(features, weight, tiles, pairs, counts, cotangent):
@@ -253,21 +245,19 @@
     total = sum(v.astype(jnp.float32) for v in [share] + swaps(share, "h"))
     sib_total = shifted(total, "c", 1)
 
-    weight_mine = lax.dynamic_slice_in_dim(weight, (at_h * 2 + at_c) * 32, 32, 1)
-    weight_mine = weight_mine.reshape(4, 2, 32, 32)
-    weight_own = lax.dynamic_index_in_dim(weight_mine, at_c, 1, False).reshape(HALF, 32).T
-    weight_sib = lax.dynamic_index_in_dim(weight_mine, 1 - at_c, 1, False).reshape(HALF, 32).T
+    weight_mine = lax.dynamic_slice_in_dim(weight, (at_h * 2 + at_c) * 32, 32, 1).T
     activation, grads = pl.pallas_call(
         dense_kernel,
         out_shape=[
             jax.ShapeDtypeStruct((32, NODE_DEV), jnp.bfloat16),
             jax.ShapeDtypeStruct((32, FEAT), jnp.float32),
         ],
-        in_specs=[VMEM] * 5,
+        in_specs=[VMEM] * 4,
         out_specs=[VMEM] * 2,
+        scratch_shapes=[pltpu.VMEM((FEAT, NODE_DEV), jnp.float32)],
         compiler_params=limit(16),
         name="dense",
-    )(total, sib_total, weight_own, weight_sib, cotangent)
+    )(total, sib_total, weight_mine, cotangent)
     pair = (grads + shifted(grads, "l", 1)).astype(jnp.bfloat16)
     many = jnp.broadcast_to(pair[None], (16, 32, FEAT))
     terms = lax.all_to_all(many, ("x", "y"), 0, 0, tiled=True)

time: 86.3 us -> 86.3 us (level)
  no operation moved by 1% of the time
where the time goes in v5:
time: 86.3 us; the launch traced here: 86 us
  starting transfers between devices  39.1 us (45%)
  waiting for transfers between devices  21.3 us (25%)
  blocking collectives  12.8 us (15%)
  Pallas kernels  9.46 us (11%)
  between operations  1.43 us (2%)
  other arithmetic  1.04 us (1%)
  local copies, waits for them, and re-layouts  0.89 us (1%)
    ppermute x17, starting transfers between devices, shifted(): lax.ppermute(value, axis, [(i, (i + step) % total) for i in range(total)])  26.7 us
    all_to_all x1, blocking collectives, body(): terms = lax.all_to_all(many, ('x', 'y'), 0, 0, tiled=True)  12.8 us
    ppermute x17, waiting for transfers between devices, shifted(): lax.ppermute(value, axis, [(i, (i + step) % total) for i in range(total)])  12.7 us
    ppermute x3, waiting for transfers between devices, swaps(): lax.ppermute(value, axis, [(i, i ^ bits) for i in range(4)])  8.69 us
    pallas_call x2, Pallas kernels, agg(): pl.pallas_call(functools.partial(agg_kernel, to_rows), out_shape=out_shap...  7.62 us
    ppermute x3, starting transfers between devices, swaps(): lax.ppermute(value, axis, [(i, i ^ bits) for i in range(4)])  6.58 us
    all_to_all x1, starting transfers between devices, body(): row_got = list(lax.all_to_all(row_part, ('y', 'l'), 0, 0, tiled=True))  5.82 us
  transfers between devices with their start and end apart: 21, of which 9 were waited for; matrix products, arithmetic and copies ran while one was open for 2% of the time, Pallas kernels for 9%

profile of v5, /device:TPU:8, one launch (start us, length us, event | category | flops | bytes accessed | tf_op | source)
XLA Modules:
  0.0 86.0 jit_solution(13364184555299977)
XLA Ops:
  0.6 0.0 copy-start
  0.6 0.1 collective-permute-start.4
  0.7 3.3 %collective-permute-start = (bf16[32,512]{1,0:T(8,128)(2,1)}, bf16[32,512]{1,0:T(8,128)(2,1)S(1)}, u32[]{:S(2)}, u32[]{:S(2)}) collective-permute-start(bf16[32,512]{1,0:T(8,128)(2,1)} %param.6), channel_id=1, source_target_pairs={{0,2},{2,4},{4,6},{6,0},{1,3},{3,5},{5,7},{7,1},{8,10},{10,12},{12... | collective-permute-start | bytes 98312 | tf_op jit(solution)/shard_map/ppermute | solution.py:34
  4.1 5.4 %collective-permute-start.1 = (bf16[32,512]{1,0:T(8,128)(2,1)}, bf16[32,512]{1,0:T(8,128)(2,1)S(1)}, u32[]{:S(2)}, u32[]{:S(2)}) collective-permute-start(bf16[32,512]{1,0:T(8,128)(2,1)} %param.6), channel_id=1, source_target_pairs={{0,4},{2,6},{4,0},{6,2},{1,5},{3,7},{5,1},{7,3},{8,12},{10,14},{12... | collective-permute-start | bytes 98312 | tf_op jit(solution)/shard_map/ppermute | solution.py:34
  9.5 2.7 %collective-permute-start.2 = (bf16[32,512]{1,0:T(8,128)(2,1)}, bf16[32,512]{1,0:T(8,128)(2,1)S(1)}, u32[]{:S(2)}, u32[]{:S(2)}) collective-permute-start(bf16[32,512]{1,0:T(8,128)(2,1)} %param.6), channel_id=1, source_target_pairs={{0,6},{2,0},{4,2},{6,4},{1,7},{3,1},{5,3},{7,5},{8,14},{10,8},{12,... | collective-permute-start | bytes 98312 | tf_op jit(solution)/shard_map/ppermute | solution.py:34
  12.8 0.7 concatenate.3.own_meta
  13.5 0.0 collective-permute-start.3
  13.5 0.8 broadcast_select_fusion.own
  14.3 0.4 collective-permute-done.3.sib_meta
  14.6 0.0 collective-permute-done.r1
  14.7 0.0 collective-permute-done.1.r2
  14.7 0.0 collective-permute-done.2.r3
  14.7 0.0 collective-permute-done.4.sib_tiles
  14.7 0.2 order.1.refs_0_.own
  14.9 1.1 %collective-permute-start.8 = (bf16[128,512]{1,0:T(8,128)(2,1)S(1)}, bf16[128,512]{1,0:T(8,128)(2,1)S(1)}, u32[]{:S(2)}, u32[]{:S(2)}) collective-permute-start(bf16[128,512]{1,0:T(8,128)(2,1)S(1)} %order.1.refs_0_.own), channel_id=1, source_target_pairs={{0,8},{8,0},{1,9},{9,1},{2,10},{10,2},{3,11},{11,3},{4,12},{12,4},... | collective-permute-start | bytes 393224 | tf_op jit(solution)/shard_map/ppermute | solution.py:34
  16.0 1.5 %collective-permute-start.5 = (bf16[128,512]{1,0:T(8,128)(2,1)S(1)}, bf16[128,512]{1,0:T(8,128)(2,1)S(1)}, u32[]{:S(2)}, u32[]{:S(2)}) collective-permute-start(bf16[128,512]{1,0:T(8,128)(2,1)S(1)} %order.1.refs_0_.own), channel_id=1, source_target_pairs={{0,64},{64,128},{128,192},{192,0},{1,65},{65,129},{129,193},{193,1... | collective-permute-start | bytes 393224 | tf_op jit(solution)/shard_map/ppermute | solution.py:34
  17.5 2.7 %collective-permute-start.6 = (bf16[128,512]{1,0:T(8,128)(2,1)S(1)}, bf16[128,512]{1,0:T(8,128)(2,1)S(1)}, u32[]{:S(2)}, u32[]{:S(2)}) collective-permute-start(bf16[128,512]{1,0:T(8,128)(2,1)S(1)} %order.1.refs_0_.own), channel_id=1, source_target_pairs={{0,128},{64,192},{128,0},{192,64},{1,129},{65,193},{129,1},{193,65... | collective-permute-start | bytes 393224 | tf_op jit(solution)/shard_map/ppermute | solution.py:34
  20.2 1.4 %collective-permute-start.7 = (bf16[128,512]{1,0:T(8,128)(2,1)S(1)}, bf16[128,512]{1,0:T(8,128)(2,1)S(1)}, u32[]{:S(2)}, u32[]{:S(2)}) collective-permute-start(bf16[128,512]{1,0:T(8,128)(2,1)S(1)} %order.1.refs_0_.own), channel_id=1, source_target_pairs={{0,192},{64,0},{128,64},{192,128},{1,193},{65,1},{129,65},{193,129... | collective-permute-start | bytes 393224 | tf_op jit(solution)/shard_map/ppermute | solution.py:34
  21.7 1.7 %collective-permute-start.9 = (bf16[2,128,512]{2,1,0:T(8,128)(2,1)S(1)}, bf16[2,128,512]{2,1,0:T(8,128)(2,1)S(1)}, u32[]{:S(2)}, u32[]{:S(2)}) collective-permute-start(bf16[2,128,512]{2,1,0:T(8,128)(2,1)S(1)} %pack.1.refs_0_), channel_id=1, source_target_pairs={{0,16},{16,32},{32,48},{48,0},{1,17},{17,33},{33,49},{49,1},{2,18}... | collective-permute-start | bytes 786440 | tf_op jit(solution)/shard_map/ppermute | solution.py:34
  23.4 0.9 %collective-permute-start.10 = (bf16[2,128,512]{2,1,0:T(8,128)(2,1)S(1)}, bf16[2,128,512]{2,1,0:T(8,128)(2,1)S(1)}, u32[]{:S(2)}, u32[]{:S(2)}) collective-permute-start(bf16[2,128,512]{2,1,0:T(8,128)(2,1)S(1)} %pack.1.refs_0_), channel_id=1, source_target_pairs={{0,32},{16,48},{32,0},{48,16},{1,33},{17,49},{33,1},{49,17},{2,34}... | collective-permute-start | bytes 786440 | tf_op jit(solution)/shard_map/ppermute | solution.py:34
  24.3 2.4 %collective-permute-start.11 = (bf16[2,128,512]{2,1,0:T(8,128)(2,1)S(1)}, bf16[2,128,512]{2,1,0:T(8,128)(2,1)S(1)}, u32[]{:S(2)}, u32[]{:S(2)}) collective-permute-start(bf16[2,128,512]{2,1,0:T(8,128)(2,1)S(1)} %pack.1.refs_0_), channel_id=1, source_target_pairs={{0,48},{16,0},{32,16},{48,32},{1,49},{17,1},{33,17},{49,33},{2,50}... | collective-permute-start | bytes 786440 | tf_op jit(solution)/shard_map/ppermute | solution.py:34
  26.7 0.0 collective-permute-done.6.refs_2_
  26.7 4.6 %to_rows.1 = bf16[8,128,512]{2,1,0:T(8,128)(2,1)} custom-call(s32[3,64]{1,0:T(4,128)S(1)} %concatenate.3.own_meta, s32[3,64]{1,0:T(4,128)S(1)} %collective-permute-done.3.sib_meta, bf16[64,128,128]{2,1,0:T(8,128)(2,1)} %bitcast.21, bf16[64,128,128]{2,1,0:T(8,128)(2,1)} %copy-done.2, bf16[128,512]{1,0:T(8,128)(2,1)S(1)} %order.1.refs_0_.own, ...), custom_call_target="tpu_custom_call" | custom-call | flops 20000000000 | bytes 6291456 | tf_op jit(solution)/shard_map/to_rows/pallas_call | solution.py:160
  31.4 5.8 %all-to-all-start = ((bf16[8,128,512]{2,1,0:T(8,128)(2,1)}), bf16[8,128,512]{2,1,0:T(8,128)(2,1)S(1)}, u32[]{:S(2)}, u32[]{:S(2)}) async-start(bf16[8,128,512]{2,1,0:T(8,128)(2,1)} %to_rows.1), calls=%async_computation | async-start | bytes 2097152 | tf_op jit(solution)/shard_map/all_to_all | solution.py:241
  37.2 3.0 %to_cols.1 = (bf16[128,512]{1,0:T(8,128)(2,1)S(1)}, bf16[128,512]{1,0:T(8,128)(2,1)S(1)}, bf16[128,512]{1,0:T(8,128)(2,1)S(1)}, bf16[128,512]{1,0:T(8,128)(2,1)S(1)}) custom-call(s32[3,64]{1,0:T(4,128)S(1)} %concatenate.3.own_meta, s32[3,64]{1,0:T(4,128)S(1)} %collective-permute-done.3.sib_meta, bf16[64,128,128]{2,1,0:T(8,128)(2,1)} %bitcast.22, ...), custom_call_target="tpu_custom_call" | custom-call | flops 20000000000 | bytes 6291456 | tf_op jit(solution)/shard_map/to_cols/pallas_call | solution.py:160
  40.2 0.0 copy-start.1
  40.2 2.2 %collective-permute-start.14 = (bf16[128,512]{1,0:T(8,128)(2,1)S(1)}, bf16[128,512]{1,0:T(8,128)(2,1)S(1)}, u32[]{:S(2)}, u32[]{:S(2)}) collective-permute-start(bf16[128,512]{1,0:T(8,128)(2,1)S(1)} %get-tuple-element.21), channel_id=1, source_target_pairs={{0,192},{64,0},{128,64},{192,128},{1,193},{65,1},{129,65},{193,129... | collective-permute-start | bytes 393224 | tf_op jit(solution)/shard_map/ppermute | solution.py:34
  42.4 0.5 collective-permute-start.13
  42.9 0.7 collective-permute-start.12
  43.5 3.3 %collective-permute-done.14 = bf16[128,512]{1,0:T(8,128)(2,1)S(1)} collective-permute-done((bf16[128,512]{1,0:T(8,128)(2,1)S(1)}, bf16[128,512]{1,0:T(8,128)(2,1)S(1)}, u32[]{:S(2)}, u32[]{:S(2)}) %collective-permute-start.14) | collective-permute-done | bytes 131104 | tf_op jit(solution)/shard_map/ppermute | solution.py:34
  46.8 2.4 %collective-permute-done.13 = bf16[128,512]{1,0:T(8,128)(2,1)S(1)} collective-permute-done((bf16[128,512]{1,0:T(8,128)(2,1)S(1)}, bf16[128,512]{1,0:T(8,128)(2,1)S(1)}, u32[]{:S(2)}, u32[]{:S(2)}) %collective-permute-start.13) | collective-permute-done | bytes 131104 | tf_op jit(solution)/shard_map/ppermute | solution.py:34
  49.2 1.3 %collective-permute-done.12 = bf16[128,512]{1,0:T(8,128)(2,1)S(1)} collective-permute-done((bf16[128,512]{1,0:T(8,128)(2,1)S(1)}, bf16[128,512]{1,0:T(8,128)(2,1)S(1)}, u32[]{:S(2)}, u32[]{:S(2)}) %collective-permute-start.12) | collective-permute-done | bytes 131104 | tf_op jit(solution)/shard_map/ppermute | solution.py:34
  50.5 0.2 fusion.3
  50.7 2.8 %collective-permute-start.17 = (bf16[128,512]{1,0:T(8,128)(2,1)S(1)}, bf16[128,512]{1,0:T(8,128)(2,1)S(1)}, u32[]{:S(2)}, u32[]{:S(2)}) collective-permute-start(bf16[128,512]{1,0:T(8,128)(2,1)S(1)} %fusion.3), channel_id=1, source_target_pairs={{0,6},{2,4},{4,2},{6,0},{1,7},{3,5},{5,3},{7,1},{8,14},{10,12},{12... | collective-permute-start | bytes 393224 | tf_op jit(solution)/shard_map/ppermute | solution.py:46
  53.5 0.4 collective-permute-start.16
  53.9 3.4 %collective-permute-start.15 = (bf16[128,512]{1,0:T(8,128)(2,1)S(1)}, bf16[128,512]{1,0:T(8,128)(2,1)S(1)}, u32[]{:S(2)}, u32[]{:S(2)}) collective-permute-start(bf16[128,512]{1,0:T(8,128)(2,1)S(1)} %fusion.3), channel_id=1, source_target_pairs={{0,4},{2,6},{4,0},{6,2},{1,5},{3,7},{5,1},{7,3},{8,12},{10,14},{12... | collective-permute-start | bytes 393224 | tf_op jit(solution)/shard_map/ppermute | solution.py:46
  57.3 4.8 %collective-permute-done.17 = bf16[128,512]{1,0:T(8,128)(2,1)S(1)} collective-permute-done((bf16[128,512]{1,0:T(8,128)(2,1)S(1)}, bf16[128,512]{1,0:T(8,128)(2,1)S(1)}, u32[]{:S(2)}, u32[]{:S(2)}) %collective-permute-start.17) | collective-permute-done | bytes 131104 | tf_op jit(solution)/shard_map/ppermute | solution.py:46
  62.2 3.6 %collective-permute-done.16 = bf16[128,512]{1,0:T(8,128)(2,1)S(1)} collective-permute-done((bf16[128,512]{1,0:T(8,128)(2,1)S(1)}, bf16[128,512]{1,0:T(8,128)(2,1)S(1)}, u32[]{:S(2)}, u32[]{:S(2)}) %collective-permute-start.16) | collective-permute-done | bytes 131104 | tf_op jit(solution)/shard_map/ppermute | solution.py:46
  65.8 0.2 collective-permute-done.15
  66.0 0.1 convert_add_fusion.own_ref
  66.1 0.1 collective-permute-start.18
  66.2 0.1 constant_dynamic-slice_fusion
  66.3 0.1 copy.9
  66.4 1.3 %collective-permute-done.18.sib_ref = f32[128,512]{1,0:T(8,128)S(1)} collective-permute-done((f32[128,512]{1,0:T(8,128)S(1)}, f32[128,512]{1,0:T(8,128)S(1)}, u32[]{:S(2)}, u32[]{:S(2)}) %collective-permute-start.18) | collective-permute-done | bytes 262176 | tf_op jit(solution)/shard_map/ppermute | solution.py:34
  67.7 0.9 %dense.1 = (bf16[32,512]{1,0:T(8,128)(2,1)}, f32[32,256]{1,0:T(8,128)S(1)}) custom-call(f32[128,512]{1,0:T(8,128)S(1)} %convert_add_fusion.own_ref, f32[128,512]{1,0:T(8,128)S(1)} %collective-permute-done.18.sib_ref, bf16[32,256]{1,0:T(8,128)(2,1)S(1)} %bitcast.17, bf16[32,512]{1,0:T(8,128)(2,1)S(1)} %copy-done.1), custom_call_target="tpu_custom_call" | custom-call | tf_op jit(solution)/shard_map/dense/pallas_call | solution.py:249
  68.6 3.9 %collective-permute-done.19 = f32[32,256]{1,0:T(8,128)S(1)} collective-permute-done((f32[32,256]{1,0:T(8,128)S(1)}, f32[32,256]{1,0:T(8,128)S(1)}, u32[]{:S(2)}, u32[]{:S(2)}) %collective-permute-start.19) | collective-permute-done | bytes 32800 | tf_op jit(solution)/shard_map/ppermute | solution.py:34
  72.6 12.8 %all_to_all.10.terms = bf16[16,32,256]{2,1,0:T(8,128)(2,1)S(1)} all-to-all(bf16[16,32,256]{2,1,0:T(8,128)(2,1)S(1)} %broadcast_in_dim.16), channel_id=1, replica_groups=mesh['x'=4,'y'=4,'l'=2,'h'=4,'c'=2] {'x','y'}, dimensions={0} | all-to-all | bytes 524288 | tf_op jit(solution)/shard_map/all_to_all | solution.py:263
  85.3 0.7 finish.1
  (15 shorter events, 0.1 us)
Async XLA Ops:
  0.6 65.6 %copy-start = (bf16[256,256]{1,0:T(8,128)(2,1)S(1)}, bf16[256,256]{1,0:T(8,128)(2,1)}, u32[]{:S(2)}) copy-start(bf16[256,256]{1,0:T(8,128)(2,1)} %param.7) | copy-start | bytes 393220
  0.6 14.0 %collective-permute-start.4 = (bf16[64,128,128]{2,1,0:T(8,128)(2,1)}, bf16[64,128,128]{2,1,0:T(8,128)(2,1)S(1)}, u32[]{:S(2)}, u32[]{:S(2)}) collective-permute-start(bf16[64,128,128]{2,1,0:T(8,128)(2,1)} %bitcast.20), channel_id=1, source_target_pairs={{0,1},{1,0},{2,3},{3,2},{4,5},{5,4},{6,7},{7,6},{8,9},{9,8},{10,11... | collective-permute-start | bytes 6291464 | tf_op jit(solution)/shard_map/ppermute | solution.py:34
  0.7 13.9 %collective-permute-start = (bf16[32,512]{1,0:T(8,128)(2,1)}, bf16[32,512]{1,0:T(8,128)(2,1)S(1)}, u32[]{:S(2)}, u32[]{:S(2)}) collective-permute-start(bf16[32,512]{1,0:T(8,128)(2,1)} %param.6), channel_id=1, source_target_pairs={{0,2},{2,4},{4,6},{6,0},{1,3},{3,5},{5,7},{7,1},{8,10},{10,12},{12... | collective-permute-start | bytes 98312 | tf_op jit(solution)/shard_map/ppermute | solution.py:34
  4.1 10.6 %collective-permute-start.1 = (bf16[32,512]{1,0:T(8,128)(2,1)}, bf16[32,512]{1,0:T(8,128)(2,1)S(1)}, u32[]{:S(2)}, u32[]{:S(2)}) collective-permute-start(bf16[32,512]{1,0:T(8,128)(2,1)} %param.6), channel_id=1, source_target_pairs={{0,4},{2,6},{4,0},{6,2},{1,5},{3,7},{5,1},{7,3},{8,12},{10,14},{12... | collective-permute-start | bytes 98312 | tf_op jit(solution)/shard_map/ppermute | solution.py:34
  9.5 5.2 %collective-permute-start.2 = (bf16[32,512]{1,0:T(8,128)(2,1)}, bf16[32,512]{1,0:T(8,128)(2,1)S(1)}, u32[]{:S(2)}, u32[]{:S(2)}) collective-permute-start(bf16[32,512]{1,0:T(8,128)(2,1)} %param.6), channel_id=1, source_target_pairs={{0,6},{2,0},{4,2},{6,4},{1,7},{3,1},{5,3},{7,5},{8,14},{10,8},{12,... | collective-permute-start | bytes 98312 | tf_op jit(solution)/shard_map/ppermute | solution.py:34
  13.5 1.2 %collective-permute-start.3 = (s32[3,64]{1,0:T(4,128)S(1)}, s32[3,64]{1,0:T(4,128)S(1)}, u32[]{:S(2)}, u32[]{:S(2)}) collective-permute-start(s32[3,64]{1,0:T(4,128)S(1)} %concatenate.3.own_meta), channel_id=1, source_target_pairs={{0,1},{1,0},{2,3},{3,2},{4,5},{5,4},{6,7},{7,6},{8,9},{9,8},{10,11... | collective-permute-start | bytes 2312 | tf_op jit(solution)/shard_map/ppermute | solution.py:34
  14.7 12.1 %copy-start.2 = (bf16[64,128,128]{2,1,0:T(8,128)(2,1)}, bf16[64,128,128]{2,1,0:T(8,128)(2,1)S(1)}, u32[]{:S(2)}) copy-start(bf16[64,128,128]{2,1,0:T(8,128)(2,1)S(1)} %collective-permute-done.4.sib_tiles) | copy-start | bytes 6291460
  14.9 6.8 %collective-permute-start.8 = (bf16[128,512]{1,0:T(8,128)(2,1)S(1)}, bf16[128,512]{1,0:T(8,128)(2,1)S(1)}, u32[]{:S(2)}, u32[]{:S(2)}) collective-permute-start(bf16[128,512]{1,0:T(8,128)(2,1)S(1)} %order.1.refs_0_.own), channel_id=1, source_target_pairs={{0,8},{8,0},{1,9},{9,1},{2,10},{10,2},{3,11},{11,3},{4,12},{12,4},... | collective-permute-start | bytes 393224 | tf_op jit(solution)/shard_map/ppermute | solution.py:34
  16.0 8.3 %collective-permute-start.5 = (bf16[128,512]{1,0:T(8,128)(2,1)S(1)}, bf16[128,512]{1,0:T(8,128)(2,1)S(1)}, u32[]{:S(2)}, u32[]{:S(2)}) collective-permute-start(bf16[128,512]{1,0:T(8,128)(2,1)S(1)} %order.1.refs_0_.own), channel_id=1, source_target_pairs={{0,64},{64,128},{128,192},{192,0},{1,65},{65,129},{129,193},{193,1... | collective-permute-start | bytes 393224 | tf_op jit(solution)/shard_map/ppermute | solution.py:34
  17.5 9.2 %collective-permute-start.6 = (bf16[128,512]{1,0:T(8,128)(2,1)S(1)}, bf16[128,512]{1,0:T(8,128)(2,1)S(1)}, u32[]{:S(2)}, u32[]{:S(2)}) collective-permute-start(bf16[128,512]{1,0:T(8,128)(2,1)S(1)} %order.1.refs_0_.own), channel_id=1, source_target_pairs={{0,128},{64,192},{128,0},{192,64},{1,129},{65,193},{129,1},{193,65... | collective-permute-start | bytes 393224 | tf_op jit(solution)/shard_map/ppermute | solution.py:34
  20.2 6.5 %collective-permute-start.7 = (bf16[128,512]{1,0:T(8,128)(2,1)S(1)}, bf16[128,512]{1,0:T(8,128)(2,1)S(1)}, u32[]{:S(2)}, u32[]{:S(2)}) collective-permute-start(bf16[128,512]{1,0:T(8,128)(2,1)S(1)} %order.1.refs_0_.own), channel_id=1, source_target_pairs={{0,192},{64,0},{128,64},{192,128},{1,193},{65,1},{129,65},{193,129... | collective-permute-start | bytes 393224 | tf_op jit(solution)/shard_map/ppermute | solution.py:34
  21.7 15.5 %collective-permute-start.9 = (bf16[2,128,512]{2,1,0:T(8,128)(2,1)S(1)}, bf16[2,128,512]{2,1,0:T(8,128)(2,1)S(1)}, u32[]{:S(2)}, u32[]{:S(2)}) collective-permute-start(bf16[2,128,512]{2,1,0:T(8,128)(2,1)S(1)} %pack.1.refs_0_), channel_id=1, source_target_pairs={{0,16},{16,32},{32,48},{48,0},{1,17},{17,33},{33,49},{49,1},{2,18}... | collective-permute-start | bytes 786440 | tf_op jit(solution)/shard_map/ppermute | solution.py:34
  23.4 13.8 %collective-permute-start.10 = (bf16[2,128,512]{2,1,0:T(8,128)(2,1)S(1)}, bf16[2,128,512]{2,1,0:T(8,128)(2,1)S(1)}, u32[]{:S(2)}, u32[]{:S(2)}) collective-permute-start(bf16[2,128,512]{2,1,0:T(8,128)(2,1)S(1)} %pack.1.refs_0_), channel_id=1, source_target_pairs={{0,32},{16,48},{32,0},{48,16},{1,33},{17,49},{33,1},{49,17},{2,34}... | collective-permute-start | bytes 786440 | tf_op jit(solution)/shard_map/ppermute | solution.py:34
  24.3 12.9 %collective-permute-start.11 = (bf16[2,128,512]{2,1,0:T(8,128)(2,1)S(1)}, bf16[2,128,512]{2,1,0:T(8,128)(2,1)S(1)}, u32[]{:S(2)}, u32[]{:S(2)}) collective-permute-start(bf16[2,128,512]{2,1,0:T(8,128)(2,1)S(1)} %pack.1.refs_0_), channel_id=1, source_target_pairs={{0,48},{16,0},{32,16},{48,32},{1,49},{17,1},{33,17},{49,33},{2,50}... | collective-permute-start | bytes 786440 | tf_op jit(solution)/shard_map/ppermute | solution.py:34
  31.4 19.1 %all-to-all-start = ((bf16[8,128,512]{2,1,0:T(8,128)(2,1)}), bf16[8,128,512]{2,1,0:T(8,128)(2,1)S(1)}, u32[]{:S(2)}, u32[]{:S(2)}) async-start(bf16[8,128,512]{2,1,0:T(8,128)(2,1)} %to_rows.1), calls=%async_computation | async-start | bytes 2097152 | tf_op jit(solution)/shard_map/all_to_all | solution.py:241
  40.2 27.5 %copy-start.1 = (bf16[32,512]{1,0:T(8,128)(2,1)S(1)}, bf16[32,512]{1,0:T(8,128)(2,1)}, u32[]{:S(2)}) copy-start(bf16[32,512]{1,0:T(8,128)(2,1)} %cotangent.1) | copy-start | bytes 98308
  40.2 6.6 %collective-permute-start.14 = (bf16[128,512]{1,0:T(8,128)(2,1)S(1)}, bf16[128,512]{1,0:T(8,128)(2,1)S(1)}, u32[]{:S(2)}, u32[]{:S(2)}) collective-permute-start(bf16[128,512]{1,0:T(8,128)(2,1)S(1)} %get-tuple-element.21), channel_id=1, source_target_pairs={{0,192},{64,0},{128,64},{192,128},{1,193},{65,1},{129,65},{193,129... | collective-permute-start | bytes 393224 | tf_op jit(solution)/shard_map/ppermute | solution.py:34
  42.4 6.8 %collective-permute-start.13 = (bf16[128,512]{1,0:T(8,128)(2,1)S(1)}, bf16[128,512]{1,0:T(8,128)(2,1)S(1)}, u32[]{:S(2)}, u32[]{:S(2)}) collective-permute-start(bf16[128,512]{1,0:T(8,128)(2,1)S(1)} %get-tuple-element.20), channel_id=1, source_target_pairs={{0,128},{64,192},{128,0},{192,64},{1,129},{65,193},{129,1},{193,65... | collective-permute-start | bytes 393224 | tf_op jit(solution)/shard_map/ppermute | solution.py:34
  42.9 7.7 %collective-permute-start.12 = (bf16[128,512]{1,0:T(8,128)(2,1)S(1)}, bf16[128,512]{1,0:T(8,128)(2,1)S(1)}, u32[]{:S(2)}, u32[]{:S(2)}) collective-permute-start(bf16[128,512]{1,0:T(8,128)(2,1)S(1)} %get-tuple-element.19), channel_id=1, source_target_pairs={{0,64},{64,128},{128,192},{192,0},{1,65},{65,129},{129,193},{193,1... | collective-permute-start | bytes 393224 | tf_op jit(solution)/shard_map/ppermute | solution.py:34
  50.7 11.4 %collective-permute-start.17 = (bf16[128,512]{1,0:T(8,128)(2,1)S(1)}, bf16[128,512]{1,0:T(8,128)(2,1)S(1)}, u32[]{:S(2)}, u32[]{:S(2)}) collective-permute-start(bf16[128,512]{1,0:T(8,128)(2,1)S(1)} %fusion.3), channel_id=1, source_target_pairs={{0,6},{2,4},{4,2},{6,0},{1,7},{3,5},{5,3},{7,1},{8,14},{10,12},{12... | collective-permute-start | bytes 393224 | tf_op jit(solution)/shard_map/ppermute | solution.py:46
  53.5 12.3 %collective-permute-start.16 = (bf16[128,512]{1,0:T(8,128)(2,1)S(1)}, bf16[128,512]{1,0:T(8,128)(2,1)S(1)}, u32[]{:S(2)}, u32[]{:S(2)}) collective-permute-start(bf16[128,512]{1,0:T(8,128)(2,1)S(1)} %fusion.3), channel_id=1, source_target_pairs={{0,2},{2,0},{4,6},{6,4},{1,3},{3,1},{5,7},{7,5},{8,10},{10,8},{12,... | collective-permute-start | bytes 393224 | tf_op jit(solution)/shard_map/ppermute | solution.py:46
  53.9 12.1 %collective-permute-start.15 = (bf16[128,512]{1,0:T(8,128)(2,1)S(1)}, bf16[128,512]{1,0:T(8,128)(2,1)S(1)}, u32[]{:S(2)}, u32[]{:S(2)}) collective-permute-start(bf16[128,512]{1,0:T(8,128)(2,1)S(1)} %fusion.3), channel_id=1, source_target_pairs={{0,4},{2,6},{4,0},{6,2},{1,5},{3,7},{5,1},{7,3},{8,12},{10,14},{12... | collective-permute-start | bytes 393224 | tf_op jit(solution)/shard_map/ppermute | solution.py:46
  66.1 1.6 %collective-permute-start.18 = (f32[128,512]{1,0:T(8,128)S(1)}, f32[128,512]{1,0:T(8,128)S(1)}, u32[]{:S(2)}, u32[]{:S(2)}) collective-permute-start(f32[128,512]{1,0:T(8,128)S(1)} %convert_add_fusion.own_ref), channel_id=1, source_target_pairs={{0,1},{1,0},{2,3},{3,2},{4,5},{5,4},{6,7},{7,6},{8,9},{9,8},{10,11... | collective-permute-start | bytes 786440 | tf_op jit(solution)/shard_map/ppermute | solution.py:34
  68.6 3.9 %collective-permute-start.19 = (f32[32,256]{1,0:T(8,128)S(1)}, f32[32,256]{1,0:T(8,128)S(1)}, u32[]{:S(2)}, u32[]{:S(2)}) collective-permute-start(f32[32,256]{1,0:T(8,128)S(1)} %get-tuple-element.23), channel_id=1, source_target_pairs={{0,8},{8,0},{1,9},{9,1},{2,10},{10,2},{3,11},{11,3},{4,12},{12,4},... | collective-permute-start | bytes 98312 | tf_op jit(solution)/shard_map/ppermute | solution.py:34

commit v6 on v5

--- a/solution.py
+++ b/solution.py
@@ -180,7 +180,7 @@
     for core, ref in ((place, own_ref), (1 - place, sib_ref)):
         for step in range(4):
             rows = pl.ds(pl.multiple_of(step * 64 + core * 32, 32), 32)
-            field[rows, :] = ref[step * 32 : (step + 1) * 32, :]
+            field[rows, :] = ref[step * 32 : (step + 1) * 32, :].astype(jnp.float32)
     high, low = split(field[...])
     preact = jnp.dot(weight[...], low, preferred_element_type=jnp.float32)
     preact += jnp.dot(weight[...], high, preferred_element_type=jnp.float32)
@@ -243,7 +243,7 @@
     col_got = [col_part[0]] + ring(col_part, "x")
     share = sum(v.astype(jnp.float32) for v in (*row_got, *col_got)).astype(jnp.bfloat16)
     total = sum(v.astype(jnp.float32) for v in [share] + swaps(share, "h"))
-    sib_total = shifted(total, "c", 1)
+    sib_total = shifted(total.astype(jnp.bfloat16), "c", 1)
 
     weight_mine = lax.dynamic_slice_in_dim(weight, (at_h * 2 + at_c) * 32, 32, 1).T
     activation, grads = pl.pallas_call(

time: 86.3 us -> 85.8 us (level)
  waiting for transfers between devices: 21.3 us -> 18.9 us
  starting transfers between devices: 39.1 us -> 40.9 us
    ppermute x17, starting transfers between devices: 26.7 us -> 28.7 us  [shifted(): lax.ppermute(value, axis, [(i, (i + step) % total) for i in range(total)])]
    ppermute x17, waiting for transfers between devices: 12.7 us -> 10.9 us  [shifted(): lax.ppermute(value, axis, [(i, (i + step) % total) for i in range(total)])]
  transfers between devices with their start and end apart: 21 -> 21, of which waited for: 9 -> 8; matrix products, arithmetic and copies ran while one was open for 2% -> 2% of each run, Pallas kernels for 9% -> 9%
where the time goes in v6:
time: 85.8 us; the launch traced here: 85.6 us
  starting transfers between devices  40.9 us (48%)
  waiting for transfers between devices  18.9 us (22%)
  blocking collectives  12.9 us (15%)
  Pallas kernels  9.46 us (11%)
  between operations  1.44 us (2%)
  other arithmetic  1.05 us (1%)
  local copies, waits for them, and re-layouts  0.89 us (1%)
    ppermute x17, starting transfers between devices, shifted(): lax.ppermute(value, axis, [(i, (i + step) % total) for i in range(total)])  28.7 us
    all_to_all x1, blocking collectives, body(): terms = lax.all_to_all(many, ('x', 'y'), 0, 0, tiled=True)  12.9 us
    ppermute x17, waiting for transfers between devices, shifted(): lax.ppermute(value, axis, [(i, (i + step) % total) for i in range(total)])  10.9 us
    ppermute x3, waiting for transfers between devices, swaps(): lax.ppermute(value, axis, [(i, i ^ bits) for i in range(4)])  8.06 us
    pallas_call x2, Pallas kernels, agg(): pl.pallas_call(functools.partial(agg_kernel, to_rows), out_shape=out_shap...  7.64 us
    ppermute x3, starting transfers between devices, swaps(): lax.ppermute(value, axis, [(i, i ^ bits) for i in range(4)])  6.58 us
    all_to_all x1, starting transfers between devices, body(): row_got = list(lax.all_to_all(row_part, ('y', 'l'), 0, 0, tiled=True))  5.64 us
  transfers between devices with their start and end apart: 21, of which 8 were waited for; matrix products, arithmetic and copies ran while one was open for 2% of the time, Pallas kernels for 9%

profile of v6, /device:TPU:8, one launch (start us, length us, event | category | flops | bytes accessed | tf_op | source)
XLA Modules:
  0.0 85.6 jit_solution(12884374649973327890)
XLA Ops:
  0.6 0.0 copy-start
  0.6 0.1 collective-permute-start.4
  0.7 3.3 %collective-permute-start = (bf16[32,512]{1,0:T(8,128)(2,1)}, bf16[32,512]{1,0:T(8,128)(2,1)S(1)}, u32[]{:S(2)}, u32[]{:S(2)}) collective-permute-start(bf16[32,512]{1,0:T(8,128)(2,1)} %param.6), channel_id=1, source_target_pairs={{0,2},{2,4},{4,6},{6,0},{1,3},{3,5},{5,7},{7,1},{8,10},{10,12},{12... | collective-permute-start | bytes 98312 | tf_op jit(solution)/shard_map/ppermute | solution.py:34
  4.1 5.4 %collective-permute-start.1 = (bf16[32,512]{1,0:T(8,128)(2,1)}, bf16[32,512]{1,0:T(8,128)(2,1)S(1)}, u32[]{:S(2)}, u32[]{:S(2)}) collective-permute-start(bf16[32,512]{1,0:T(8,128)(2,1)} %param.6), channel_id=1, source_target_pairs={{0,4},{2,6},{4,0},{6,2},{1,5},{3,7},{5,1},{7,3},{8,12},{10,14},{12... | collective-permute-start | bytes 98312 | tf_op jit(solution)/shard_map/ppermute | solution.py:34
  9.5 2.7 %collective-permute-start.2 = (bf16[32,512]{1,0:T(8,128)(2,1)}, bf16[32,512]{1,0:T(8,128)(2,1)S(1)}, u32[]{:S(2)}, u32[]{:S(2)}) collective-permute-start(bf16[32,512]{1,0:T(8,128)(2,1)} %param.6), channel_id=1, source_target_pairs={{0,6},{2,0},{4,2},{6,4},{1,7},{3,1},{5,3},{7,5},{8,14},{10,8},{12,... | collective-permute-start | bytes 98312 | tf_op jit(solution)/shard_map/ppermute | solution.py:34
  12.8 0.7 concatenate.3.own_meta
  13.5 0.8 broadcast_select_fusion.own
  14.3 0.4 collective-permute-done.3.sib_meta
  14.6 0.0 collective-permute-done.r1
  14.7 0.0 collective-permute-done.1.r2
  14.7 0.2 order.1.refs_0_.own
  14.9 1.1 %collective-permute-start.8 = (bf16[128,512]{1,0:T(8,128)(2,1)S(1)}, bf16[128,512]{1,0:T(8,128)(2,1)S(1)}, u32[]{:S(2)}, u32[]{:S(2)}) collective-permute-start(bf16[128,512]{1,0:T(8,128)(2,1)S(1)} %order.1.refs_0_.own), channel_id=1, source_target_pairs={{0,8},{8,0},{1,9},{9,1},{2,10},{10,2},{3,11},{11,3},{4,12},{12,4},... | collective-permute-start | bytes 393224 | tf_op jit(solution)/shard_map/ppermute | solution.py:34
  16.0 1.5 %collective-permute-start.5 = (bf16[128,512]{1,0:T(8,128)(2,1)S(1)}, bf16[128,512]{1,0:T(8,128)(2,1)S(1)}, u32[]{:S(2)}, u32[]{:S(2)}) collective-permute-start(bf16[128,512]{1,0:T(8,128)(2,1)S(1)} %order.1.refs_0_.own), channel_id=1, source_target_pairs={{0,64},{64,128},{128,192},{192,0},{1,65},{65,129},{129,193},{193,1... | collective-permute-start | bytes 393224 | tf_op jit(solution)/shard_map/ppermute | solution.py:34
  17.5 2.7 %collective-permute-start.6 = (bf16[128,512]{1,0:T(8,128)(2,1)S(1)}, bf16[128,512]{1,0:T(8,128)(2,1)S(1)}, u32[]{:S(2)}, u32[]{:S(2)}) collective-permute-start(bf16[128,512]{1,0:T(8,128)(2,1)S(1)} %order.1.refs_0_.own), channel_id=1, source_target_pairs={{0,128},{64,192},{128,0},{192,64},{1,129},{65,193},{129,1},{193,65... | collective-permute-start | bytes 393224 | tf_op jit(solution)/shard_map/ppermute | solution.py:34
  20.2 1.4 %collective-permute-start.7 = (bf16[128,512]{1,0:T(8,128)(2,1)S(1)}, bf16[128,512]{1,0:T(8,128)(2,1)S(1)}, u32[]{:S(2)}, u32[]{:S(2)}) collective-permute-start(bf16[128,512]{1,0:T(8,128)(2,1)S(1)} %order.1.refs_0_.own), channel_id=1, source_target_pairs={{0,192},{64,0},{128,64},{192,128},{1,193},{65,1},{129,65},{193,129... | collective-permute-start | bytes 393224 | tf_op jit(solution)/shard_map/ppermute | solution.py:34
  21.7 0.0 collective-permute-done.8.other
  21.7 1.7 %collective-permute-start.9 = (bf16[2,128,512]{2,1,0:T(8,128)(2,1)S(1)}, bf16[2,128,512]{2,1,0:T(8,128)(2,1)S(1)}, u32[]{:S(2)}, u32[]{:S(2)}) collective-permute-start(bf16[2,128,512]{2,1,0:T(8,128)(2,1)S(1)} %pack.1.refs_0_), channel_id=1, source_target_pairs={{0,16},{16,32},{32,48},{48,0},{1,17},{17,33},{33,49},{49,1},{2,18}... | collective-permute-start | bytes 786440 | tf_op jit(solution)/shard_map/ppermute | solution.py:34
  23.4 0.9 %collective-permute-start.10 = (bf16[2,128,512]{2,1,0:T(8,128)(2,1)S(1)}, bf16[2,128,512]{2,1,0:T(8,128)(2,1)S(1)}, u32[]{:S(2)}, u32[]{:S(2)}) collective-permute-start(bf16[2,128,512]{2,1,0:T(8,128)(2,1)S(1)} %pack.1.refs_0_), channel_id=1, source_target_pairs={{0,32},{16,48},{32,0},{48,16},{1,33},{17,49},{33,1},{49,17},{2,34}... | collective-permute-start | bytes 786440 | tf_op jit(solution)/shard_map/ppermute | solution.py:34
  24.3 0.0 collective-permute-done.5.refs_1_
  24.3 2.4 %collective-permute-start.11 = (bf16[2,128,512]{2,1,0:T(8,128)(2,1)S(1)}, bf16[2,128,512]{2,1,0:T(8,128)(2,1)S(1)}, u32[]{:S(2)}, u32[]{:S(2)}) collective-permute-start(bf16[2,128,512]{2,1,0:T(8,128)(2,1)S(1)} %pack.1.refs_0_), channel_id=1, source_target_pairs={{0,48},{16,0},{32,16},{48,32},{1,49},{17,1},{33,17},{49,33},{2,50}... | collective-permute-start | bytes 786440 | tf_op jit(solution)/shard_map/ppermute | solution.py:34
  26.7 4.7 %to_rows.1 = bf16[8,128,512]{2,1,0:T(8,128)(2,1)} custom-call(s32[3,64]{1,0:T(4,128)S(1)} %concatenate.3.own_meta, s32[3,64]{1,0:T(4,128)S(1)} %collective-permute-done.3.sib_meta, bf16[64,128,128]{2,1,0:T(8,128)(2,1)} %bitcast.21, bf16[64,128,128]{2,1,0:T(8,128)(2,1)} %copy-done.2, bf16[128,512]{1,0:T(8,128)(2,1)S(1)} %order.1.refs_0_.own, ...), custom_call_target="tpu_custom_call" | custom-call | flops 20000000000 | bytes 6291456 | tf_op jit(solution)/shard_map/to_rows/pallas_call | solution.py:160
  31.4 5.6 %all-to-all-start = ((bf16[8,128,512]{2,1,0:T(8,128)(2,1)}), bf16[8,128,512]{2,1,0:T(8,128)(2,1)S(1)}, u32[]{:S(2)}, u32[]{:S(2)}) async-start(bf16[8,128,512]{2,1,0:T(8,128)(2,1)} %to_rows.1), calls=%async_computation | async-start | bytes 2097152 | tf_op jit(solution)/shard_map/all_to_all | solution.py:241
  37.0 0.0 collective-permute-done.11.refs_3_
  37.1 3.0 %to_cols.1 = (bf16[128,512]{1,0:T(8,128)(2,1)S(1)}, bf16[128,512]{1,0:T(8,128)(2,1)S(1)}, bf16[128,512]{1,0:T(8,128)(2,1)S(1)}, bf16[128,512]{1,0:T(8,128)(2,1)S(1)}) custom-call(s32[3,64]{1,0:T(4,128)S(1)} %concatenate.3.own_meta, s32[3,64]{1,0:T(4,128)S(1)} %collective-permute-done.3.sib_meta, bf16[64,128,128]{2,1,0:T(8,128)(2,1)} %bitcast.22, ...), custom_call_target="tpu_custom_call" | custom-call | flops 20000000000 | bytes 6291456 | tf_op jit(solution)/shard_map/to_cols/pallas_call | solution.py:160
  40.0 0.0 copy-start.1
  40.1 2.7 %collective-permute-start.14 = (bf16[128,512]{1,0:T(8,128)(2,1)S(1)}, bf16[128,512]{1,0:T(8,128)(2,1)S(1)}, u32[]{:S(2)}, u32[]{:S(2)}) collective-permute-start(bf16[128,512]{1,0:T(8,128)(2,1)S(1)} %get-tuple-element.21), channel_id=1, source_target_pairs={{0,192},{64,0},{128,64},{192,128},{1,193},{65,1},{129,65},{193,129... | collective-permute-start | bytes 393224 | tf_op jit(solution)/shard_map/ppermute | solution.py:34
  42.8 0.5 collective-permute-start.13
  43.3 1.1 %collective-permute-start.12 = (bf16[128,512]{1,0:T(8,128)(2,1)S(1)}, bf16[128,512]{1,0:T(8,128)(2,1)S(1)}, u32[]{:S(2)}, u32[]{:S(2)}) collective-permute-start(bf16[128,512]{1,0:T(8,128)(2,1)S(1)} %get-tuple-element.19), channel_id=1, source_target_pairs={{0,64},{64,128},{128,192},{192,0},{1,65},{65,129},{129,193},{193,1... | collective-permute-start | bytes 393224 | tf_op jit(solution)/shard_map/ppermute | solution.py:34
  44.4 2.8 %collective-permute-done.14 = bf16[128,512]{1,0:T(8,128)(2,1)S(1)} collective-permute-done((bf16[128,512]{1,0:T(8,128)(2,1)S(1)}, bf16[128,512]{1,0:T(8,128)(2,1)S(1)}, u32[]{:S(2)}, u32[]{:S(2)}) %collective-permute-start.14) | collective-permute-done | bytes 131104 | tf_op jit(solution)/shard_map/ppermute | solution.py:34
  47.2 2.4 %collective-permute-done.13 = bf16[128,512]{1,0:T(8,128)(2,1)S(1)} collective-permute-done((bf16[128,512]{1,0:T(8,128)(2,1)S(1)}, bf16[128,512]{1,0:T(8,128)(2,1)S(1)}, u32[]{:S(2)}, u32[]{:S(2)}) %collective-permute-start.13) | collective-permute-done | bytes 131104 | tf_op jit(solution)/shard_map/ppermute | solution.py:34
  49.6 1.2 %collective-permute-done.12 = bf16[128,512]{1,0:T(8,128)(2,1)S(1)} collective-permute-done((bf16[128,512]{1,0:T(8,128)(2,1)S(1)}, bf16[128,512]{1,0:T(8,128)(2,1)S(1)}, u32[]{:S(2)}, u32[]{:S(2)}) %collective-permute-start.12) | collective-permute-done | bytes 131104 | tf_op jit(solution)/shard_map/ppermute | solution.py:34
  50.8 0.0 all-to-all-done
  50.8 0.2 fusion.3
  51.0 2.6 %collective-permute-start.17 = (bf16[128,512]{1,0:T(8,128)(2,1)S(1)}, bf16[128,512]{1,0:T(8,128)(2,1)S(1)}, u32[]{:S(2)}, u32[]{:S(2)}) collective-permute-start(bf16[128,512]{1,0:T(8,128)(2,1)S(1)} %fusion.3), channel_id=1, source_target_pairs={{0,6},{2,4},{4,2},{6,0},{1,7},{3,5},{5,3},{7,1},{8,14},{10,12},{12... | collective-permute-start | bytes 393224 | tf_op jit(solution)/shard_map/ppermute | solution.py:46
  53.6 0.4 collective-permute-start.16
  54.1 3.5 %collective-permute-start.15 = (bf16[128,512]{1,0:T(8,128)(2,1)S(1)}, bf16[128,512]{1,0:T(8,128)(2,1)S(1)}, u32[]{:S(2)}, u32[]{:S(2)}) collective-permute-start(bf16[128,512]{1,0:T(8,128)(2,1)S(1)} %fusion.3), channel_id=1, source_target_pairs={{0,4},{2,6},{4,0},{6,2},{1,5},{3,7},{5,1},{7,3},{8,12},{10,14},{12... | collective-permute-start | bytes 393224 | tf_op jit(solution)/shard_map/ppermute | solution.py:46
  57.6 3.9 %collective-permute-done.17 = bf16[128,512]{1,0:T(8,128)(2,1)S(1)} collective-permute-done((bf16[128,512]{1,0:T(8,128)(2,1)S(1)}, bf16[128,512]{1,0:T(8,128)(2,1)S(1)}, u32[]{:S(2)}, u32[]{:S(2)}) %collective-permute-start.17) | collective-permute-done | bytes 131104 | tf_op jit(solution)/shard_map/ppermute | solution.py:46
  61.5 4.2 %collective-permute-done.16 = bf16[128,512]{1,0:T(8,128)(2,1)S(1)} collective-permute-done((bf16[128,512]{1,0:T(8,128)(2,1)S(1)}, bf16[128,512]{1,0:T(8,128)(2,1)S(1)}, u32[]{:S(2)}, u32[]{:S(2)}) %collective-permute-start.16) | collective-permute-done | bytes 131104 | tf_op jit(solution)/shard_map/ppermute | solution.py:46
  65.7 0.1 fusion.4
  65.7 0.1 collective-permute-start.18
  65.9 0.1 constant_dynamic-slice_fusion
  66.0 0.1 copy.9
  66.0 1.2 %collective-permute-done.18.sib_ref = bf16[128,512]{1,0:T(8,128)(2,1)S(1)} collective-permute-done((bf16[128,512]{1,0:T(8,128)(2,1)S(1)}, bf16[128,512]{1,0:T(8,128)(2,1)S(1)}, u32[]{:S(2)}, u32[]{:S(2)}) %collective-permute-start.18) | collective-permute-done | bytes 131104 | tf_op jit(solution)/shard_map/ppermute | solution.py:34
  67.2 0.9 %dense.1 = (bf16[32,512]{1,0:T(8,128)(2,1)}, f32[32,256]{1,0:T(8,128)S(1)}) custom-call(f32[128,512]{1,0:T(8,128)S(1)} %get-tuple-element.25.own_ref, bf16[128,512]{1,0:T(8,128)(2,1)S(1)} %collective-permute-done.18.sib_ref, bf16[32,256]{1,0:T(8,128)(2,1)S(1)} %bitcast.17, bf16[32,512]{1,0:T(8,128)(2,1)S(1)} %copy-done.1), custom_call_target="tpu_custom_call" | custom-call | tf_op jit(solution)/shard_map/dense/pallas_call | solution.py:249
  68.1 1.0 %collective-permute-start.19 = (f32[32,256]{1,0:T(8,128)S(1)}, f32[32,256]{1,0:T(8,128)S(1)}, u32[]{:S(2)}, u32[]{:S(2)}) collective-permute-start(f32[32,256]{1,0:T(8,128)S(1)} %get-tuple-element.23), channel_id=1, source_target_pairs={{0,8},{8,0},{1,9},{9,1},{2,10},{10,2},{3,11},{11,3},{4,12},{12,4},... | collective-permute-start | bytes 98312 | tf_op jit(solution)/shard_map/ppermute | solution.py:34
  69.1 2.9 %collective-permute-done.19 = f32[32,256]{1,0:T(8,128)S(1)} collective-permute-done((f32[32,256]{1,0:T(8,128)S(1)}, f32[32,256]{1,0:T(8,128)S(1)}, u32[]{:S(2)}, u32[]{:S(2)}) %collective-permute-start.19) | collective-permute-done | bytes 32800 | tf_op jit(solution)/shard_map/ppermute | solution.py:34
  72.0 12.9 %all_to_all.10.terms = bf16[16,32,256]{2,1,0:T(8,128)(2,1)S(1)} all-to-all(bf16[16,32,256]{2,1,0:T(8,128)(2,1)S(1)} %broadcast_in_dim.16), channel_id=1, replica_groups=mesh['x'=4,'y'=4,'l'=2,'h'=4,'c'=2] {'x','y'}, dimensions={0} | all-to-all | bytes 524288 | tf_op jit(solution)/shard_map/all_to_all | solution.py:263
  85.0 0.7 finish.1
  (15 shorter events, 0.1 us)
Async XLA Ops:
  0.6 65.2 %copy-start = (bf16[256,256]{1,0:T(8,128)(2,1)S(1)}, bf16[256,256]{1,0:T(8,128)(2,1)}, u32[]{:S(2)}) copy-start(bf16[256,256]{1,0:T(8,128)(2,1)} %param.7) | copy-start | bytes 393220
  0.6 14.0 %collective-permute-start.4 = (bf16[64,128,128]{2,1,0:T(8,128)(2,1)}, bf16[64,128,128]{2,1,0:T(8,128)(2,1)S(1)}, u32[]{:S(2)}, u32[]{:S(2)}) collective-permute-start(bf16[64,128,128]{2,1,0:T(8,128)(2,1)} %bitcast.20), channel_id=1, source_target_pairs={{0,1},{1,0},{2,3},{3,2},{4,5},{5,4},{6,7},{7,6},{8,9},{9,8},{10,11... | collective-permute-start | bytes 6291464 | tf_op jit(solution)/shard_map/ppermute | solution.py:34
  0.7 13.9 %collective-permute-start = (bf16[32,512]{1,0:T(8,128)(2,1)}, bf16[32,512]{1,0:T(8,128)(2,1)S(1)}, u32[]{:S(2)}, u32[]{:S(2)}) collective-permute-start(bf16[32,512]{1,0:T(8,128)(2,1)} %param.6), channel_id=1, source_target_pairs={{0,2},{2,4},{4,6},{6,0},{1,3},{3,5},{5,7},{7,1},{8,10},{10,12},{12... | collective-permute-start | bytes 98312 | tf_op jit(solution)/shard_map/ppermute | solution.py:34
  4.1 10.6 %collective-permute-start.1 = (bf16[32,512]{1,0:T(8,128)(2,1)}, bf16[32,512]{1,0:T(8,128)(2,1)S(1)}, u32[]{:S(2)}, u32[]{:S(2)}) collective-permute-start(bf16[32,512]{1,0:T(8,128)(2,1)} %param.6), channel_id=1, source_target_pairs={{0,4},{2,6},{4,0},{6,2},{1,5},{3,7},{5,1},{7,3},{8,12},{10,14},{12... | collective-permute-start | bytes 98312 | tf_op jit(solution)/shard_map/ppermute | solution.py:34
  9.5 5.2 %collective-permute-start.2 = (bf16[32,512]{1,0:T(8,128)(2,1)}, bf16[32,512]{1,0:T(8,128)(2,1)S(1)}, u32[]{:S(2)}, u32[]{:S(2)}) collective-permute-start(bf16[32,512]{1,0:T(8,128)(2,1)} %param.6), channel_id=1, source_target_pairs={{0,6},{2,0},{4,2},{6,4},{1,7},{3,1},{5,3},{7,5},{8,14},{10,8},{12,... | collective-permute-start | bytes 98312 | tf_op jit(solution)/shard_map/ppermute | solution.py:34
  13.5 1.2 %collective-permute-start.3 = (s32[3,64]{1,0:T(4,128)S(1)}, s32[3,64]{1,0:T(4,128)S(1)}, u32[]{:S(2)}, u32[]{:S(2)}) collective-permute-start(s32[3,64]{1,0:T(4,128)S(1)} %concatenate.3.own_meta), channel_id=1, source_target_pairs={{0,1},{1,0},{2,3},{3,2},{4,5},{5,4},{6,7},{7,6},{8,9},{9,8},{10,11... | collective-permute-start | bytes 2312 | tf_op jit(solution)/shard_map/ppermute | solution.py:34
  14.7 12.1 %copy-start.2 = (bf16[64,128,128]{2,1,0:T(8,128)(2,1)}, bf16[64,128,128]{2,1,0:T(8,128)(2,1)S(1)}, u32[]{:S(2)}) copy-start(bf16[64,128,128]{2,1,0:T(8,128)(2,1)S(1)} %collective-permute-done.4.sib_tiles) | copy-start | bytes 6291460
  14.9 6.8 %collective-permute-start.8 = (bf16[128,512]{1,0:T(8,128)(2,1)S(1)}, bf16[128,512]{1,0:T(8,128)(2,1)S(1)}, u32[]{:S(2)}, u32[]{:S(2)}) collective-permute-start(bf16[128,512]{1,0:T(8,128)(2,1)S(1)} %order.1.refs_0_.own), channel_id=1, source_target_pairs={{0,8},{8,0},{1,9},{9,1},{2,10},{10,2},{3,11},{11,3},{4,12},{12,4},... | collective-permute-start | bytes 393224 | tf_op jit(solution)/shard_map/ppermute | solution.py:34
  16.0 8.3 %collective-permute-start.5 = (bf16[128,512]{1,0:T(8,128)(2,1)S(1)}, bf16[128,512]{1,0:T(8,128)(2,1)S(1)}, u32[]{:S(2)}, u32[]{:S(2)}) collective-permute-start(bf16[128,512]{1,0:T(8,128)(2,1)S(1)} %order.1.refs_0_.own), channel_id=1, source_target_pairs={{0,64},{64,128},{128,192},{192,0},{1,65},{65,129},{129,193},{193,1... | collective-permute-start | bytes 393224 | tf_op jit(solution)/shard_map/ppermute | solution.py:34
  17.5 9.2 %collective-permute-start.6 = (bf16[128,512]{1,0:T(8,128)(2,1)S(1)}, bf16[128,512]{1,0:T(8,128)(2,1)S(1)}, u32[]{:S(2)}, u32[]{:S(2)}) collective-permute-start(bf16[128,512]{1,0:T(8,128)(2,1)S(1)} %order.1.refs_0_.own), channel_id=1, source_target_pairs={{0,128},{64,192},{128,0},{192,64},{1,129},{65,193},{129,1},{193,65... | collective-permute-start | bytes 393224 | tf_op jit(solution)/shard_map/ppermute | solution.py:34
  20.2 6.5 %collective-permute-start.7 = (bf16[128,512]{1,0:T(8,128)(2,1)S(1)}, bf16[128,512]{1,0:T(8,128)(2,1)S(1)}, u32[]{:S(2)}, u32[]{:S(2)}) collective-permute-start(bf16[128,512]{1,0:T(8,128)(2,1)S(1)} %order.1.refs_0_.own), channel_id=1, source_target_pairs={{0,192},{64,0},{128,64},{192,128},{1,193},{65,1},{129,65},{193,129... | collective-permute-start | bytes 393224 | tf_op jit(solution)/shard_map/ppermute | solution.py:34
  21.7 15.3 %collective-permute-start.9 = (bf16[2,128,512]{2,1,0:T(8,128)(2,1)S(1)}, bf16[2,128,512]{2,1,0:T(8,128)(2,1)S(1)}, u32[]{:S(2)}, u32[]{:S(2)}) collective-permute-start(bf16[2,128,512]{2,1,0:T(8,128)(2,1)S(1)} %pack.1.refs_0_), channel_id=1, source_target_pairs={{0,16},{16,32},{32,48},{48,0},{1,17},{17,33},{33,49},{49,1},{2,18}... | collective-permute-start | bytes 786440 | tf_op jit(solution)/shard_map/ppermute | solution.py:34
  23.4 13.7 %collective-permute-start.10 = (bf16[2,128,512]{2,1,0:T(8,128)(2,1)S(1)}, bf16[2,128,512]{2,1,0:T(8,128)(2,1)S(1)}, u32[]{:S(2)}, u32[]{:S(2)}) collective-permute-start(bf16[2,128,512]{2,1,0:T(8,128)(2,1)S(1)} %pack.1.refs_0_), channel_id=1, source_target_pairs={{0,32},{16,48},{32,0},{48,16},{1,33},{17,49},{33,1},{49,17},{2,34}... | collective-permute-start | bytes 786440 | tf_op jit(solution)/shard_map/ppermute | solution.py:34
  24.3 12.7 %collective-permute-start.11 = (bf16[2,128,512]{2,1,0:T(8,128)(2,1)S(1)}, bf16[2,128,512]{2,1,0:T(8,128)(2,1)S(1)}, u32[]{:S(2)}, u32[]{:S(2)}) collective-permute-start(bf16[2,128,512]{2,1,0:T(8,128)(2,1)S(1)} %pack.1.refs_0_), channel_id=1, source_target_pairs={{0,48},{16,0},{32,16},{48,32},{1,49},{17,1},{33,17},{49,33},{2,50}... | collective-permute-start | bytes 786440 | tf_op jit(solution)/shard_map/ppermute | solution.py:34
  31.4 19.4 %all-to-all-start = ((bf16[8,128,512]{2,1,0:T(8,128)(2,1)}), bf16[8,128,512]{2,1,0:T(8,128)(2,1)S(1)}, u32[]{:S(2)}, u32[]{:S(2)}) async-start(bf16[8,128,512]{2,1,0:T(8,128)(2,1)} %to_rows.1), calls=%async_computation | async-start | bytes 2097152 | tf_op jit(solution)/shard_map/all_to_all | solution.py:241
  40.0 27.1 %copy-start.1 = (bf16[32,512]{1,0:T(8,128)(2,1)S(1)}, bf16[32,512]{1,0:T(8,128)(2,1)}, u32[]{:S(2)}) copy-start(bf16[32,512]{1,0:T(8,128)(2,1)} %cotangent.1) | copy-start | bytes 98308
  40.1 7.2 %collective-permute-start.14 = (bf16[128,512]{1,0:T(8,128)(2,1)S(1)}, bf16[128,512]{1,0:T(8,128)(2,1)S(1)}, u32[]{:S(2)}, u32[]{:S(2)}) collective-permute-start(bf16[128,512]{1,0:T(8,128)(2,1)S(1)} %get-tuple-element.21), channel_id=1, source_target_pairs={{0,192},{64,0},{128,64},{192,128},{1,193},{65,1},{129,65},{193,129... | collective-permute-start | bytes 393224 | tf_op jit(solution)/shard_map/ppermute | solution.py:34
  42.8 6.8 %collective-permute-start.13 = (bf16[128,512]{1,0:T(8,128)(2,1)S(1)}, bf16[128,512]{1,0:T(8,128)(2,1)S(1)}, u32[]{:S(2)}, u32[]{:S(2)}) collective-permute-start(bf16[128,512]{1,0:T(8,128)(2,1)S(1)} %get-tuple-element.20), channel_id=1, source_target_pairs={{0,128},{64,192},{128,0},{192,64},{1,129},{65,193},{129,1},{193,65... | collective-permute-start | bytes 393224 | tf_op jit(solution)/shard_map/ppermute | solution.py:34
  43.3 7.5 %collective-permute-start.12 = (bf16[128,512]{1,0:T(8,128)(2,1)S(1)}, bf16[128,512]{1,0:T(8,128)(2,1)S(1)}, u32[]{:S(2)}, u32[]{:S(2)}) collective-permute-start(bf16[128,512]{1,0:T(8,128)(2,1)S(1)} %get-tuple-element.19), channel_id=1, source_target_pairs={{0,64},{64,128},{128,192},{192,0},{1,65},{65,129},{129,193},{193,1... | collective-permute-start | bytes 393224 | tf_op jit(solution)/shard_map/ppermute | solution.py:34
  51.0 10.5 %collective-permute-start.17 = (bf16[128,512]{1,0:T(8,128)(2,1)S(1)}, bf16[128,512]{1,0:T(8,128)(2,1)S(1)}, u32[]{:S(2)}, u32[]{:S(2)}) collective-permute-start(bf16[128,512]{1,0:T(8,128)(2,1)S(1)} %fusion.3), channel_id=1, source_target_pairs={{0,6},{2,4},{4,2},{6,0},{1,7},{3,5},{5,3},{7,1},{8,14},{10,12},{12... | collective-permute-start | bytes 393224 | tf_op jit(solution)/shard_map/ppermute | solution.py:46
  53.6 12.0 %collective-permute-start.16 = (bf16[128,512]{1,0:T(8,128)(2,1)S(1)}, bf16[128,512]{1,0:T(8,128)(2,1)S(1)}, u32[]{:S(2)}, u32[]{:S(2)}) collective-permute-start(bf16[128,512]{1,0:T(8,128)(2,1)S(1)} %fusion.3), channel_id=1, source_target_pairs={{0,2},{2,0},{4,6},{6,4},{1,3},{3,1},{5,7},{7,5},{8,10},{10,8},{12,... | collective-permute-start | bytes 393224 | tf_op jit(solution)/shard_map/ppermute | solution.py:46
  54.1 11.6 %collective-permute-start.15 = (bf16[128,512]{1,0:T(8,128)(2,1)S(1)}, bf16[128,512]{1,0:T(8,128)(2,1)S(1)}, u32[]{:S(2)}, u32[]{:S(2)}) collective-permute-start(bf16[128,512]{1,0:T(8,128)(2,1)S(1)} %fusion.3), channel_id=1, source_target_pairs={{0,4},{2,6},{4,0},{6,2},{1,5},{3,7},{5,1},{7,3},{8,12},{10,14},{12... | collective-permute-start | bytes 393224 | tf_op jit(solution)/shard_map/ppermute | solution.py:46
  65.7 1.4 %collective-permute-start.18 = (bf16[128,512]{1,0:T(8,128)(2,1)S(1)}, bf16[128,512]{1,0:T(8,128)(2,1)S(1)}, u32[]{:S(2)}, u32[]{:S(2)}) collective-permute-start(bf16[128,512]{1,0:T(8,128)(2,1)S(1)} %get-tuple-element.24), channel_id=1, source_target_pairs={{0,1},{1,0},{2,3},{3,2},{4,5},{5,4},{6,7},{7,6},{8,9},{9,8},{10,11... | collective-permute-start | bytes 393224 | tf_op jit(solution)/shard_map/ppermute | solution.py:34
  68.1 3.9 %collective-permute-start.19 = (f32[32,256]{1,0:T(8,128)S(1)}, f32[32,256]{1,0:T(8,128)S(1)}, u32[]{:S(2)}, u32[]{:S(2)}) collective-permute-start(f32[32,256]{1,0:T(8,128)S(1)} %get-tuple-element.23), channel_id=1, source_target_pairs={{0,8},{8,0},{1,9},{9,1},{2,10},{10,2},{3,11},{11,3},{4,12},{12,4},... | collective-permute-start | bytes 98312 | tf_op jit(solution)/shard_map/ppermute | solution.py:34

commit v7 on v5

--- a/solution.py
+++ b/solution.py
@@ -78,9 +78,11 @@
 
     sides = ((0, own_meta, own_tiles), (1, sib_meta, sib_tiles))
 
-    def tile_copy(side, turn, tiles):
+    def tile_copy(side, turn, half, tiles):
         return pltpu.make_async_copy(
-            tiles.at[pl.ds(turn * GROUP, GROUP)], held.at[side, turn], tile_sem.at[side, turn]
+            tiles.at[pl.ds(turn * GROUP + half * (GROUP // 2), GROUP // 2)],
+            held.at[side, turn, pl.ds(half * (GROUP // 2), GROUP // 2)],
+            tile_sem.at[side, turn, half],
         )
 
     for side, meta, tiles in sides:
@@ -88,7 +90,8 @@
 
             @pl.when(meta[2, 0] > turn * GROUP)
             def _(side=side, turn=turn, tiles=tiles):
-                tile_copy(side, turn, tiles).start()
+                for half in range(2):
+                    tile_copy(side, turn, half, tiles).start()
 
     for piece, source in enumerate(sources):
         for part in range(PER_PIECE):
@@ -112,9 +115,10 @@
 
         def visiting(turn, carry, side=side, used=used, tiles=tiles, ends=ends):
             source, target = ends
-            tile_copy(side, turn, tiles).wait()
             terms = []
             for member in range(GROUP):
+                if member % (GROUP // 2) == 0:
+                    tile_copy(side, turn, member // (GROUP // 2), tiles).wait()
                 terms.append(
                     lax.dot_general(
                         field[source(turn * GROUP + member)],
@@ -150,7 +154,7 @@
         pltpu.VMEM((outs * PER_PIECE + 1, HALF, TILE), jnp.float32),
         pltpu.VMEM((2, SLOTS // GROUP, GROUP, TILE, TILE), jnp.bfloat16),
     ]
-    sems = [pltpu.SemaphoreType.DMA((2, SLOTS // GROUP))]
+    sems = [pltpu.SemaphoreType.DMA((2, SLOTS // GROUP, 2))]
     if to_rows:
         scratch += [pltpu.VMEM((outs,) + PIECE, jnp.bfloat16)]
         sems += [pltpu.SemaphoreType.DMA((outs,))]

time: 86.3 us -> 86.6 us (level)
  no operation moved by 1% of the time
where the time goes in v7:
time: 86.6 us; the launch traced here: 86.5 us
  starting transfers between devices  39.4 us (45%)
  waiting for transfers between devices  21.6 us (25%)
  blocking collectives  12.4 us (14%)
  Pallas kernels  9.84 us (11%)
  between operations  1.43 us (2%)
  other arithmetic  1.04 us (1%)
  local copies, waits for them, and re-layouts  0.89 us (1%)
    ppermute x17, starting transfers between devices, shifted(): lax.ppermute(value, axis, [(i, (i + step) % total) for i in range(total)])  27.3 us
    ppermute x17, waiting for transfers between devices, shifted(): lax.ppermute(value, axis, [(i, (i + step) % total) for i in range(total)])  12.8 us
    all_to_all x1, blocking collectives, body(): terms = lax.all_to_all(many, ('x', 'y'), 0, 0, tiled=True)  12.4 us
    ppermute x3, waiting for transfers between devices, swaps(): lax.ppermute(value, axis, [(i, i ^ bits) for i in range(4)])  8.78 us
    pallas_call x2, Pallas kernels, agg(): pl.pallas_call(functools.partial(agg_kernel, to_rows), out_shape=out_shap...  8 us
    ppermute x3, starting transfers between devices, swaps(): lax.ppermute(value, axis, [(i, i ^ bits) for i in range(4)])  6.58 us
    all_to_all x1, starting transfers between devices, body(): row_got = list(lax.all_to_all(row_part, ('y', 'l'), 0, 0, tiled=True))  5.52 us
  transfers between devices with their start and end apart: 21, of which 9 were waited for; matrix products, arithmetic and copies ran while one was open for 2% of the time, Pallas kernels for 9%

profile of v7, /device:TPU:8, one launch (start us, length us, event | category | flops | bytes accessed | tf_op | source)
XLA Modules:
  0.0 86.5 jit_solution(5447583213413372995)
XLA Ops:
  0.6 0.0 copy-start
  0.6 0.1 collective-permute-start.4
  0.7 3.3 %collective-permute-start = (bf16[32,512]{1,0:T(8,128)(2,1)}, bf16[32,512]{1,0:T(8,128)(2,1)S(1)}, u32[]{:S(2)}, u32[]{:S(2)}) collective-permute-start(bf16[32,512]{1,0:T(8,128)(2,1)} %param.6), channel_id=1, source_target_pairs={{0,2},{2,4},{4,6},{6,0},{1,3},{3,5},{5,7},{7,1},{8,10},{10,12},{12... | collective-permute-start | bytes 98312 | tf_op jit(solution)/shard_map/ppermute | solution.py:34
  4.1 5.4 %collective-permute-start.1 = (bf16[32,512]{1,0:T(8,128)(2,1)}, bf16[32,512]{1,0:T(8,128)(2,1)S(1)}, u32[]{:S(2)}, u32[]{:S(2)}) collective-permute-start(bf16[32,512]{1,0:T(8,128)(2,1)} %param.6), channel_id=1, source_target_pairs={{0,4},{2,6},{4,0},{6,2},{1,5},{3,7},{5,1},{7,3},{8,12},{10,14},{12... | collective-permute-start | bytes 98312 | tf_op jit(solution)/shard_map/ppermute | solution.py:34
  9.5 2.7 %collective-permute-start.2 = (bf16[32,512]{1,0:T(8,128)(2,1)}, bf16[32,512]{1,0:T(8,128)(2,1)S(1)}, u32[]{:S(2)}, u32[]{:S(2)}) collective-permute-start(bf16[32,512]{1,0:T(8,128)(2,1)} %param.6), channel_id=1, source_target_pairs={{0,6},{2,0},{4,2},{6,4},{1,7},{3,1},{5,3},{7,5},{8,14},{10,8},{12,... | collective-permute-start | bytes 98312 | tf_op jit(solution)/shard_map/ppermute | solution.py:34
  12.8 0.7 concatenate.3.own_meta
  13.5 0.0 collective-permute-start.3
  13.5 0.8 broadcast_select_fusion.own
  14.3 0.4 collective-permute-done.3.sib_meta
  14.7 0.0 collective-permute-done.2.r3
  14.7 0.0 collective-permute-done.4.sib_tiles
  14.7 0.2 order.1.refs_0_.own
  14.9 1.1 %collective-permute-start.8 = (bf16[128,512]{1,0:T(8,128)(2,1)S(1)}, bf16[128,512]{1,0:T(8,128)(2,1)S(1)}, u32[]{:S(2)}, u32[]{:S(2)}) collective-permute-start(bf16[128,512]{1,0:T(8,128)(2,1)S(1)} %order.1.refs_0_.own), channel_id=1, source_target_pairs={{0,8},{8,0},{1,9},{9,1},{2,10},{10,2},{3,11},{11,3},{4,12},{12,4},... | collective-permute-start | bytes 393224 | tf_op jit(solution)/shard_map/ppermute | solution.py:34
  16.0 1.5 %collective-permute-start.5 = (bf16[128,512]{1,0:T(8,128)(2,1)S(1)}, bf16[128,512]{1,0:T(8,128)(2,1)S(1)}, u32[]{:S(2)}, u32[]{:S(2)}) collective-permute-start(bf16[128,512]{1,0:T(8,128)(2,1)S(1)} %order.1.refs_0_.own), channel_id=1, source_target_pairs={{0,64},{64,128},{128,192},{192,0},{1,65},{65,129},{129,193},{193,1... | collective-permute-start | bytes 393224 | tf_op jit(solution)/shard_map/ppermute | solution.py:34
  17.5 2.7 %collective-permute-start.6 = (bf16[128,512]{1,0:T(8,128)(2,1)S(1)}, bf16[128,512]{1,0:T(8,128)(2,1)S(1)}, u32[]{:S(2)}, u32[]{:S(2)}) collective-permute-start(bf16[128,512]{1,0:T(8,128)(2,1)S(1)} %order.1.refs_0_.own), channel_id=1, source_target_pairs={{0,128},{64,192},{128,0},{192,64},{1,129},{65,193},{129,1},{193,65... | collective-permute-start | bytes 393224 | tf_op jit(solution)/shard_map/ppermute | solution.py:34
  20.2 1.4 %collective-permute-start.7 = (bf16[128,512]{1,0:T(8,128)(2,1)S(1)}, bf16[128,512]{1,0:T(8,128)(2,1)S(1)}, u32[]{:S(2)}, u32[]{:S(2)}) collective-permute-start(bf16[128,512]{1,0:T(8,128)(2,1)S(1)} %order.1.refs_0_.own), channel_id=1, source_target_pairs={{0,192},{64,0},{128,64},{192,128},{1,193},{65,1},{129,65},{193,129... | collective-permute-start | bytes 393224 | tf_op jit(solution)/shard_map/ppermute | solution.py:34
  21.7 1.7 %collective-permute-start.9 = (bf16[2,128,512]{2,1,0:T(8,128)(2,1)S(1)}, bf16[2,128,512]{2,1,0:T(8,128)(2,1)S(1)}, u32[]{:S(2)}, u32[]{:S(2)}) collective-permute-start(bf16[2,128,512]{2,1,0:T(8,128)(2,1)S(1)} %pack.1.refs_0_), channel_id=1, source_target_pairs={{0,16},{16,32},{32,48},{48,0},{1,17},{17,33},{33,49},{49,1},{2,18}... | collective-permute-start | bytes 786440 | tf_op jit(solution)/shard_map/ppermute | solution.py:34
  23.4 0.9 %collective-permute-start.10 = (bf16[2,128,512]{2,1,0:T(8,128)(2,1)S(1)}, bf16[2,128,512]{2,1,0:T(8,128)(2,1)S(1)}, u32[]{:S(2)}, u32[]{:S(2)}) collective-permute-start(bf16[2,128,512]{2,1,0:T(8,128)(2,1)S(1)} %pack.1.refs_0_), channel_id=1, source_target_pairs={{0,32},{16,48},{32,0},{48,16},{1,33},{17,49},{33,1},{49,17},{2,34}... | collective-permute-start | bytes 786440 | tf_op jit(solution)/shard_map/ppermute | solution.py:34
  24.3 2.4 %collective-permute-start.11 = (bf16[2,128,512]{2,1,0:T(8,128)(2,1)S(1)}, bf16[2,128,512]{2,1,0:T(8,128)(2,1)S(1)}, u32[]{:S(2)}, u32[]{:S(2)}) collective-permute-start(bf16[2,128,512]{2,1,0:T(8,128)(2,1)S(1)} %pack.1.refs_0_), channel_id=1, source_target_pairs={{0,48},{16,0},{32,16},{48,32},{1,49},{17,1},{33,17},{49,33},{2,50}... | collective-permute-start | bytes 786440 | tf_op jit(solution)/shard_map/ppermute | solution.py:34
  26.7 0.0 collective-permute-done.6.refs_2_
  26.7 0.0 collective-permute-done.7.refs_3_
  26.7 4.7 %to_rows.1 = bf16[8,128,512]{2,1,0:T(8,128)(2,1)} custom-call(s32[3,64]{1,0:T(4,128)S(1)} %concatenate.3.own_meta, s32[3,64]{1,0:T(4,128)S(1)} %collective-permute-done.3.sib_meta, bf16[64,128,128]{2,1,0:T(8,128)(2,1)} %bitcast.21, bf16[64,128,128]{2,1,0:T(8,128)(2,1)} %copy-done.2, bf16[128,512]{1,0:T(8,128)(2,1)S(1)} %order.1.refs_0_.own, ...), custom_call_target="tpu_custom_call" | custom-call | flops 20000000000 | bytes 6291456 | tf_op jit(solution)/shard_map/to_rows/pallas_call | solution.py:164
  31.5 5.5 %all-to-all-start = ((bf16[8,128,512]{2,1,0:T(8,128)(2,1)}), bf16[8,128,512]{2,1,0:T(8,128)(2,1)S(1)}, u32[]{:S(2)}, u32[]{:S(2)}) async-start(bf16[8,128,512]{2,1,0:T(8,128)(2,1)} %to_rows.1), calls=%async_computation | async-start | bytes 2097152 | tf_op jit(solution)/shard_map/all_to_all | solution.py:245
  37.0 0.0 collective-permute-done.9.refs_1_
  37.0 0.0 collective-permute-done.10.refs_2_
  37.0 3.3 %to_cols.1 = (bf16[128,512]{1,0:T(8,128)(2,1)S(1)}, bf16[128,512]{1,0:T(8,128)(2,1)S(1)}, bf16[128,512]{1,0:T(8,128)(2,1)S(1)}, bf16[128,512]{1,0:T(8,128)(2,1)S(1)}) custom-call(s32[3,64]{1,0:T(4,128)S(1)} %concatenate.3.own_meta, s32[3,64]{1,0:T(4,128)S(1)} %collective-permute-done.3.sib_meta, bf16[64,128,128]{2,1,0:T(8,128)(2,1)} %bitcast.22, ...), custom_call_target="tpu_custom_call" | custom-call | flops 20000000000 | bytes 6291456 | tf_op jit(solution)/shard_map/to_cols/pallas_call | solution.py:164
  40.3 0.0 copy-start.1
  40.3 3.0 %collective-permute-start.14 = (bf16[128,512]{1,0:T(8,128)(2,1)S(1)}, bf16[128,512]{1,0:T(8,128)(2,1)S(1)}, u32[]{:S(2)}, u32[]{:S(2)}) collective-permute-start(bf16[128,512]{1,0:T(8,128)(2,1)S(1)} %get-tuple-element.21), channel_id=1, source_target_pairs={{0,192},{64,0},{128,64},{192,128},{1,193},{65,1},{129,65},{193,129... | collective-permute-start | bytes 393224 | tf_op jit(solution)/shard_map/ppermute | solution.py:34
  43.3 0.9 %collective-permute-start.13 = (bf16[128,512]{1,0:T(8,128)(2,1)S(1)}, bf16[128,512]{1,0:T(8,128)(2,1)S(1)}, u32[]{:S(2)}, u32[]{:S(2)}) collective-permute-start(bf16[128,512]{1,0:T(8,128)(2,1)S(1)} %get-tuple-element.20), channel_id=1, source_target_pairs={{0,128},{64,192},{128,0},{192,64},{1,129},{65,193},{129,1},{193,65... | collective-permute-start | bytes 393224 | tf_op jit(solution)/shard_map/ppermute | solution.py:34
  44.2 0.0 collective-permute-start.12
  44.2 3.4 %collective-permute-done.14 = bf16[128,512]{1,0:T(8,128)(2,1)S(1)} collective-permute-done((bf16[128,512]{1,0:T(8,128)(2,1)S(1)}, bf16[128,512]{1,0:T(8,128)(2,1)S(1)}, u32[]{:S(2)}, u32[]{:S(2)}) %collective-permute-start.14) | collective-permute-done | bytes 131104 | tf_op jit(solution)/shard_map/ppermute | solution.py:34
  47.7 2.4 %collective-permute-done.13 = bf16[128,512]{1,0:T(8,128)(2,1)S(1)} collective-permute-done((bf16[128,512]{1,0:T(8,128)(2,1)S(1)}, bf16[128,512]{1,0:T(8,128)(2,1)S(1)}, u32[]{:S(2)}, u32[]{:S(2)}) %collective-permute-start.13) | collective-permute-done | bytes 131104 | tf_op jit(solution)/shard_map/ppermute | solution.py:34
  50.0 1.3 %collective-permute-done.12 = bf16[128,512]{1,0:T(8,128)(2,1)S(1)} collective-permute-done((bf16[128,512]{1,0:T(8,128)(2,1)S(1)}, bf16[128,512]{1,0:T(8,128)(2,1)S(1)}, u32[]{:S(2)}, u32[]{:S(2)}) %collective-permute-start.12) | collective-permute-done | bytes 131104 | tf_op jit(solution)/shard_map/ppermute | solution.py:34
  51.3 0.2 fusion.3
  51.5 3.8 %collective-permute-start.17 = (bf16[128,512]{1,0:T(8,128)(2,1)S(1)}, bf16[128,512]{1,0:T(8,128)(2,1)S(1)}, u32[]{:S(2)}, u32[]{:S(2)}) collective-permute-start(bf16[128,512]{1,0:T(8,128)(2,1)S(1)} %fusion.3), channel_id=1, source_target_pairs={{0,6},{2,4},{4,2},{6,0},{1,7},{3,5},{5,3},{7,1},{8,14},{10,12},{12... | collective-permute-start | bytes 393224 | tf_op jit(solution)/shard_map/ppermute | solution.py:46
  55.3 2.8 %collective-permute-start.15 = (bf16[128,512]{1,0:T(8,128)(2,1)S(1)}, bf16[128,512]{1,0:T(8,128)(2,1)S(1)}, u32[]{:S(2)}, u32[]{:S(2)}) collective-permute-start(bf16[128,512]{1,0:T(8,128)(2,1)S(1)} %fusion.3), channel_id=1, source_target_pairs={{0,4},{2,6},{4,0},{6,2},{1,5},{3,7},{5,1},{7,3},{8,12},{10,14},{12... | collective-permute-start | bytes 393224 | tf_op jit(solution)/shard_map/ppermute | solution.py:46
  58.1 4.1 %collective-permute-done.17 = bf16[128,512]{1,0:T(8,128)(2,1)S(1)} collective-permute-done((bf16[128,512]{1,0:T(8,128)(2,1)S(1)}, bf16[128,512]{1,0:T(8,128)(2,1)S(1)}, u32[]{:S(2)}, u32[]{:S(2)}) %collective-permute-start.17) | collective-permute-done | bytes 131104 | tf_op jit(solution)/shard_map/ppermute | solution.py:46
  62.3 1.1 %collective-permute-done.16 = bf16[128,512]{1,0:T(8,128)(2,1)S(1)} collective-permute-done((bf16[128,512]{1,0:T(8,128)(2,1)S(1)}, bf16[128,512]{1,0:T(8,128)(2,1)S(1)}, u32[]{:S(2)}, u32[]{:S(2)}) %collective-permute-start.16) | collective-permute-done | bytes 131104 | tf_op jit(solution)/shard_map/ppermute | solution.py:46
  63.4 3.5 %collective-permute-done.15 = bf16[128,512]{1,0:T(8,128)(2,1)S(1)} collective-permute-done((bf16[128,512]{1,0:T(8,128)(2,1)S(1)}, bf16[128,512]{1,0:T(8,128)(2,1)S(1)}, u32[]{:S(2)}, u32[]{:S(2)}) %collective-permute-start.15) | collective-permute-done | bytes 131104 | tf_op jit(solution)/shard_map/ppermute | solution.py:46
  66.9 0.1 convert_add_fusion.own_ref
  67.0 0.1 collective-permute-start.18
  67.1 0.1 constant_dynamic-slice_fusion
  67.2 0.1 copy.9
  67.3 1.3 %collective-permute-done.18.sib_ref = f32[128,512]{1,0:T(8,128)S(1)} collective-permute-done((f32[128,512]{1,0:T(8,128)S(1)}, f32[128,512]{1,0:T(8,128)S(1)}, u32[]{:S(2)}, u32[]{:S(2)}) %collective-permute-start.18) | collective-permute-done | bytes 262176 | tf_op jit(solution)/shard_map/ppermute | solution.py:34
  68.6 0.9 %dense.1 = (bf16[32,512]{1,0:T(8,128)(2,1)}, f32[32,256]{1,0:T(8,128)S(1)}) custom-call(f32[128,512]{1,0:T(8,128)S(1)} %convert_add_fusion.own_ref, f32[128,512]{1,0:T(8,128)S(1)} %collective-permute-done.18.sib_ref, bf16[32,256]{1,0:T(8,128)(2,1)S(1)} %bitcast.17, bf16[32,512]{1,0:T(8,128)(2,1)S(1)} %copy-done.1), custom_call_target="tpu_custom_call" | custom-call | tf_op jit(solution)/shard_map/dense/pallas_call | solution.py:253
  69.5 3.9 %collective-permute-done.19 = f32[32,256]{1,0:T(8,128)S(1)} collective-permute-done((f32[32,256]{1,0:T(8,128)S(1)}, f32[32,256]{1,0:T(8,128)S(1)}, u32[]{:S(2)}, u32[]{:S(2)}) %collective-permute-start.19) | collective-permute-done | bytes 32800 | tf_op jit(solution)/shard_map/ppermute | solution.py:34
  73.5 12.4 %all_to_all.10.terms = bf16[16,32,256]{2,1,0:T(8,128)(2,1)S(1)} all-to-all(bf16[16,32,256]{2,1,0:T(8,128)(2,1)S(1)} %broadcast_in_dim.16), channel_id=1, replica_groups=mesh['x'=4,'y'=4,'l'=2,'h'=4,'c'=2] {'x','y'}, dimensions={0} | all-to-all | bytes 524288 | tf_op jit(solution)/shard_map/all_to_all | solution.py:267
  85.9 0.7 finish.1
  (15 shorter events, 0.1 us)
Async XLA Ops:
  0.6 66.5 %copy-start = (bf16[256,256]{1,0:T(8,128)(2,1)S(1)}, bf16[256,256]{1,0:T(8,128)(2,1)}, u32[]{:S(2)}) copy-start(bf16[256,256]{1,0:T(8,128)(2,1)} %param.7) | copy-start | bytes 393220
  0.6 14.0 %collective-permute-start.4 = (bf16[64,128,128]{2,1,0:T(8,128)(2,1)}, bf16[64,128,128]{2,1,0:T(8,128)(2,1)S(1)}, u32[]{:S(2)}, u32[]{:S(2)}) collective-permute-start(bf16[64,128,128]{2,1,0:T(8,128)(2,1)} %bitcast.20), channel_id=1, source_target_pairs={{0,1},{1,0},{2,3},{3,2},{4,5},{5,4},{6,7},{7,6},{8,9},{9,8},{10,11... | collective-permute-start | bytes 6291464 | tf_op jit(solution)/shard_map/ppermute | solution.py:34
  0.7 13.9 %collective-permute-start = (bf16[32,512]{1,0:T(8,128)(2,1)}, bf16[32,512]{1,0:T(8,128)(2,1)S(1)}, u32[]{:S(2)}, u32[]{:S(2)}) collective-permute-start(bf16[32,512]{1,0:T(8,128)(2,1)} %param.6), channel_id=1, source_target_pairs={{0,2},{2,4},{4,6},{6,0},{1,3},{3,5},{5,7},{7,1},{8,10},{10,12},{12... | collective-permute-start | bytes 98312 | tf_op jit(solution)/shard_map/ppermute | solution.py:34
  4.1 10.6 %collective-permute-start.1 = (bf16[32,512]{1,0:T(8,128)(2,1)}, bf16[32,512]{1,0:T(8,128)(2,1)S(1)}, u32[]{:S(2)}, u32[]{:S(2)}) collective-permute-start(bf16[32,512]{1,0:T(8,128)(2,1)} %param.6), channel_id=1, source_target_pairs={{0,4},{2,6},{4,0},{6,2},{1,5},{3,7},{5,1},{7,3},{8,12},{10,14},{12... | collective-permute-start | bytes 98312 | tf_op jit(solution)/shard_map/ppermute | solution.py:34
  9.5 5.2 %collective-permute-start.2 = (bf16[32,512]{1,0:T(8,128)(2,1)}, bf16[32,512]{1,0:T(8,128)(2,1)S(1)}, u32[]{:S(2)}, u32[]{:S(2)}) collective-permute-start(bf16[32,512]{1,0:T(8,128)(2,1)} %param.6), channel_id=1, source_target_pairs={{0,6},{2,0},{4,2},{6,4},{1,7},{3,1},{5,3},{7,5},{8,14},{10,8},{12,... | collective-permute-start | bytes 98312 | tf_op jit(solution)/shard_map/ppermute | solution.py:34
  13.5 1.2 %collective-permute-start.3 = (s32[3,64]{1,0:T(4,128)S(1)}, s32[3,64]{1,0:T(4,128)S(1)}, u32[]{:S(2)}, u32[]{:S(2)}) collective-permute-start(s32[3,64]{1,0:T(4,128)S(1)} %concatenate.3.own_meta), channel_id=1, source_target_pairs={{0,1},{1,0},{2,3},{3,2},{4,5},{5,4},{6,7},{7,6},{8,9},{9,8},{10,11... | collective-permute-start | bytes 2312 | tf_op jit(solution)/shard_map/ppermute | solution.py:34
  14.7 12.1 %copy-start.2 = (bf16[64,128,128]{2,1,0:T(8,128)(2,1)}, bf16[64,128,128]{2,1,0:T(8,128)(2,1)S(1)}, u32[]{:S(2)}) copy-start(bf16[64,128,128]{2,1,0:T(8,128)(2,1)S(1)} %collective-permute-done.4.sib_tiles) | copy-start | bytes 6291460
  14.9 6.8 %collective-permute-start.8 = (bf16[128,512]{1,0:T(8,128)(2,1)S(1)}, bf16[128,512]{1,0:T(8,128)(2,1)S(1)}, u32[]{:S(2)}, u32[]{:S(2)}) collective-permute-start(bf16[128,512]{1,0:T(8,128)(2,1)S(1)} %order.1.refs_0_.own), channel_id=1, source_target_pairs={{0,8},{8,0},{1,9},{9,1},{2,10},{10,2},{3,11},{11,3},{4,12},{12,4},... | collective-permute-start | bytes 393224 | tf_op jit(solution)/shard_map/ppermute | solution.py:34
  16.0 8.3 %collective-permute-start.5 = (bf16[128,512]{1,0:T(8,128)(2,1)S(1)}, bf16[128,512]{1,0:T(8,128)(2,1)S(1)}, u32[]{:S(2)}, u32[]{:S(2)}) collective-permute-start(bf16[128,512]{1,0:T(8,128)(2,1)S(1)} %order.1.refs_0_.own), channel_id=1, source_target_pairs={{0,64},{64,128},{128,192},{192,0},{1,65},{65,129},{129,193},{193,1... | collective-permute-start | bytes 393224 | tf_op jit(solution)/shard_map/ppermute | solution.py:34
  17.5 9.2 %collective-permute-start.6 = (bf16[128,512]{1,0:T(8,128)(2,1)S(1)}, bf16[128,512]{1,0:T(8,128)(2,1)S(1)}, u32[]{:S(2)}, u32[]{:S(2)}) collective-permute-start(bf16[128,512]{1,0:T(8,128)(2,1)S(1)} %order.1.refs_0_.own), channel_id=1, source_target_pairs={{0,128},{64,192},{128,0},{192,64},{1,129},{65,193},{129,1},{193,65... | collective-permute-start | bytes 393224 | tf_op jit(solution)/shard_map/ppermute | solution.py:34
  20.2 6.5 %collective-permute-start.7 = (bf16[128,512]{1,0:T(8,128)(2,1)S(1)}, bf16[128,512]{1,0:T(8,128)(2,1)S(1)}, u32[]{:S(2)}, u32[]{:S(2)}) collective-permute-start(bf16[128,512]{1,0:T(8,128)(2,1)S(1)} %order.1.refs_0_.own), channel_id=1, source_target_pairs={{0,192},{64,0},{128,64},{192,128},{1,193},{65,1},{129,65},{193,129... | collective-permute-start | bytes 393224 | tf_op jit(solution)/shard_map/ppermute | solution.py:34
  21.7 15.3 %collective-permute-start.9 = (bf16[2,128,512]{2,1,0:T(8,128)(2,1)S(1)}, bf16[2,128,512]{2,1,0:T(8,128)(2,1)S(1)}, u32[]{:S(2)}, u32[]{:S(2)}) collective-permute-start(bf16[2,128,512]{2,1,0:T(8,128)(2,1)S(1)} %pack.1.refs_0_), channel_id=1, source_target_pairs={{0,16},{16,32},{32,48},{48,0},{1,17},{17,33},{33,49},{49,1},{2,18}... | collective-permute-start | bytes 786440 | tf_op jit(solution)/shard_map/ppermute | solution.py:34
  23.4 13.6 %collective-permute-start.10 = (bf16[2,128,512]{2,1,0:T(8,128)(2,1)S(1)}, bf16[2,128,512]{2,1,0:T(8,128)(2,1)S(1)}, u32[]{:S(2)}, u32[]{:S(2)}) collective-permute-start(bf16[2,128,512]{2,1,0:T(8,128)(2,1)S(1)} %pack.1.refs_0_), channel_id=1, source_target_pairs={{0,32},{16,48},{32,0},{48,16},{1,33},{17,49},{33,1},{49,17},{2,34}... | collective-permute-start | bytes 786440 | tf_op jit(solution)/shard_map/ppermute | solution.py:34
  24.3 12.7 %collective-permute-start.11 = (bf16[2,128,512]{2,1,0:T(8,128)(2,1)S(1)}, bf16[2,128,512]{2,1,0:T(8,128)(2,1)S(1)}, u32[]{:S(2)}, u32[]{:S(2)}) collective-permute-start(bf16[2,128,512]{2,1,0:T(8,128)(2,1)S(1)} %pack.1.refs_0_), channel_id=1, source_target_pairs={{0,48},{16,0},{32,16},{48,32},{1,49},{17,1},{33,17},{49,33},{2,50}... | collective-permute-start | bytes 786440 | tf_op jit(solution)/shard_map/ppermute | solution.py:34
  31.5 19.9 %all-to-all-start = ((bf16[8,128,512]{2,1,0:T(8,128)(2,1)}), bf16[8,128,512]{2,1,0:T(8,128)(2,1)S(1)}, u32[]{:S(2)}, u32[]{:S(2)}) async-start(bf16[8,128,512]{2,1,0:T(8,128)(2,1)} %to_rows.1), calls=%async_computation | async-start | bytes 2097152 | tf_op jit(solution)/shard_map/all_to_all | solution.py:245
  40.3 28.3 %copy-start.1 = (bf16[32,512]{1,0:T(8,128)(2,1)S(1)}, bf16[32,512]{1,0:T(8,128)(2,1)}, u32[]{:S(2)}) copy-start(bf16[32,512]{1,0:T(8,128)(2,1)} %cotangent.1) | copy-start | bytes 98308
  40.3 7.4 %collective-permute-start.14 = (bf16[128,512]{1,0:T(8,128)(2,1)S(1)}, bf16[128,512]{1,0:T(8,128)(2,1)S(1)}, u32[]{:S(2)}, u32[]{:S(2)}) collective-permute-start(bf16[128,512]{1,0:T(8,128)(2,1)S(1)} %get-tuple-element.21), channel_id=1, source_target_pairs={{0,192},{64,0},{128,64},{192,128},{1,193},{65,1},{129,65},{193,129... | collective-permute-start | bytes 393224 | tf_op jit(solution)/shard_map/ppermute | solution.py:34
  43.3 6.8 %collective-permute-start.13 = (bf16[128,512]{1,0:T(8,128)(2,1)S(1)}, bf16[128,512]{1,0:T(8,128)(2,1)S(1)}, u32[]{:S(2)}, u32[]{:S(2)}) collective-permute-start(bf16[128,512]{1,0:T(8,128)(2,1)S(1)} %get-tuple-element.20), channel_id=1, source_target_pairs={{0,128},{64,192},{128,0},{192,64},{1,129},{65,193},{129,1},{193,65... | collective-permute-start | bytes 393224 | tf_op jit(solution)/shard_map/ppermute | solution.py:34
  44.2 7.1 %collective-permute-start.12 = (bf16[128,512]{1,0:T(8,128)(2,1)S(1)}, bf16[128,512]{1,0:T(8,128)(2,1)S(1)}, u32[]{:S(2)}, u32[]{:S(2)}) collective-permute-start(bf16[128,512]{1,0:T(8,128)(2,1)S(1)} %get-tuple-element.19), channel_id=1, source_target_pairs={{0,64},{64,128},{128,192},{192,0},{1,65},{65,129},{129,193},{193,1... | collective-permute-start | bytes 393224 | tf_op jit(solution)/shard_map/ppermute | solution.py:34
  51.5 10.7 %collective-permute-start.17 = (bf16[128,512]{1,0:T(8,128)(2,1)S(1)}, bf16[128,512]{1,0:T(8,128)(2,1)S(1)}, u32[]{:S(2)}, u32[]{:S(2)}) collective-permute-start(bf16[128,512]{1,0:T(8,128)(2,1)S(1)} %fusion.3), channel_id=1, source_target_pairs={{0,6},{2,4},{4,2},{6,0},{1,7},{3,5},{5,3},{7,1},{8,14},{10,12},{12... | collective-permute-start | bytes 393224 | tf_op jit(solution)/shard_map/ppermute | solution.py:46
  55.3 8.1 %collective-permute-start.16 = (bf16[128,512]{1,0:T(8,128)(2,1)S(1)}, bf16[128,512]{1,0:T(8,128)(2,1)S(1)}, u32[]{:S(2)}, u32[]{:S(2)}) collective-permute-start(bf16[128,512]{1,0:T(8,128)(2,1)S(1)} %fusion.3), channel_id=1, source_target_pairs={{0,2},{2,0},{4,6},{6,4},{1,3},{3,1},{5,7},{7,5},{8,10},{10,8},{12,... | collective-permute-start | bytes 393224 | tf_op jit(solution)/shard_map/ppermute | solution.py:46
  55.3 11.6 %collective-permute-start.15 = (bf16[128,512]{1,0:T(8,128)(2,1)S(1)}, bf16[128,512]{1,0:T(8,128)(2,1)S(1)}, u32[]{:S(2)}, u32[]{:S(2)}) collective-permute-start(bf16[128,512]{1,0:T(8,128)(2,1)S(1)} %fusion.3), channel_id=1, source_target_pairs={{0,4},{2,6},{4,0},{6,2},{1,5},{3,7},{5,1},{7,3},{8,12},{10,14},{12... | collective-permute-start | bytes 393224 | tf_op jit(solution)/shard_map/ppermute | solution.py:46
  67.0 1.6 %collective-permute-start.18 = (f32[128,512]{1,0:T(8,128)S(1)}, f32[128,512]{1,0:T(8,128)S(1)}, u32[]{:S(2)}, u32[]{:S(2)}) collective-permute-start(f32[128,512]{1,0:T(8,128)S(1)} %convert_add_fusion.own_ref), channel_id=1, source_target_pairs={{0,1},{1,0},{2,3},{3,2},{4,5},{5,4},{6,7},{7,6},{8,9},{9,8},{10,11... | collective-permute-start | bytes 786440 | tf_op jit(solution)/shard_map/ppermute | solution.py:34
  69.5 3.9 %collective-permute-start.19 = (f32[32,256]{1,0:T(8,128)S(1)}, f32[32,256]{1,0:T(8,128)S(1)}, u32[]{:S(2)}, u32[]{:S(2)}) collective-permute-start(f32[32,256]{1,0:T(8,128)S(1)} %get-tuple-element.23), channel_id=1, source_target_pairs={{0,8},{8,0},{1,9},{9,1},{2,10},{10,2},{3,11},{11,3},{4,12},{12,4},... | collective-permute-start | bytes 98312 | tf_op jit(solution)/shard_map/ppermute | solution.py:34
